TPU v7x, 32 devices: a whole 2x2x4 slice. The times are simulated.
32 devices in a mesh: seq: 8 (over z, y), dp: 4 (over x, core).
Axes of the slice: x: 2, y: 2, z: 4, core: 2. Of those that a mesh axis runs over, the one named last changes fastest.
Arguments:
- resid: bfloat16 [4, 4096, 2048], P('dp', 'seq'), may hold values from -6 to 6
- token_ids: int32 [4, 4096], P('dp', 'seq'), may hold values from 0 to 63999
- code_proj: float32 [6, 2048], replicated, may hold values from -2.5 to 2.5
- w_query: bfloat16 [2048, 1024], replicated, may hold values from -0.125 to 0.125
- w_key: bfloat16 [2048, 1024], replicated, may hold values from -0.125 to 0.125
- w_value: bfloat16 [2048, 1024], replicated, may hold values from -0.125 to 0.125
- gain: float32 [1024], replicated, may hold values from 0.1 to 1.9
- out_grad: bfloat16 [4, 4096, 1024], P('dp', 'seq'), may hold values from -6 to 6
Outputs:
- resid_grad: bfloat16 [4, 4096, 2048], P('dp', 'seq')
- weight_grads: float32 [2048, 3, 1024], P(('seq', 'dp'))
- gain_grad: float32 [1024], replicated
- code_grad: float32 [6, 2048], replicated
Inputs may be any that keep to these rules, and one draw needn't show every extreme that they name: `token_ids`: ids of the codebook of 64000 codes.
All inputs are finite; a program needn't handle non-finite values.
Results may differ from a plain program's by a relative error of at most 0.0084.
Values sent between devices are 32-bit elements; how exact they have to be, the bound alone decides.
No kernel may reach another device: no remote copies, remote signals or barrier semaphores. Data moves between devices by JAX's collectives and lax.ppermute only.
A program may use at most 128 MiB of HBM per device.

v0:
```python
import math

import jax
import jax.numpy as jnp
from jax import lax
from jax.sharding import PartitionSpec as P

HEADS = 8
DH = 128


fsq_levels = (8, 8, 8, 5, 5, 5)
fsq_bases = (1, 8, 64, 512, 2560, 12800)


def entering(part, axis, combine, identity, reverse):
    count = lax.axis_size(axis)
    place = lax.axis_index(axis)
    ahead = count - 1 - place if reverse else place
    gathered = lax.all_gather(part, axis)
    state = jnp.zeros_like(part) + jnp.asarray(identity, part.dtype)

    def one(hop, state):
        source = count - 1 - hop if reverse else hop
        return combine(state, lax.dynamic_index_in_dim(gathered, source, 0, False))

    return lax.fori_loop(0, ahead, one, state)


def code_rows(token_ids):
    code_list = []
    for fsq_level, fsq_base in zip(fsq_levels, fsq_bases):
        fsq_digit = token_ids // fsq_base % fsq_level
        code_list.append((2.0 * fsq_digit.astype(jnp.float32) - (fsq_level - 1)) / (fsq_level - 1))
    return jnp.stack(code_list)


def silu_slope(value):
    sigma = jax.nn.sigmoid(value)
    return sigma * (1.0 + value * (1.0 - sigma))


def add_states(earlier, later):
    return earlier + later


def body(resid, token_ids, code_proj, w_query, w_key, w_value, gain, out_grad):
    f32 = jnp.float32
    positions = resid.shape[1]
    code_values = code_rows(token_ids[0])
    summed = resid[0].astype(f32)
    for index in range(code_values.shape[0]):
        summed = summed + code_values[index][:, None] * code_proj[index]
    inputs = summed.astype(jnp.bfloat16)
    query_pre = jnp.dot(inputs, w_query, preferred_element_type=f32)
    key_pre = jnp.dot(inputs, w_key, preferred_element_type=f32)
    value_pre = jnp.dot(inputs, w_value, preferred_element_type=f32)

    def to_heads(array):
        return array.reshape(positions, HEADS, DH).transpose(1, 0, 2)

    def from_heads(array):
        return array.transpose(1, 0, 2).reshape(positions, HEADS * DH)

    queries = to_heads(jax.nn.silu(query_pre).astype(jnp.bfloat16))
    keys = to_heads(jax.nn.silu(key_pre).astype(jnp.bfloat16))
    values = to_heads(value_pre.astype(jnp.bfloat16))
    grads_out = to_heads(out_grad[0])
    block_kv = jnp.einsum("hte,htd->hed", keys, values, preferred_element_type=f32)
    empty_state = jnp.zeros_like(block_kv)
    prefix = entering(block_kv, "seq", add_states, empty_state, False).astype(jnp.bfloat16)
    row_ids = lax.broadcasted_iota(jnp.int32, (positions, positions), 0)
    col_ids = lax.broadcasted_iota(jnp.int32, (positions, positions), 1)
    causal = col_ids <= row_ids
    scores = jnp.where(
        causal, jnp.einsum("hte,hse->hts", queries, keys, preferred_element_type=f32), 0.0
    ).astype(jnp.bfloat16)
    attended = jnp.einsum("hts,hsd->htd", scores, values, preferred_element_type=f32)
    attended = attended + jnp.einsum("hte,hed->htd", queries, prefix, preferred_element_type=f32)
    root = jnp.sqrt(jnp.mean(attended * attended, axis=-1, keepdims=True) + 1e-06)
    normed = attended / root
    d_normed = grads_out.astype(f32) * gain.reshape(HEADS, 1, DH)
    d_att = (
        (d_normed - normed * jnp.mean(d_normed * normed, axis=-1, keepdims=True)) / root
    ).astype(jnp.bfloat16)
    gain_term = jnp.sum(grads_out.astype(f32) * normed, axis=1).reshape(HEADS * DH)
    block_grad = jnp.einsum("hte,htd->hed", queries, d_att, preferred_element_type=f32)
    suffix = entering(block_grad, "seq", add_states, empty_state, True).astype(jnp.bfloat16)
    back_scores = jnp.where(
        causal, jnp.einsum("htd,hsd->hts", d_att, values, preferred_element_type=f32), 0.0
    ).astype(jnp.bfloat16)
    d_query = jnp.einsum("hts,hse->hte", back_scores, keys, preferred_element_type=f32)
    d_query = d_query + jnp.einsum("htd,hed->hte", d_att, prefix, preferred_element_type=f32)
    d_key = jnp.einsum("hts,hte->hse", back_scores, queries, preferred_element_type=f32)
    d_key = d_key + jnp.einsum("hsd,hed->hse", values, suffix, preferred_element_type=f32)
    d_value = jnp.einsum("hts,htd->hsd", scores, d_att, preferred_element_type=f32)
    d_value = d_value + jnp.einsum("hse,hed->hsd", keys, suffix, preferred_element_type=f32)
    grad_q = (from_heads(d_query) * silu_slope(query_pre)).astype(jnp.bfloat16)
    grad_k = (from_heads(d_key) * silu_slope(key_pre)).astype(jnp.bfloat16)
    grad_v = from_heads(d_value).astype(jnp.bfloat16)
    transpose_dims = (((1,), (1,)), ((), ()))
    input_grad = lax.dot_general(grad_q, w_query, transpose_dims, preferred_element_type=f32)
    input_grad = input_grad + lax.dot_general(
        grad_k, w_key, transpose_dims, preferred_element_type=f32
    )
    input_grad = input_grad + lax.dot_general(
        grad_v, w_value, transpose_dims, preferred_element_type=f32
    )
    resid_grad = input_grad.astype(jnp.bfloat16)[None]
    all_tokens = positions * lax.axis_size("seq") * lax.axis_size("dp")
    grad_scale = 1.0 / math.sqrt(all_tokens)
    code_term = jnp.dot(code_values, input_grad, precision=lax.Precision.HIGHEST)
    gain_sum, code_sum = lax.psum((gain_term, code_term), ("seq", "dp"))
    row_dims = (((0,), (0,)), ((), ()))
    products = [
        lax.dot_general(inputs, grad_part, row_dims, preferred_element_type=f32)
        for grad_part in (grad_q, grad_k, grad_v)
    ]
    weight_sum = lax.psum_scatter(
        jnp.stack(products, axis=1), ("seq", "dp"), scatter_dimension=0, tiled=True
    )
    return (resid_grad, weight_sum * grad_scale, gain_sum * grad_scale, code_sum * grad_scale)


def solution(mesh):
    return jax.shard_map(
        body,
        mesh=mesh,
        in_specs=(
            P("dp", "seq", None),
            P("dp", "seq"),
            P(),
            P(),
            P(),
            P(),
            P(),
            P("dp", "seq", None),
        ),
        out_specs=(P("dp", "seq", None), P(("seq", "dp"), None, None), P(), P()),
        check_vma=False,
    )
```

profile of v0, /device:TPU:13, one launch (start us, length us, event | category | flops | bytes accessed | tf_op | source)
XLA Modules:
  0.0 499.6 jit_solution(7028275678719462998)
XLA Ops:
  8.1 1.3 fusion.102
  9.4 3.7 fusion.6
  13.1 2.4 convolution_convert_fusion
  16.1 3.8 multiply_convert_fusion.2
  19.9 1.1 copy-done.16
  22.3 1.5 fusion.27
  23.8 1.2 copy.65
  25.1 1.5 copy.28
  26.6 7.0 %multiply_convert_fusion.3 = (bf16[512,1024]{1,0:T(8,128)(2,1)}, f32[512,1024]{1,0:T(8,128)}) fusion(bf16[512,2048]{1,0:T(8,128)(2,1)} %copy-done.17, bf16[2048,1024]{1,0:T(8,128)(2,1)} %param.15), kind=kOutput, calls=%fused_computation.47 | convolution fusion | flops 2150105088 | bytes 9437184 | tf_op jit(solution)/shard_map/dot_general | solution.py:55
  33.6 2.3 copy.54
  36.0 3.0 select_convert_fusion.1
  39.0 2.0 copy-done
  41.0 2.9 fusion.28
  43.8 52.0 %all-gather.5.cloned.1.call-done = f32[64,128,128]{2,1,0:T(8,128)} async-done(((f32[8,128,128]{2,1,0:T(8,128)}), f32[64,128,128]{2,1,0:T(8,128)}) %all-gather.5.cloned.1.call-update) | async-done | bytes 4194320 | tf_op jit(solution)/shard_map/all_gather | solution.py:20
  95.8 3.8 while.22
  95.9 1.2 bitcast_add_fusion.4
  97.1 1.2 bitcast_add_fusion.4
  98.3 1.2 bitcast_add_fusion.4
  99.6 2.4 multiply_reduce_fusion.2
  104.4 1.2 fusion.104
  105.7 3.0 select_convert_fusion
  108.7 1.5 fusion.32
  110.7 1.8 convolution_add_fusion
  112.5 2.9 copy.61
  115.5 4.4 fusion.108
  119.9 2.1 fusion.107
  124.7 5.7 %convolution_bitcast_fusion.2 = f32[2048,1,1024]{2,0,1:T(8,128)} fusion(bf16[512,2048]{1,0:T(8,128)(2,1)S(1)} %copy-done.18, bf16[512,1024]{1,0:T(8,128)(2,1)S(1)} %multiply_convert_fusion.1), kind=kOutput, calls=%fused_computation.9 | convolution fusion | flops 2147483648 | bytes 11534336 | tf_op jit(solution)/shard_map/dot_general | solution.py:116
  130.4 51.7 %all-gather.7.cloned.1.call-done = f32[64,128,128]{2,1,0:T(8,128)} async-done(((f32[8,128,128]{2,1,0:T(8,128)}), f32[64,128,128]{2,1,0:T(8,128)}) %all-gather.7.cloned.1.call-update) | async-done | bytes 4194320 | tf_op jit(solution)/shard_map/all_gather | solution.py:20
  182.2 5.1 %while.23 = (s32[]{:T(128)}, f32[8,128,128]{2,1,0:T(8,128)S(1)}, s32[]{:T(128)}, f32[8,8,128,128]{3,2,1,0:T(8,128)}, s32[]{:T(128)}, /*index=5*/s32[]{:T(128)}, s32[]{:T(128)}, s32[]{:T(128)}) while((s32[]{:T(128)}, f32[8,128,128]{2,1,0:T(8,128)S(1)}, s32[]{:T(128)}, f32[8,8,128,128]{3,2,1,0:T(8,128)}, s32[]{:T(128)}, /*index=5*/s32[]{:T(128)}, ...), condition=%wide.region_5.6_spmd, body=%wide.region_4.5_spmd.sunk | while | flops 131078 | bytes 1573007 | solution.py:27
  182.2 1.3 bitcast_add_fusion.5
  183.6 1.2 bitcast_add_fusion.5
  184.7 1.2 bitcast_add_fusion.5
  185.9 1.2 bitcast_add_fusion.5
  187.4 2.9 add_convert_fusion
  190.2 1.9 convolution_add_fusion.1
  192.1 1.9 copy.62
  194.0 5.7 %convolution_bitcast_fusion = f32[2048,1,1024]{2,0,1:T(8,128)S(1)} fusion(bf16[512,1024]{0,1:T(8,128)(2,1)S(1)} %bitcast.153, bf16[1,512,2048]{2,1,0:T(8,128)(2,1)} %param.12, f32[2048]{0:T(1024)S(1)} %bitcast.164, f32[512]{0:T(512)S(1)} %get-tuple-element.121, f32[2048]{0:T(1024)S(1)} %bitcast.166, f32[512]{0:T(512)S(1)} %get-tuple-element.119, ...), kind=kOutput, calls=%fused_computation.7 | convolution fusion | flops 2162163712 | bytes 11595776 | tf_op jit(solution)/shard_map/dot_general | solution.py:116
  201.3 2.4 convolution_bitcast_fusion.1
  204.0 9.0 %pad_maximum_fusion = f32[2048,3,1024]{2,0,1:T(8,128)} fusion(f32[2048,1,1024]{2,0,1:T(8,128)S(1)} %convolution_bitcast_fusion, f32[2048,1,1024]{2,0,1:T(8,128)S(1)} %convolution_bitcast_fusion.1, f32[2048,1,1024]{2,0,1:T(8,128)S(1)} %bitcast.145), kind=kLoop, calls=%fused_computation.2 | loop fusion | flops 12582912 | bytes 50331648 | tf_op jit(solution)/shard_map/stack | solution.py:120
  214.2 4.7 fusion.103
  219.0 2.4 fusion.105
  221.4 2.4 add_add_fusion
  223.9 2.0 copy-done.3
  225.9 2.1 fusion.106
  228.0 50.1 %all-reduce = (f32[1024]{0:T(1024)S(1)}, f32[6,2048]{1,0:T(8,128)S(1)}) all-reduce(f32[1024]{0:T(1024)S(1)} %bitcast.167, f32[6,2048]{1,0:T(8,128)S(1)} %fusion.106), channel_id=1, replica_groups=mesh['seq'=8,'dp'=4] {'seq','dp'}, use_global_device_ids=true, to_apply=%region_8.9 | all-reduce | flops 13312 | bytes 106496 | tf_op jit(solution)/shard_map/psum | solution.py:113
  279.3 3.9 convert_bitcast_fusion.1
  283.2 207.4 %reduce-scatter.2.cloned.1.call-done = f32[64,3,1024]{2,0,1:T(8,128)} async-done(((f32[2048,3,1024]{2,0,1:T(8,128)}), f32[64,3,1024]{2,0,1:T(8,128)}) %reduce-scatter.2.cloned.1.call-update) | async-done | bytes 786448 | tf_op jit(solution)/shard_map/reduce_scatter | solution.py:119
  490.6 2.1 broadcast_multiply_fusion
  (87 shorter events, 13.0 us)
Async XLA Ops:
  7.2 88.6 %all-gather.5.cloned.1.call-start = ((), (), s32[]{:S(2)}) async-start(), calls=%async_computation.2 | async-start | bytes 4718592 | tf_op jit(solution)/shard_map/all_gather | solution.py:20
  7.2 5.9 %copy-start.30 = (bf16[2048,1024]{1,0:T(8,128)(2,1)S(1)}, bf16[2048,1024]{1,0:T(8,128)(2,1)}, u32[]{:S(2)}) copy-start(bf16[2048,1024]{1,0:T(8,128)(2,1)} %param.17) | copy-start | bytes 12582916
  13.1 2.4 copy-start.17
  13.1 2.9 copy-start.28
  16.1 7.7 %copy-start.14 = (bf16[512,1024]{1,0:T(8,128)(2,1)}, bf16[512,1024]{1,0:T(8,128)(2,1)S(1)}, u32[]{:S(2)}) copy-start(bf16[512,1024]{1,0:T(8,128)(2,1)S(1)} %convolution_convert_fusion) | copy-start | bytes 3145732
  19.9 1.1 copy-start.16
  21.3 1.0 copy-start.11
  23.7 158.4 %all-gather.7.cloned.1.call-start = ((), (), s32[]{:S(2)}) async-start(), calls=%async_computation.3 | async-start | bytes 4718592 | tf_op jit(solution)/shard_map/all_gather | solution.py:20
  35.9 5.1 %copy-start.13 = (bf16[64,8,8,128]{3,2,1,0:T(8,128)(2,1)S(1)}, bf16[64,8,8,128]{3,2,1,0:T(8,128)(2,1)}, u32[]{:S(2)}) copy-start(bf16[64,8,8,128]{3,2,1,0:T(8,128)(2,1)} %copy.65) | copy-start | bytes 3145732
  39.0 2.0 copy-start
  99.6 2.5 copy-start.26
  102.1 2.3 copy-start.4
  103.4 1.0 copy-start.6
  105.6 3.1 copy-start.12
  105.6 384.9 %reduce-scatter.2.cloned.1.call-start = ((), (), s32[]{:S(2)}) async-start(), calls=%async_computation.1 | async-start | bytes 25952256 | tf_op jit(solution)/shard_map/reduce_scatter | solution.py:119
  108.7 3.8 copy-start.1
  108.7 2.0 copy-start.7
  115.5 4.4 copy-start.2
  115.5 4.4 copy-start.5
  119.9 2.1 copy-start.10
  119.9 3.1 copy-start.21
  121.9 2.8 copy-start.18
  123.7 1.0 copy-start.22
  182.2 5.2 %copy-start.8 = (f32[8,512,128]{1,2,0:T(8,128)S(1)}, f32[8,512,128]{1,2,0:T(8,128)}, u32[]{:S(2)}) copy-start(f32[8,512,128]{1,2,0:T(8,128)} %fusion.108) | copy-start | bytes 6291460
  187.3 2.9 copy-start.9
  187.3 2.9 copy-start.15
  190.2 3.8 copy-start.24
  194.0 5.7 %copy-start.20 = (f32[512,1024]{1,0:T(8,128)S(1)}, f32[512,1024]{1,0:T(8,128)}, u32[]{:S(2)}) copy-start(f32[512,1024]{1,0:T(8,128)} %get-tuple-element.126) | copy-start | bytes 6291460
  199.7 1.6 copy-start.19
  199.8 4.0 slice-start
  201.3 2.7 slice-start.1
  213.0 0.7 copy-start.27
  213.0 1.2 copy-start.23
  214.2 4.7 copy-start.29
  218.9 2.4 copy-start.25
  218.9 2.5 copy-start.31
  223.9 2.0 copy-start.3
Sparse Core Ops, SparseCore 0:
  23.9 71.8 all-gather.4
  105.7 76.3 all-gather.6
  213.1 277.3 reduce-scatter.1
where the time goes:
time: 509 us; the launch traced here: 500 us
  waiting for transfers between devices  311 us (61%)
  matrix products  67.1 us (13%)
  blocking collectives  50.1 us (10%)
  other arithmetic  32.1 us (6%)
  local copies, waits for them, and re-layouts  23.9 us (5%)
  between operations  14.7 us (3%)
    reduce_scatter x1, waiting for transfers between devices, body(): lax.psum_scatter(jnp.stack(products, axis=1), ('seq', 'dp'), scatter_dime...  207 us
    all_gather x2, waiting for transfers between devices, entering(): gathered = lax.all_gather(part, axis)  104 us
    psum x1, blocking collectives, body(): gain_sum, code_sum = lax.psum((gain_term, code_term), ('seq', 'dp'))  50.1 us
    unnamed x70, local copies, waits for them, and re-layouts  13.9 us
    dot_general x3, matrix products, body(): lax.dot_general(inputs, grad_part, row_dims, preferred_element_type=f32)  13.8 us
  transfers between devices with their start and end apart: 3, of which 3 were waited for; matrix products, arithmetic and copies ran while one was open for 11% of the time, Pallas kernels for 0%

commit v1 on v0

v1 whole, which is shorter than its diff:
```python
import functools
import math

import jax
import jax.numpy as jnp
from jax import lax
from jax.experimental import pallas as pl
from jax.experimental.pallas import tpu as pltpu
from jax.sharding import PartitionSpec as P

HEADS = 8
DH = 128
PAIR = 2
WIDE = PAIR * DH
AXES = ("seq", "dp")
F32 = jnp.float32
BF16 = jnp.bfloat16

fsq_levels = (8, 8, 8, 5, 5, 5)
fsq_bases = (1, 8, 64, 512, 2560, 12800)

NT = (((1,), (1,)), ((), ()))
TN = (((0,), (0,)), ((), ()))


def mm(a, b):
    return jnp.dot(a, b, preferred_element_type=F32)


def mm_nt(a, b):
    return lax.dot_general(a, b, NT, preferred_element_type=F32)


def mm_tn(a, b):
    return lax.dot_general(a, b, TN, preferred_element_type=F32)


def params():
    return pltpu.CompilerParams(vmem_limit_bytes=48 * 1024 * 1024)


def cost(flops, moved):
    return pl.CostEstimate(flops=int(flops), bytes_accessed=int(moved), transcendentals=0)


def shape(dims, dtype):
    return jax.ShapeDtypeStruct(dims, dtype)


def code_rows(token_ids):
    code_list = []
    for fsq_level, fsq_base in zip(fsq_levels, fsq_bases):
        fsq_digit = token_ids // fsq_base % fsq_level
        code_list.append((2.0 * fsq_digit.astype(F32) - (fsq_level - 1)) / (fsq_level - 1))
    return jnp.stack(code_list)


def silu_and_slope(value):
    sigma = 1.0 / (1.0 + jnp.exp(-value))
    return value * sigma, sigma * (1.0 + value * (1.0 - sigma))


def columns(rows):
    return pl.BlockSpec((rows, WIDE), lambda p, *_: (0, p))


def states():
    return pl.BlockSpec((PAIR, DH, DH), lambda p, *_: (p, 0, 0))


def picked_states():
    return pl.BlockSpec((1, PAIR, DH, DH), lambda p, owner: (owner[0] ^ p, 0, 0, 0))


def whole(dims):
    return pl.BlockSpec(dims, lambda p, *_: (0,) * len(dims))


def kv_kernel(x_ref, wk_ref, wv_ref, k_ref, slope_ref, v_ref, kv_ref):
    x = x_ref[...]
    key, slope = silu_and_slope(mm(x, wk_ref[...]))
    key = key.astype(BF16)
    value = mm(x, wv_ref[...]).astype(BF16)
    k_ref[...] = key
    slope_ref[...] = slope
    v_ref[...] = value
    for h in range(PAIR):
        at = slice(h * DH, (h + 1) * DH)
        kv_ref[h] = mm_tn(key[:, at], value[:, at])


def keys_values(x, w_key, w_value):
    t, d = x.shape
    hd = w_key.shape[1]
    return pl.pallas_call(
        kv_kernel,
        grid=(hd // WIDE,),
        in_specs=[whole((t, d)), columns(d), columns(d)],
        out_specs=[columns(t), columns(t), columns(t), states()],
        out_shape=[
            shape((t, hd), BF16),
            shape((t, hd), F32),
            shape((t, hd), BF16),
            shape((hd // DH, DH, DH), F32),
        ],
        compiler_params=params(),
        cost_estimate=cost(4 * t * d * hd, 4 * d * hd + 10 * t * hd),
        name="keys_values",
    )(x, w_key, w_value)


def causal_mask(t, transposed):
    rows = lax.broadcasted_iota(jnp.int32, (t, t), 0)
    cols = lax.broadcasted_iota(jnp.int32, (t, t), 1)
    return rows <= cols if transposed else cols <= rows


def query_kernel(x_ref, wq_ref, k_ref, v_ref, q_ref, slope_ref, sv_ref):
    t = x_ref.shape[0]
    query, slope = silu_and_slope(mm(x_ref[...], wq_ref[...]))
    query = query.astype(BF16)
    q_ref[...] = query
    slope_ref[...] = slope
    mask = causal_mask(t, False)
    for h in range(PAIR):
        at = slice(h * DH, (h + 1) * DH)
        scores = jnp.where(mask, mm_nt(query[:, at], k_ref[:, at]), 0.0).astype(BF16)
        sv_ref[:, at] = mm(scores, v_ref[:, at])


def queries_scores(x, w_query, keys, values):
    t, d = x.shape
    hd = w_query.shape[1]
    return pl.pallas_call(
        query_kernel,
        grid=(hd // WIDE,),
        in_specs=[whole((t, d)), columns(d), columns(t), columns(t)],
        out_specs=[columns(t), columns(t), columns(t)],
        out_shape=[shape((t, hd), BF16), shape((t, hd), F32), shape((t, hd), F32)],
        compiler_params=params(),
        cost_estimate=cost(2 * t * d * hd + 4 * t * t * hd, 2 * d * hd + 14 * t * hd),
        name="queries_scores",
    )(x, w_query, keys, values)


def norm_kernel(owner, sv_ref, q_ref, prefix_ref, og_ref, gain_ref, datt_ref, term_ref, grad_ref):
    for h in range(PAIR):
        at = slice(h * DH, (h + 1) * DH)
        query = q_ref[:, at]
        attended = sv_ref[:, at] + mm(query, prefix_ref[0, h].astype(BF16))
        inverse = lax.rsqrt(jnp.mean(attended * attended, axis=-1, keepdims=True) + 1e-06)
        normed = attended * inverse
        grad = og_ref[:, at].astype(F32)
        term_ref[:, at] = jnp.sum(grad * normed, axis=0, keepdims=True)
        d_normed = grad * gain_ref[:, at]
        inner = jnp.mean(d_normed * normed, axis=-1, keepdims=True)
        d_att = ((d_normed - normed * inner) * inverse).astype(BF16)
        datt_ref[:, at] = d_att
        grad_ref[h] = mm_tn(query, d_att)


def norm_gradient(owner, sv, queries, prefix, out_grad, gain):
    t, hd = sv.shape
    return pl.pallas_call(
        norm_kernel,
        grid_spec=pltpu.PrefetchScalarGridSpec(
            num_scalar_prefetch=1,
            grid=(hd // WIDE,),
            in_specs=[columns(t), columns(t), picked_states(), columns(t), columns(1)],
            out_specs=[columns(t), columns(1), states()],
        ),
        out_shape=[shape((t, hd), BF16), shape((1, hd), F32), shape((hd // DH, DH, DH), F32)],
        compiler_params=params(),
        cost_estimate=cost(4 * t * hd * DH, 10 * t * hd),
        name="norm_gradient",
    )(owner, sv, queries, prefix, out_grad, gain)


def dquery_kernel(owner, datt_ref, v_ref, k_ref, prefix_ref, slope_ref, g16_ref, g32_ref):
    t = datt_ref.shape[0]
    mask = causal_mask(t, False)
    for h in range(PAIR):
        at = slice(h * DH, (h + 1) * DH)
        d_att = datt_ref[:, at]
        back = jnp.where(mask, mm_nt(d_att, v_ref[:, at]), 0.0).astype(BF16)
        d_query = mm(back, k_ref[:, at]) + mm_nt(d_att, prefix_ref[0, h].astype(BF16))
        grad = (d_query * slope_ref[:, at]).astype(BF16)
        g16_ref[:, at] = grad
        g32_ref[:, at] = grad.astype(F32)


def query_gradient(owner, d_att, values, keys, prefix, slope):
    t, hd = d_att.shape
    return pl.pallas_call(
        dquery_kernel,
        grid_spec=pltpu.PrefetchScalarGridSpec(
            num_scalar_prefetch=1,
            grid=(hd // WIDE,),
            in_specs=[columns(t), columns(t), columns(t), picked_states(), columns(t)],
            out_specs=[columns(t), columns(t)],
        ),
        out_shape=[shape((t, hd), BF16), shape((t, hd), F32)],
        compiler_params=params(),
        cost_estimate=cost(4 * t * t * hd, 16 * t * hd),
        name="query_gradient",
    )(owner, d_att, values, keys, prefix, slope)


def within_kernel(datt_ref, v_ref, k_ref, q_ref, dk_ref, dv_ref):
    t = datt_ref.shape[0]
    mask = causal_mask(t, True)
    for h in range(PAIR):
        at = slice(h * DH, (h + 1) * DH)
        d_att, query = datt_ref[:, at], q_ref[:, at]
        back = jnp.where(mask, mm_nt(v_ref[:, at], d_att), 0.0).astype(BF16)
        dk_ref[:, at] = mm(back, query)
        scores = jnp.where(mask, mm_nt(k_ref[:, at], query), 0.0).astype(BF16)
        dv_ref[:, at] = mm(scores, d_att)


def within_block(d_att, values, keys, queries):
    t, hd = d_att.shape
    return pl.pallas_call(
        within_kernel,
        grid=(hd // WIDE,),
        in_specs=[columns(t)] * 4,
        out_specs=[columns(t), columns(t)],
        out_shape=[shape((t, hd), F32), shape((t, hd), F32)],
        compiler_params=params(),
        cost_estimate=cost(8 * t * t * hd, 16 * t * hd),
        name="within_block",
    )(d_att, values, keys, queries)


def dkv_kernel(owner, dk_ref, dv_ref, v_ref, k_ref, suffix_ref, slope_ref, k16, k32, v16, v32):
    for h in range(PAIR):
        at = slice(h * DH, (h + 1) * DH)
        suffix = suffix_ref[0, h].astype(BF16)
        grad = ((dk_ref[:, at] + mm_nt(v_ref[:, at], suffix)) * slope_ref[:, at]).astype(BF16)
        k16[:, at] = grad
        k32[:, at] = grad.astype(F32)
        grad = (dv_ref[:, at] + mm(k_ref[:, at], suffix)).astype(BF16)
        v16[:, at] = grad
        v32[:, at] = grad.astype(F32)


def key_value_gradients(owner, dk, dv, values, keys, suffix, slope):
    t, hd = dk.shape
    return pl.pallas_call(
        dkv_kernel,
        grid_spec=pltpu.PrefetchScalarGridSpec(
            num_scalar_prefetch=1,
            grid=(hd // WIDE,),
            in_specs=[columns(t)] * 4 + [picked_states(), columns(t)],
            out_specs=[columns(t)] * 4,
        ),
        out_shape=[shape((t, hd), BF16), shape((t, hd), F32)] * 2,
        compiler_params=params(),
        cost_estimate=cost(4 * t * hd * DH, 28 * t * hd),
        name="key_value_gradients",
    )(owner, dk, dv, values, keys, suffix, slope)


def exchange(array, axis, mask):
    count = lax.axis_size(axis)
    return lax.ppermute(array, axis, [(i, i ^ mask) for i in range(count)])


def entering(part, reverse):
    count = lax.axis_size("seq")
    group = min(HEADS // PAIR, count)
    clusters = count // group
    place = lax.axis_index("seq")
    if reverse:
        place = count - 1 - place
    inner, cluster = place % group, place // group
    twist = group // 2
    owner = inner ^ (twist * (cluster % 2))
    pieces = part.reshape(group, HEADS // group, DH, DH)

    def piece(index):
        return lax.dynamic_index_in_dim(pieces, index, 0, False)

    blocks = [piece(owner)]
    for mask in range(1, group):
        blocks.append(exchange(piece(owner ^ mask), "seq", mask))
    total = sum(blocks[1:], blocks[0])
    base = jnp.zeros_like(total)
    for shift in range(1, clusters):
        pairs = []
        for source in range(clusters - shift):
            for slot in range(group):
                a = source * group + (slot ^ (twist * (source % 2)))
                target = source + shift
                b = target * group + (slot ^ (twist * (target % 2)))
                pairs.append((count - 1 - a, count - 1 - b) if reverse else (a, b))
        base = base + lax.ppermute(total, "seq", pairs)
    outs = []
    for mask in range(group):
        local = base
        for other in range(group):
            if other != mask:
                local = local + jnp.where((inner ^ other) < (inner ^ mask), blocks[other], 0.0)
        outs.append(exchange(local, "seq", mask) if mask else local)
    return jnp.stack(outs), owner.astype(jnp.int32).reshape(1)


def sum_everywhere(array):
    for axis in AXES:
        step = 1
        while step < lax.axis_size(axis):
            array = array + exchange(array, axis, step)
            step *= 2
    return array


def merge_kernel(own_ref, other_ref, out_ref):
    half = own_ref.shape[1]
    out_ref[:, :half] = own_ref[...]
    out_ref[:, half:] = other_ref[...].astype(BF16)


def merge(own, other):
    rows, t = own.shape
    return pl.pallas_call(
        merge_kernel,
        out_shape=shape((rows, 2 * t), BF16),
        compiler_params=params(),
        cost_estimate=cost(0, 10 * rows * t),
        name="merge",
    )(own, other)


def product_kernel(picks, cuts, x_ref, own_ref, other_ref, *out_refs):
    grads = jnp.concatenate([own_ref[...], other_ref[...].astype(BF16)], axis=0)
    depth = grads.shape[0]
    for out_ref, pick, (start, stop) in zip(out_refs, picks, cuts):
        rows = x_ref[pick].reshape(-1, depth)
        out_ref[...] = mm(rows, grads[:, start:stop]).reshape(out_ref.shape)


def products(x, own, other, picks, cuts):
    dims = x.shape
    kept = math.prod(dims[:-1]) // 2
    return pl.pallas_call(
        functools.partial(product_kernel, picks, cuts),
        out_shape=[
            shape((2,) * (len(dims) - 3) + (dims[-2], stop - start), F32) for start, stop in cuts
        ],
        compiler_params=params(),
        cost_estimate=cost(2 * kept * dims[-1] * own.shape[1], 2 * x.size + 6 * own.size + 4 * kept * own.shape[1]),
        name="weight_products",
    )(x, own, other)


def at_axis(count, axis, index):
    return (slice(None),) * axis + (index,) + (slice(None),) * (count - axis - 1)


def scattered(x, own, other, masks, orders, cuts):
    count = len(masks)
    sent = products(x, own, other, [at_axis(count, order[0], 1) for order in orders], cuts)
    kept = products(x, own, other, [at_axis(count, order[0], 0) for order in orders], cuts)
    outs = []
    for order, first, rest in zip(orders, sent, kept):
        left = list(range(count))
        sending = first
        for at, axis in enumerate(order):
            got = both_exchange(sending, masks[axis])
            left.remove(axis)
            if at + 1 < len(order):
                place = left.index(order[at + 1])
                sending = rest[at_axis(len(left), place, 1)] + got[at_axis(len(left), place, 1)]
                rest = rest[at_axis(len(left), place, 0)] + got[at_axis(len(left), place, 0)]
            else:
                rest = rest + got
        outs.append(rest)
    return jnp.concatenate(outs, axis=-1)


def both_exchange(array, mask):
    total = lax.axis_size("seq") * lax.axis_size("dp")
    return lax.ppermute(array, AXES, [(i, i ^ mask) for i in range(total)])


def body(resid, token_ids, code_proj, w_query, w_key, w_value, gain, out_grad):
    positions, width = resid.shape[1:]
    features = w_query.shape[1]
    n_seq, n_dp = lax.axis_size("seq"), lax.axis_size("dp")
    total = n_seq * n_dp
    me = lax.axis_index("seq") * n_dp + lax.axis_index("dp")
    code_values = code_rows(token_ids[0])
    summed = resid[0].astype(F32)
    for index in range(code_values.shape[0]):
        summed = summed + code_values[index][:, None] * code_proj[index]
    inputs = summed.astype(BF16)

    keys, key_slope, values, block_kv = keys_values(inputs, w_key, w_value)
    prefix, owner = entering(block_kv, False)
    queries, query_slope, within = queries_scores(inputs, w_query, keys, values)

    bits = total.bit_length() - 1
    masks = [1 << b for b in range(1, bits)]
    masks[-1] |= masks[-2]
    rows = width // total
    turned = inputs.T.reshape(total // 2, 2, rows, positions)
    core, chip = me % 2, me // 2
    offsets = []
    for pick in range(1 << (bits - 1)):
        offset = 0
        for place, mask in enumerate(masks):
            if pick >> (bits - 2 - place) & 1:
                offset ^= mask >> 1
        offsets.append(offset)

    def ordered(which):
        mine = lax.dynamic_index_in_dim(turned, which, 1, False)
        return jnp.concatenate(
            [lax.dynamic_index_in_dim(mine, chip ^ offset, 0, False) for offset in offsets], axis=0
        )

    own_rows = ordered(core)
    other_rows = both_exchange(ordered(1 - core).astype(F32), 1)
    x = merge(own_rows, other_rows).reshape((2,) * (bits - 1) + (rows, 2 * positions))

    gain_row = gain.reshape(1, features)
    d_att, gain_term, block_grad = norm_gradient(
        owner, within, queries, prefix, out_grad[0], gain_row
    )
    suffix, back_owner = entering(block_grad, True)
    grad_q, wide_q = query_gradient(owner, d_att, values, keys, prefix, query_slope)

    dims = len(masks)
    orders = [tuple((start + i) % dims for i in range(dims)) for start in range(min(3, dims))]
    unit = features // 8
    cuts = [(0, 4 * unit), (4 * unit, 7 * unit), (7 * unit, 8 * unit)][: len(orders)]
    weight_q = scattered(x, grad_q, both_exchange(wide_q, 1), masks, orders, cuts)

    dk, dv = within_block(d_att, values, keys, queries)
    grad_k, wide_k, grad_v, wide_v = key_value_gradients(
        back_owner, dk, dv, values, keys, suffix, key_slope
    )
    weight_k = scattered(x, grad_k, both_exchange(wide_k, 1), masks, orders, cuts)
    weight_v = scattered(x, grad_v, both_exchange(wide_v, 1), masks, orders, cuts)

    input_grad = mm_nt(grad_q, w_query)
    input_grad = input_grad + mm_nt(grad_k, w_key)
    input_grad = input_grad + mm_nt(grad_v, w_value)
    resid_grad = input_grad.astype(BF16)[None]
    grad_scale = 1.0 / math.sqrt(positions * total)
    code_term = jnp.dot(code_values, input_grad, precision=lax.Precision.HIGHEST)
    small = jnp.concatenate([gain_term.reshape(-1), code_term.reshape(-1)]).reshape(-1, DH)
    small = sum_everywhere(small).reshape(-1) * grad_scale
    gain_sum, code_sum = small[:features], small[features:].reshape(code_term.shape)
    weights = jnp.stack([weight_q, weight_k, weight_v], axis=1) * grad_scale
    return resid_grad, weights, gain_sum, code_sum


def solution(mesh):
    return jax.shard_map(
        body,
        mesh=mesh,
        in_specs=(
            P("dp", "seq", None),
            P("dp", "seq"),
            P(),
            P(),
            P(),
            P(),
            P(),
            P("dp", "seq", None),
        ),
        out_specs=(P("dp", "seq", None), P(AXES, None, None), P(), P()),
        check_vma=False,
    )
```

time: 509 us -> 332 us (0.65)
  the two profiles are of different devices: /device:TPU:13 before, /device:TPU:0 now
where the time goes in v1:
time: 332 us; the launch traced here: 331 us
  waiting for transfers between devices  103 us (31%)
  starting transfers between devices  71.7 us (22%)
  Pallas kernels  66.3 us (20%)
  local copies, waits for them, and re-layouts  47.8 us (14%)
  other arithmetic  24.9 us (8%)
  matrix products  15.5 us (5%)
    ppermute x40, waiting for transfers between devices, both_exchange(): return lax.ppermute(array, AXES, [(i, i ^ mask) for i in range(total)])  88.9 us
    ppermute x40, starting transfers between devices, both_exchange(): return lax.ppermute(array, AXES, [(i, i ^ mask) for i in range(total)])  43.9 us
    unnamed x69, local copies, waits for them, and re-layouts  36.8 us
    ppermute x17, starting transfers between devices, exchange(): return lax.ppermute(array, axis, [(i, i ^ mask) for i in range(count)])  19.8 us
    pallas_call x6, Pallas kernels, products(): pl.pallas_call(functools.partial(product_kernel, picks, cuts), out_shape=...  19.1 us
    pallas_call x1, Pallas kernels, queries_scores(): pl.pallas_call(query_kernel, grid=(hd // WIDE,), in_specs=[whole((t, d)),...  12.8 us
    dot_general x3, matrix products, mm_nt(): return lax.dot_general(a, b, NT, preferred_element_type=F32)  11.2 us
    ppermute x17, waiting for transfers between devices, exchange(): return lax.ppermute(array, axis, [(i, i ^ mask) for i in range(count)])  11.2 us
  transfers between devices with their start and end apart: 59, of which 25 were waited for; matrix products, arithmetic and copies ran while one was open for 20% of the time, Pallas kernels for 17%

profile of v1, /device:TPU:0, one launch (start us, length us, event | category | flops | bytes accessed | tf_op | source)
XLA Modules:
  0.0 330.6 jit_solution(10871604442697759169)
XLA Ops:
  2.6 4.7 %fusion.5.x_ref = bf16[512,2048]{1,0:T(8,128)(2,1)} fusion(bf16[1,512,2048]{2,1,0:T(8,128)(2,1)} %param.8, f32[2048]{0:T(1024)S(1)} %bitcast.460, f32[512]{0:T(512)S(1)} %get-tuple-element.170, f32[2048]{0:T(1024)S(1)} %bitcast.462, f32[512]{0:T(512)S(1)} %get-tuple-element.168, f32[2048]{0:T(1024)S(1)} %bitcast.454, f32[512]{0:T(512)S(1)} %get-tuple-element.169, ...), kind=kLoop, calls=%fused_computation.6 | loop fusion | flops 14680064 | bytes 4255744 | tf_op jit(solution)/shard_map/convert_element_type | solution.py:396
  7.2 8.9 %keys_values.1 = (bf16[512,1024]{1,0:T(8,128)(2,1)S(1)}, f32[512,1024]{1,0:T(8,128)S(1)}, bf16[512,1024]{1,0:T(8,128)(2,1)S(1)}, f32[8,128,128]{2,1,0:T(8,128)S(1)}) custom-call(bf16[512,2048]{1,0:T(8,128)(2,1)} %fusion.5.x_ref, bf16[2048,1024]{1,0:T(8,128)(2,1)} %wk_ref.1, bf16[2048,1024]{1,0:T(8,128)(2,1)} %wv_ref.1), custom_call_target="tpu_custom_call" | custom-call | flops 4294967296 | bytes 13631488 | tf_op jit(solution)/shard_map/keys_values/pallas_call | solution.py:95
  17.6 3.0 collective-permute-start
  22.2 4.7 %fusion.152 = bf16[2048,512]{0,1:T(8,128)(2,1)} fusion(f32[2048]{0:T(1024)S(1)} %bitcast.461, f32[512]{0:T(512)S(1)} %get-tuple-element.170, f32[2048]{0:T(1024)S(1)} %bitcast.463, f32[512]{0:T(512)S(1)} %get-tuple-element.168, f32[2048]{0:T(1024)S(1)} %bitcast.455, f32[512]{0:T(512)S(1)} %get-tuple-element.169, f32[2048]{0:T(1024)S(1)} %bitcast.457, ...), kind=kLoop, calls=%fused_computation.338 | loop fusion | flops 14680064 | bytes 4255744 | tf_op jit(solution)/shard_map/transpose | solution.py:406
  26.9 3.9 %copy.60 = bf16[2048,512]{1,0:T(8,128)(2,1)} copy(bf16[2048,512]{0,1:T(8,128)(2,1)} %fusion.152) | data formatting | bytes 4194304 | tf_op jit(solution)/shard_map/transpose | solution.py:406
  52.3 6.6 %collective-permute-start.3 = (f32[2,128,128]{2,1,0:T(8,128)S(1)}, f32[2,128,128]{2,1,0:T(8,128)}, u32[]{:S(2)}, u32[]{:S(2)}) collective-permute-start(f32[2,128,128]{2,1,0:T(8,128)S(1)} %fusion.47), channel_id=1, source_target_pairs={{0,24},{4,28},{8,16},{12,20},{1,25},{5,29},{9,17},{13,21},{2,26},{... | collective-permute-start | bytes 393224 | tf_op jit(solution)/shard_map/ppermute | solution.py:297
  61.9 2.9 convert_element_type.85
  69.4 12.8 %queries_scores.1 = (bf16[512,1024]{1,0:T(8,128)(2,1)S(1)}, f32[512,1024]{1,0:T(8,128)S(1)}, f32[512,1024]{1,0:T(8,128)}) custom-call(bf16[512,2048]{1,0:T(8,128)(2,1)} %fusion.5.x_ref, bf16[2048,1024]{1,0:T(8,128)(2,1)} %wq_ref.1, bf16[512,1024]{1,0:T(8,128)(2,1)S(1)} %get-tuple-element.40.k_ref, bf16[512,1024]{1,0:T(8,128)(2,1)S(1)} %get-tuple-element.41.v_ref), custom_call_target="tpu_custom_call" | custom-call | flops 3221225472 | bytes 11534336 | tf_op jit(solution)/shard_map/queries_scores/pallas_call | solution.py:134
  88.5 4.5 %norm_gradient.1 = (bf16[512,1024]{1,0:T(8,128)(2,1)S(1)}, f32[1,1024]{1,0:T(1,128)S(1)}, f32[8,128,128]{2,1,0:T(8,128)S(1)}) custom-call(s32[1]{0:T(128)} %bitcast.owner, f32[512,1024]{1,0:T(8,128)} %get-tuple-element.42.sv_ref, bf16[512,1024]{1,0:T(8,128)(2,1)S(1)} %copy-done.10, f32[4,2,128,128]{3,2,1,0:T(8,128)S(1)} %pad_maximum_fusion.prefix_ref, ...), custom_call_target="tpu_custom_call" | custom-call | flops 268435456 | bytes 5242880 | tf_op jit(solution)/shard_map/norm_gradient/pallas_call | solution.py:164
  101.5 5.9 %query_gradient.1 = (bf16[512,1024]{1,0:T(8,128)(2,1)S(1)}, f32[512,1024]{1,0:T(8,128)}) custom-call(s32[1]{0:T(128)} %bitcast.owner, bf16[512,1024]{1,0:T(8,128)(2,1)S(1)} %copy-done.13, bf16[512,1024]{1,0:T(8,128)(2,1)S(1)} %copy-done.5, bf16[512,1024]{1,0:T(8,128)(2,1)S(1)} %get-tuple-element.40.k_ref, f32[4,2,128,128]{3,2,1,0:T(8,128)S(1)} %pad_maximum_fusion.prefix_ref, ...), custom_call_target="tpu_custom_call" | custom-call | flops 1073741824 | bytes 8388608 | tf_op jit(solution)/shard_map/query_gradient/pallas_call | solution.py:194
  109.0 4.4 %fusion.140 = f32[512,2048]{1,0:T(8,128)} fusion(bf16[512,1024]{1,0:T(8,128)(2,1)S(1)} %get-tuple-element.47.own_ref, bf16[2048,1024]{1,0:T(8,128)(2,1)S(1)} %copy-done.23), kind=kOutput, calls=%fused_computation.334 | convolution fusion | flops 2147483648 | bytes 9437184 | tf_op jit(solution)/shard_map/dot_general | solution.py:31
  113.4 2.8 collective-permute-done.10
  119.9 6.9 %within_block.1 = (f32[512,1024]{1,0:T(8,128)}, f32[512,1024]{1,0:T(8,128)}) custom-call(bf16[512,1024]{1,0:T(8,128)(2,1)S(1)} %copy-done.14, bf16[512,1024]{1,0:T(8,128)(2,1)S(1)} %copy-done.5, bf16[512,1024]{1,0:T(8,128)(2,1)S(1)} %get-tuple-element.40.k_ref, bf16[512,1024]{1,0:T(8,128)(2,1)S(1)} %copy-done.11), custom_call_target="tpu_custom_call" | custom-call | flops 2147483648 | bytes 8388608 | tf_op jit(solution)/shard_map/within_block/pallas_call | solution.py:223
  126.9 6.2 %key_value_gradients.1 = (bf16[512,1024]{1,0:T(8,128)(2,1)S(1)}, f32[512,1024]{1,0:T(8,128)}, bf16[512,1024]{1,0:T(8,128)(2,1)S(1)}, f32[512,1024]{1,0:T(8,128)}) custom-call(s32[1]{0:T(128)} %bitcast.20.owner, f32[512,1024]{1,0:T(8,128)} %get-tuple-element.48.dk_ref, f32[512,1024]{1,0:T(8,128)} %get-tuple-element.49.dv_ref, ...), custom_call_target="tpu_custom_call" | custom-call | flops 268435456 | bytes 14680064 | tf_op jit(solution)/shard_map/key_value_gradients/pallas_call | solution.py:249
  137.3 4.5 %add_add_fusion = f32[512,2048]{1,0:T(8,128)} fusion(f32[512,2048]{1,0:T(8,128)S(1)} %copy-done.26, f32[512,2048]{1,0:T(8,128)S(1)} %fusion.141, bf16[512,1024]{1,0:T(8,128)(2,1)S(1)} %get-tuple-element.53.own_ref, bf16[2048,1024]{1,0:T(8,128)(2,1)S(1)} %copy-done.25), kind=kOutput, calls=%fused_computation.7 | convolution fusion | flops 2149580800 | bytes 17825792 | tf_op jit(solution)/shard_map/dot_general | solution.py:31
  141.7 4.3 %fusion.142 = f32[6,2048]{1,0:T(8,128)S(1)} fusion(f32[6,512]{1,0:T(8,128)S(1)} %copy-done.21, f32[512,2048]{1,0:T(8,128)} %add_add_fusion), kind=kOutput, calls=%fused_computation.336 | convolution fusion | flops 75497472 | bytes 4255744 | tf_op jit(solution)/shard_map/dot_general | solution.py:451
  147.6 2.6 collective-permute-done.54
  151.3 3.2 collective-permute-done.55
  154.7 5.4 %collective-permute-done.56 = f32[104,128]{1,0:T(8,128)S(1)} collective-permute-done((f32[104,128]{1,0:T(8,128)S(1)}, f32[104,128]{1,0:T(8,128)S(1)}, u32[]{:S(2)}, u32[]{:S(2)}) %collective-permute-start.56) | collective-permute-done | bytes 53280 | tf_op jit(solution)/shard_map/ppermute | solution.py:266
  160.2 3.8 %convert_bitcast_fusion = bf16[1,512,2048]{2,1,0:T(8,128)(2,1)} fusion(f32[512,2048]{1,0:T(8,128)} %add_add_fusion), kind=kLoop, calls=%fused_computation.8 | loop fusion | flops 1048576 | bytes 6291456 | tf_op jit(solution)/shard_map/broadcast_in_dim | solution.py:449
  167.7 3.1 weight_products.7
  174.6 3.3 weight_products.6
  177.9 4.2 %collective-permute-done.24 = f32[2,2,2,64,128]{4,3,1,2,0:T(8,128)S(1)} collective-permute-done((f32[2,2,2,64,128]{4,3,1,2,0:T(8,128)}, f32[2,2,2,64,128]{4,3,1,2,0:T(8,128)S(1)}, u32[]{:S(2)}, u32[]{:S(2)}) %collective-permute-start.24) | collective-permute-done | bytes 262176 | tf_op jit(solution)/shard_map/ppermute | solution.py:383
  189.6 3.1 weight_products.9
  194.3 3.4 %weight_products.11 = (f32[2,2,2,64,512]{4,3,2,1,0:T(8,128)S(1)}, f32[2,2,2,64,384]{4,3,2,1,0:T(8,128)S(1)}, f32[2,2,2,64,128]{4,3,2,1,0:T(8,128)S(1)}) custom-call(bf16[2,2,2,2,64,1024]{5,4,3,2,1,0:T(8,128)(2,1)S(1)} %bitcast.416, bf16[512,1024]{1,0:T(8,128)(2,1)S(1)} %copy-done.1, f32[512,1024]{1,0:T(8,128)} %collective-permute-done.41.other_ref), custom_call_target="tpu_custom_call" | custom-call | flops 1073741824 | bytes 7340032 | tf_op jit(solution)/shard_map/weight_products/pallas_call | solution.py:345
  199.2 3.1 weight_products.8
  202.3 9.1 %collective-permute-done.26 = f32[2,64,128]{2,1,0:T(8,128)S(1)} collective-permute-done((f32[2,64,128]{2,1,0:T(8,128)S(1)}, f32[2,64,128]{2,1,0:T(8,128)S(1)}, u32[]{:S(2)}, u32[]{:S(2)}) %collective-permute-start.26) | collective-permute-done | bytes 65568 | tf_op jit(solution)/shard_map/ppermute | solution.py:383
  212.9 3.1 weight_products.10
  218.1 6.3 %collective-permute-done.37 = f32[2,2,2,64,128]{4,3,1,2,0:T(8,128)S(1)} collective-permute-done((f32[2,2,2,64,128]{4,3,1,2,0:T(8,128)S(1)}, f32[2,2,2,64,128]{4,3,1,2,0:T(8,128)S(1)}, u32[]{:S(2)}, u32[]{:S(2)}) %collective-permute-start.37) | collective-permute-done | bytes 262176 | tf_op jit(solution)/shard_map/ppermute | solution.py:383
  225.6 4.1 %collective-permute-start.38 = (f32[2,2,64,128]{3,2,1,0:T(8,128)S(1)}, f32[2,2,64,128]{3,2,1,0:T(8,128)S(1)}, u32[]{:S(2)}, u32[]{:S(2)}) collective-permute-start(f32[2,2,64,128]{3,2,1,0:T(8,128)S(1)} %get-tuple-element.141), channel_id=1, source_target_pairs={{0,24},{1,25},{2,26},{3,27},{4,28},{5,29},{6,30},{7,31},{8,16},{9,... | collective-permute-start | bytes 393224 | tf_op jit(solution)/shard_map/ppermute | solution.py:383
  230.9 2.8 collective-permute-done.38
  233.6 2.8 collective-permute-start.51
  236.5 3.9 %collective-permute-done.51 = f32[2,2,64,128]{3,2,1,0:T(8,128)S(1)} collective-permute-done((f32[2,2,64,128]{3,2,1,0:T(8,128)S(1)}, f32[2,2,64,128]{3,2,1,0:T(8,128)S(1)}, u32[]{:S(2)}, u32[]{:S(2)}) %collective-permute-start.51) | collective-permute-done | bytes 131104 | tf_op jit(solution)/shard_map/ppermute | solution.py:383
  240.9 3.7 %collective-permute-done.39 = f32[2,64,128]{2,1,0:T(8,128)S(1)} collective-permute-done((f32[2,64,128]{2,1,0:T(8,128)S(1)}, f32[2,64,128]{2,1,0:T(8,128)S(1)}, u32[]{:S(2)}, u32[]{:S(2)}) %collective-permute-start.39) | collective-permute-done | bytes 65568 | tf_op jit(solution)/shard_map/ppermute | solution.py:383
  245.2 3.7 %collective-permute-done.52 = f32[2,64,128]{2,1,0:T(8,128)S(1)} collective-permute-done((f32[2,64,128]{2,1,0:T(8,128)S(1)}, f32[2,64,128]{2,1,0:T(8,128)S(1)}, u32[]{:S(2)}, u32[]{:S(2)}) %collective-permute-start.52) | collective-permute-done | bytes 65568 | tf_op jit(solution)/shard_map/ppermute | solution.py:383
  249.9 2.9 collective-permute-done.40
  253.8 2.9 collective-permute-done.53
  258.8 11.6 %collective-permute-done.21 = f32[2,2,64,384]{3,2,1,0:T(8,128)S(1)} collective-permute-done((f32[2,2,64,384]{3,2,1,0:T(8,128)S(1)}, f32[2,2,64,384]{3,2,1,0:T(8,128)S(1)}, u32[]{:S(2)}, u32[]{:S(2)}) %collective-permute-start.21) | collective-permute-done | bytes 393248 | tf_op jit(solution)/shard_map/ppermute | solution.py:383
  274.1 7.1 %collective-permute-done.22 = f32[2,64,384]{2,1,0:T(8,128)S(1)} collective-permute-done((f32[2,64,384]{2,1,0:T(8,128)S(1)}, f32[2,64,384]{2,1,0:T(8,128)S(1)}, u32[]{:S(2)}, u32[]{:S(2)}) %collective-permute-start.22) | collective-permute-done | bytes 196640 | tf_op jit(solution)/shard_map/ppermute | solution.py:383
  282.1 3.8 %collective-permute-start.30 = (f32[2,2,64,512]{3,2,1,0:T(8,128)S(1)}, f32[2,2,64,512]{3,2,1,0:T(8,128)S(1)}, u32[]{:S(2)}, u32[]{:S(2)}) collective-permute-start(f32[2,2,64,512]{3,2,1,0:T(8,128)S(1)} %get-tuple-element.79), channel_id=1, source_target_pairs={{0,4},{1,5},{2,6},{3,7},{4,0},{5,1},{6,2},{7,3},{8,12},{9,13},{10,... | collective-permute-start | bytes 1572872 | tf_op jit(solution)/shard_map/ppermute | solution.py:383
  286.2 3.5 %collective-permute-start.43 = (f32[2,2,64,512]{3,2,1,0:T(8,128)S(1)}, f32[2,2,64,512]{3,2,1,0:T(8,128)S(1)}, u32[]{:S(2)}, u32[]{:S(2)}) collective-permute-start(f32[2,2,64,512]{3,2,1,0:T(8,128)S(1)} %get-tuple-element.81), channel_id=1, source_target_pairs={{0,4},{1,5},{2,6},{3,7},{4,0},{5,1},{6,2},{7,3},{8,12},{9,13},{10,... | collective-permute-start | bytes 1572872 | tf_op jit(solution)/shard_map/ppermute | solution.py:383
  290.0 4.2 %collective-permute-start.35 = (f32[2,64,384]{2,1,0:T(8,128)S(1)}, f32[2,64,384]{2,1,0:T(8,128)S(1)}, u32[]{:S(2)}, u32[]{:S(2)}) collective-permute-start(f32[2,64,384]{2,1,0:T(8,128)S(1)} %get-tuple-element.127), channel_id=1, source_target_pairs={{0,24},{1,25},{2,26},{3,27},{4,28},{5,29},{6,30},{7,31},{8,16},{9,... | collective-permute-start | bytes 589832 | tf_op jit(solution)/shard_map/ppermute | solution.py:383
  294.8 10.8 %collective-permute-done.35 = f32[2,64,384]{2,1,0:T(8,128)S(1)} collective-permute-done((f32[2,64,384]{2,1,0:T(8,128)S(1)}, f32[2,64,384]{2,1,0:T(8,128)S(1)}, u32[]{:S(2)}, u32[]{:S(2)}) %collective-permute-start.35) | collective-permute-done | bytes 196640 | tf_op jit(solution)/shard_map/ppermute | solution.py:383
  306.1 2.5 collective-permute-done.48
  310.3 3.0 collective-permute-done.49
  316.9 3.0 collective-permute-done.31
  323.9 3.0 collective-permute-done.32
  326.9 2.6 collective-permute-done.45
  (230 shorter events, 106.5 us)
Async XLA Ops:
  17.6 34.7 %collective-permute-start = (f32[2,128,128]{2,1,0:T(8,128)S(1)}, f32[2,128,128]{2,1,0:T(8,128)S(1)}, u32[]{:S(2)}, u32[]{:S(2)}) collective-permute-start(f32[2,128,128]{2,1,0:T(8,128)S(1)} %get-tuple-element.145), channel_id=1, source_target_pairs={{0,4},{4,0},{8,12},{12,8},{16,20},{20,16},{24,28},{28,24},{1,5},{5... | collective-permute-start | bytes 393224 | tf_op jit(solution)/shard_map/ppermute | solution.py:266
  20.6 31.6 %collective-permute-start.1 = (f32[2,128,128]{2,1,0:T(8,128)S(1)}, f32[2,128,128]{2,1,0:T(8,128)S(1)}, u32[]{:S(2)}, u32[]{:S(2)}) collective-permute-start(f32[2,128,128]{2,1,0:T(8,128)S(1)} %get-tuple-element.147), channel_id=1, source_target_pairs={{0,8},{4,12},{8,0},{12,4},{16,24},{20,28},{24,16},{28,20},{1,9},{5... | collective-permute-start | bytes 393224 | tf_op jit(solution)/shard_map/ppermute | solution.py:266
  22.2 30.1 %collective-permute-start.2 = (f32[2,128,128]{2,1,0:T(8,128)S(1)}, f32[2,128,128]{2,1,0:T(8,128)S(1)}, u32[]{:S(2)}, u32[]{:S(2)}) collective-permute-start(f32[2,128,128]{2,1,0:T(8,128)S(1)} %get-tuple-element.146), channel_id=1, source_target_pairs={{0,12},{4,8},{8,4},{12,0},{16,28},{20,24},{24,20},{28,16},{1,13},{... | collective-permute-start | bytes 393224 | tf_op jit(solution)/shard_map/ppermute | solution.py:266
  52.3 12.5 %collective-permute-start.3 = (f32[2,128,128]{2,1,0:T(8,128)S(1)}, f32[2,128,128]{2,1,0:T(8,128)}, u32[]{:S(2)}, u32[]{:S(2)}) collective-permute-start(f32[2,128,128]{2,1,0:T(8,128)S(1)} %fusion.47), channel_id=1, source_target_pairs={{0,24},{4,28},{8,16},{12,20},{1,25},{5,29},{9,17},{13,21},{2,26},{... | collective-permute-start | bytes 393224 | tf_op jit(solution)/shard_map/ppermute | solution.py:297
  64.8 100.8 %collective-permute-start.14 = (f32[1024,512]{1,0:T(8,128)}, f32[1024,512]{1,0:T(8,128)}, u32[]{:S(2)}, u32[]{:S(2)}) collective-permute-start(f32[1024,512]{1,0:T(8,128)} %convert_element_type.85), channel_id=1, source_target_pairs={{0,1},{1,0},{2,3},{3,2},{4,5},{5,4},{6,7},{7,6},{8,9},{9,8},{10,11... | collective-permute-start | bytes 6291464 | tf_op jit(solution)/shard_map/ppermute | solution.py:383
  65.8 18.6 %collective-permute-start.4 = (f32[2,128,128]{2,1,0:T(8,128)S(1)}, f32[2,128,128]{2,1,0:T(8,128)S(1)}, u32[]{:S(2)}, u32[]{:S(2)}) collective-permute-start(f32[2,128,128]{2,1,0:T(8,128)S(1)} %get-tuple-element.133), channel_id=1, source_target_pairs={{0,4},{4,0},{8,12},{12,8},{16,20},{20,16},{24,28},{28,24},{1,5},{5... | collective-permute-start | bytes 393224 | tf_op jit(solution)/shard_map/ppermute | solution.py:266
  67.4 17.0 %collective-permute-start.5 = (f32[2,128,128]{2,1,0:T(8,128)S(1)}, f32[2,128,128]{2,1,0:T(8,128)S(1)}, u32[]{:S(2)}, u32[]{:S(2)}) collective-permute-start(f32[2,128,128]{2,1,0:T(8,128)S(1)} %get-tuple-element.135), channel_id=1, source_target_pairs={{0,8},{4,12},{8,0},{12,4},{16,24},{20,28},{24,16},{28,20},{1,9},{5... | collective-permute-start | bytes 393224 | tf_op jit(solution)/shard_map/ppermute | solution.py:266
  67.4 17.0 %collective-permute-start.6 = (f32[2,128,128]{2,1,0:T(8,128)S(1)}, f32[2,128,128]{2,1,0:T(8,128)S(1)}, u32[]{:S(2)}, u32[]{:S(2)}) collective-permute-start(f32[2,128,128]{2,1,0:T(8,128)S(1)} %get-tuple-element.134), channel_id=1, source_target_pairs={{0,12},{4,8},{8,4},{12,0},{16,28},{20,24},{24,20},{28,16},{1,13},{... | collective-permute-start | bytes 393224 | tf_op jit(solution)/shard_map/ppermute | solution.py:266
  94.7 12.7 %collective-permute-start.7 = (f32[2,128,128]{2,1,0:T(8,128)}, f32[2,128,128]{2,1,0:T(8,128)S(1)}, u32[]{:S(2)}, u32[]{:S(2)}) collective-permute-start(f32[2,128,128]{2,1,0:T(8,128)} %get-tuple-element.142), channel_id=1, source_target_pairs={{0,4},{4,0},{8,12},{12,8},{16,20},{20,16},{24,28},{28,24},{1,5},{5... | collective-permute-start | bytes 393224 | tf_op jit(solution)/shard_map/ppermute | solution.py:266
  96.3 11.1 %collective-permute-start.8 = (f32[2,128,128]{2,1,0:T(8,128)}, f32[2,128,128]{2,1,0:T(8,128)S(1)}, u32[]{:S(2)}, u32[]{:S(2)}) collective-permute-start(f32[2,128,128]{2,1,0:T(8,128)} %get-tuple-element.144), channel_id=1, source_target_pairs={{0,8},{4,12},{8,0},{12,4},{16,24},{20,28},{24,16},{28,20},{1,9},{5... | collective-permute-start | bytes 393224 | tf_op jit(solution)/shard_map/ppermute | solution.py:266
  96.3 11.1 %collective-permute-start.9 = (f32[2,128,128]{2,1,0:T(8,128)}, f32[2,128,128]{2,1,0:T(8,128)S(1)}, u32[]{:S(2)}, u32[]{:S(2)}) collective-permute-start(f32[2,128,128]{2,1,0:T(8,128)} %get-tuple-element.143), channel_id=1, source_target_pairs={{0,12},{4,8},{8,4},{12,0},{16,28},{20,24},{24,20},{28,16},{1,13},{... | collective-permute-start | bytes 393224 | tf_op jit(solution)/shard_map/ppermute | solution.py:266
  107.5 8.8 %collective-permute-start.10 = (f32[2,128,128]{2,1,0:T(8,128)S(1)}, f32[2,128,128]{2,1,0:T(8,128)S(1)}, u32[]{:S(2)}, u32[]{:S(2)}) collective-permute-start(f32[2,128,128]{2,1,0:T(8,128)S(1)} %fusion.36), channel_id=1, source_target_pairs={{28,4},{24,0},{20,12},{16,8},{29,5},{25,1},{21,13},{17,9},{30,6},{... | collective-permute-start | bytes 393224 | tf_op jit(solution)/shard_map/ppermute | solution.py:297
  113.4 54.3 %collective-permute-start.15 = (f32[512,1024]{1,0:T(8,128)}, f32[512,1024]{1,0:T(8,128)}, u32[]{:S(2)}, u32[]{:S(2)}) collective-permute-start(f32[512,1024]{1,0:T(8,128)} %get-tuple-element.54), channel_id=1, source_target_pairs={{0,1},{1,0},{2,3},{3,2},{4,5},{5,4},{6,7},{7,6},{8,9},{9,8},{10,11... | collective-permute-start | bytes 6291464 | tf_op jit(solution)/shard_map/ppermute | solution.py:383
  116.3 10.5 %collective-permute-start.11 = (f32[2,128,128]{2,1,0:T(8,128)S(1)}, f32[2,128,128]{2,1,0:T(8,128)S(1)}, u32[]{:S(2)}, u32[]{:S(2)}) collective-permute-start(f32[2,128,128]{2,1,0:T(8,128)S(1)} %get-tuple-element.130), channel_id=1, source_target_pairs={{0,4},{4,0},{8,12},{12,8},{16,20},{20,16},{24,28},{28,24},{1,5},{5... | collective-permute-start | bytes 393224 | tf_op jit(solution)/shard_map/ppermute | solution.py:266
  117.9 8.9 %collective-permute-start.12 = (f32[2,128,128]{2,1,0:T(8,128)S(1)}, f32[2,128,128]{2,1,0:T(8,128)S(1)}, u32[]{:S(2)}, u32[]{:S(2)}) collective-permute-start(f32[2,128,128]{2,1,0:T(8,128)S(1)} %get-tuple-element.132), channel_id=1, source_target_pairs={{0,8},{4,12},{8,0},{12,4},{16,24},{20,28},{24,16},{28,20},{1,9},{5... | collective-permute-start | bytes 393224 | tf_op jit(solution)/shard_map/ppermute | solution.py:266
  118.8 8.0 %collective-permute-start.13 = (f32[2,128,128]{2,1,0:T(8,128)S(1)}, f32[2,128,128]{2,1,0:T(8,128)S(1)}, u32[]{:S(2)}, u32[]{:S(2)}) collective-permute-start(f32[2,128,128]{2,1,0:T(8,128)S(1)} %get-tuple-element.131), channel_id=1, source_target_pairs={{0,12},{4,8},{8,4},{12,0},{16,28},{20,24},{24,20},{28,16},{1,13},{... | collective-permute-start | bytes 393224 | tf_op jit(solution)/shard_map/ppermute | solution.py:266
  147.6 42.0 %collective-permute-start.28 = (f32[512,1024]{1,0:T(8,128)}, f32[512,1024]{1,0:T(8,128)}, u32[]{:S(2)}, u32[]{:S(2)}) collective-permute-start(f32[512,1024]{1,0:T(8,128)} %get-tuple-element.61), channel_id=1, source_target_pairs={{0,1},{1,0},{2,3},{3,2},{4,5},{5,4},{6,7},{7,6},{8,9},{9,8},{10,11... | collective-permute-start | bytes 6291464 | tf_op jit(solution)/shard_map/ppermute | solution.py:383
  151.3 43.0 %collective-permute-start.41 = (f32[512,1024]{1,0:T(8,128)}, f32[512,1024]{1,0:T(8,128)}, u32[]{:S(2)}, u32[]{:S(2)}) collective-permute-start(f32[512,1024]{1,0:T(8,128)} %get-tuple-element.68), channel_id=1, source_target_pairs={{0,1},{1,0},{2,3},{3,2},{4,5},{5,4},{6,7},{7,6},{8,9},{9,8},{10,11... | collective-permute-start | bytes 6291464 | tf_op jit(solution)/shard_map/ppermute | solution.py:383
  154.4 5.7 %collective-permute-start.56 = (f32[104,128]{1,0:T(8,128)S(1)}, f32[104,128]{1,0:T(8,128)S(1)}, u32[]{:S(2)}, u32[]{:S(2)}) collective-permute-start(f32[104,128]{1,0:T(8,128)S(1)} %fusion.151), channel_id=1, source_target_pairs={{0,16},{4,20},{8,24},{12,28},{16,0},{20,4},{24,8},{28,12},{1,17},{... | collective-permute-start | bytes 159752 | tf_op jit(solution)/shard_map/ppermute | solution.py:266
  164.0 9.9 %collective-permute-start.58 = (f32[104,128]{1,0:T(8,128)S(1)}, f32[104,128]{1,0:T(8,128)S(1)}, u32[]{:S(2)}, u32[]{:S(2)}) collective-permute-start(f32[104,128]{1,0:T(8,128)S(1)} %add.1022), channel_id=1, source_target_pairs={{0,2},{1,3},{2,0},{3,1},{4,6},{5,7},{6,4},{7,5},{8,10},{9,11},{10,... | collective-permute-start | bytes 159752 | tf_op jit(solution)/shard_map/ppermute | solution.py:266
  173.4 8.6 %collective-permute-start.24 = (f32[2,2,2,64,128]{4,3,1,2,0:T(8,128)}, f32[2,2,2,64,128]{4,3,1,2,0:T(8,128)S(1)}, u32[]{:S(2)}, u32[]{:S(2)}) collective-permute-start(f32[2,2,2,64,128]{4,3,1,2,0:T(8,128)} %copy.65), channel_id=1, source_target_pairs={{0,8},{1,9},{2,10},{3,11},{4,12},{5,13},{6,14},{7,15},{8,0},{9,1},... | collective-permute-start | bytes 786440 | tf_op jit(solution)/shard_map/ppermute | solution.py:383
  182.1 6.9 %collective-permute-start.25 = (f32[2,2,64,128]{3,2,1,0:T(8,128)S(1)}, f32[2,2,64,128]{3,2,1,0:T(8,128)S(1)}, u32[]{:S(2)}, u32[]{:S(2)}) collective-permute-start(f32[2,2,64,128]{3,2,1,0:T(8,128)S(1)} %get-tuple-element.139), channel_id=1, source_target_pairs={{0,24},{1,25},{2,26},{3,27},{4,28},{5,29},{6,30},{7,31},{8,16},{9,... | collective-permute-start | bytes 393224 | tf_op jit(solution)/shard_map/ppermute | solution.py:383
  183.9 72.9 %collective-permute-start.16 = (f32[2,2,2,64,512]{4,3,2,1,0:T(8,128)S(1)}, f32[2,2,2,64,512]{4,3,2,1,0:T(8,128)}, u32[]{:S(2)}, u32[]{:S(2)}) collective-permute-start(f32[2,2,2,64,512]{4,3,2,1,0:T(8,128)S(1)} %copy-done.19), channel_id=1, source_target_pairs={{0,2},{1,3},{2,0},{3,1},{4,6},{5,7},{6,4},{7,5},{8,10},{9,11},{10,... | collective-permute-start | bytes 3145736 | tf_op jit(solution)/shard_map/ppermute | solution.py:383
  185.4 40.2 %collective-permute-start.20 = (f32[2,2,2,64,384]{4,3,2,0,1:T(8,128)}, f32[2,2,2,64,384]{4,3,2,0,1:T(8,128)}, u32[]{:S(2)}, u32[]{:S(2)}) collective-permute-start(f32[2,2,2,64,384]{4,3,2,0,1:T(8,128)} %copy.62), channel_id=1, source_target_pairs={{0,4},{1,5},{2,6},{3,7},{4,0},{5,1},{6,2},{7,3},{8,12},{9,13},{10,... | collective-permute-start | bytes 2359304 | tf_op jit(solution)/shard_map/ppermute | solution.py:383
  189.0 22.4 %collective-permute-start.26 = (f32[2,64,128]{2,1,0:T(8,128)S(1)}, f32[2,64,128]{2,1,0:T(8,128)S(1)}, u32[]{:S(2)}, u32[]{:S(2)}) collective-permute-start(f32[2,64,128]{2,1,0:T(8,128)S(1)} %get-tuple-element.149), channel_id=1, source_target_pairs={{0,2},{1,3},{2,0},{3,1},{4,6},{5,7},{6,4},{7,5},{8,10},{9,11},{10,... | collective-permute-start | bytes 196616 | tf_op jit(solution)/shard_map/ppermute | solution.py:383
  192.7 88.5 %collective-permute-start.29 = (f32[2,2,2,64,512]{4,3,2,1,0:T(8,128)S(1)}, f32[2,2,2,64,512]{4,3,2,1,0:T(8,128)S(1)}, u32[]{:S(2)}, u32[]{:S(2)}) collective-permute-start(f32[2,2,2,64,512]{4,3,2,1,0:T(8,128)S(1)} %get-tuple-element.63), channel_id=1, source_target_pairs={{0,2},{1,3},{2,0},{3,1},{4,6},{5,7},{6,4},{7,5},{8,10},{9,11},{10,... | collective-permute-start | bytes 3145736 | tf_op jit(solution)/shard_map/ppermute | solution.py:383
  197.7 20.3 %collective-permute-start.50 = (f32[2,2,2,64,128]{4,3,2,1,0:T(8,128)S(1)}, f32[2,2,2,64,128]{4,3,2,1,0:T(8,128)S(1)}, u32[]{:S(2)}, u32[]{:S(2)}) collective-permute-start(f32[2,2,2,64,128]{4,3,2,1,0:T(8,128)S(1)} %get-tuple-element.74), channel_id=1, source_target_pairs={{0,8},{1,9},{2,10},{3,11},{4,12},{5,13},{6,14},{7,15},{8,0},{9,1},... | collective-permute-start | bytes 786440 | tf_op jit(solution)/shard_map/ppermute | solution.py:383
  216.1 55.3 %collective-permute-start.33 = (f32[2,2,2,64,384]{4,3,2,0,1:T(8,128)S(1)}, f32[2,2,2,64,384]{4,3,2,0,1:T(8,128)S(1)}, u32[]{:S(2)}, u32[]{:S(2)}) collective-permute-start(f32[2,2,2,64,384]{4,3,2,0,1:T(8,128)S(1)} %copy.68), channel_id=1, source_target_pairs={{0,4},{1,5},{2,6},{3,7},{4,0},{5,1},{6,2},{7,3},{8,12},{9,13},{10,... | collective-permute-start | bytes 2359304 | tf_op jit(solution)/shard_map/ppermute | solution.py:383
  218.0 6.4 %collective-permute-start.37 = (f32[2,2,2,64,128]{4,3,1,2,0:T(8,128)S(1)}, f32[2,2,2,64,128]{4,3,1,2,0:T(8,128)S(1)}, u32[]{:S(2)}, u32[]{:S(2)}) collective-permute-start(f32[2,2,2,64,128]{4,3,1,2,0:T(8,128)S(1)} %copy.71), channel_id=1, source_target_pairs={{0,8},{1,9},{2,10},{3,11},{4,12},{5,13},{6,14},{7,15},{8,0},{9,1},... | collective-permute-start | bytes 786440 | tf_op jit(solution)/shard_map/ppermute | solution.py:383
  224.4 49.5 %collective-permute-start.46 = (f32[2,2,2,64,384]{4,3,2,1,0:T(8,128)S(1)}, f32[2,2,2,64,384]{4,3,2,1,0:T(8,128)S(1)}, u32[]{:S(2)}, u32[]{:S(2)}) collective-permute-start(f32[2,2,2,64,384]{4,3,2,1,0:T(8,128)S(1)} %get-tuple-element.72), channel_id=1, source_target_pairs={{0,4},{1,5},{2,6},{3,7},{4,0},{5,1},{6,2},{7,3},{8,12},{9,13},{10,... | collective-permute-start | bytes 2359304 | tf_op jit(solution)/shard_map/ppermute | solution.py:383
  225.6 8.0 %collective-permute-start.38 = (f32[2,2,64,128]{3,2,1,0:T(8,128)S(1)}, f32[2,2,64,128]{3,2,1,0:T(8,128)S(1)}, u32[]{:S(2)}, u32[]{:S(2)}) collective-permute-start(f32[2,2,64,128]{3,2,1,0:T(8,128)S(1)} %get-tuple-element.141), channel_id=1, source_target_pairs={{0,24},{1,25},{2,26},{3,27},{4,28},{5,29},{6,30},{7,31},{8,16},{9,... | collective-permute-start | bytes 393224 | tf_op jit(solution)/shard_map/ppermute | solution.py:383
  233.6 6.8 %collective-permute-start.51 = (f32[2,2,64,128]{3,2,1,0:T(8,128)S(1)}, f32[2,2,64,128]{3,2,1,0:T(8,128)S(1)}, u32[]{:S(2)}, u32[]{:S(2)}) collective-permute-start(f32[2,2,64,128]{3,2,1,0:T(8,128)S(1)} %fusion.22), channel_id=1, source_target_pairs={{0,24},{1,25},{2,26},{3,27},{4,28},{5,29},{6,30},{7,31},{8,16},{9,... | collective-permute-start | bytes 393224 | tf_op jit(solution)/shard_map/ppermute | solution.py:383
  256.7 13.6 %collective-permute-start.21 = (f32[2,2,64,384]{3,2,1,0:T(8,128)S(1)}, f32[2,2,64,384]{3,2,1,0:T(8,128)S(1)}, u32[]{:S(2)}, u32[]{:S(2)}) collective-permute-start(f32[2,2,64,384]{3,2,1,0:T(8,128)S(1)} %get-tuple-element.115), channel_id=1, source_target_pairs={{0,8},{1,9},{2,10},{3,11},{4,12},{5,13},{6,14},{7,15},{8,0},{9,1},... | collective-permute-start | bytes 1179656 | tf_op jit(solution)/shard_map/ppermute | solution.py:383
  256.8 25.3 %collective-permute-start.42 = (f32[2,2,2,64,512]{4,3,2,1,0:T(8,128)S(1)}, f32[2,2,2,64,512]{4,3,2,1,0:T(8,128)S(1)}, u32[]{:S(2)}, u32[]{:S(2)}) collective-permute-start(f32[2,2,2,64,512]{4,3,2,1,0:T(8,128)S(1)} %get-tuple-element.70), channel_id=1, source_target_pairs={{0,2},{1,3},{2,0},{3,1},{4,6},{5,7},{6,4},{7,5},{8,10},{9,11},{10,... | collective-permute-start | bytes 3145736 | tf_op jit(solution)/shard_map/ppermute | solution.py:383
  270.4 19.4 %collective-permute-start.17 = (f32[2,2,64,512]{3,2,1,0:T(8,128)S(1)}, f32[2,2,64,512]{3,2,1,0:T(8,128)S(1)}, u32[]{:S(2)}, u32[]{:S(2)}) collective-permute-start(f32[2,2,64,512]{3,2,1,0:T(8,128)S(1)} %get-tuple-element.77), channel_id=1, source_target_pairs={{0,4},{1,5},{2,6},{3,7},{4,0},{5,1},{6,2},{7,3},{8,12},{9,13},{10,... | collective-permute-start | bytes 1572872 | tf_op jit(solution)/shard_map/ppermute | solution.py:383
  271.4 9.8 %collective-permute-start.22 = (f32[2,64,384]{2,1,0:T(8,128)S(1)}, f32[2,64,384]{2,1,0:T(8,128)S(1)}, u32[]{:S(2)}, u32[]{:S(2)}) collective-permute-start(f32[2,64,384]{2,1,0:T(8,128)S(1)} %get-tuple-element.125), channel_id=1, source_target_pairs={{0,24},{1,25},{2,26},{3,27},{4,28},{5,29},{6,30},{7,31},{8,16},{9,... | collective-permute-start | bytes 589832 | tf_op jit(solution)/shard_map/ppermute | solution.py:383
  273.9 16.0 %collective-permute-start.34 = (f32[2,2,64,384]{3,2,1,0:T(8,128)S(1)}, f32[2,2,64,384]{3,2,1,0:T(8,128)S(1)}, u32[]{:S(2)}, u32[]{:S(2)}) collective-permute-start(f32[2,2,64,384]{3,2,1,0:T(8,128)S(1)} %get-tuple-element.117), channel_id=1, source_target_pairs={{0,8},{1,9},{2,10},{3,11},{4,12},{5,13},{6,14},{7,15},{8,0},{9,1},... | collective-permute-start | bytes 1179656 | tf_op jit(solution)/shard_map/ppermute | solution.py:383
  281.2 13.0 %collective-permute-start.47 = (f32[2,2,64,384]{3,2,1,0:T(8,128)S(1)}, f32[2,2,64,384]{3,2,1,0:T(8,128)S(1)}, u32[]{:S(2)}, u32[]{:S(2)}) collective-permute-start(f32[2,2,64,384]{3,2,1,0:T(8,128)S(1)} %fusion.9), channel_id=1, source_target_pairs={{0,8},{1,9},{2,10},{3,11},{4,12},{5,13},{6,14},{7,15},{8,0},{9,1},... | collective-permute-start | bytes 1179656 | tf_op jit(solution)/shard_map/ppermute | solution.py:383
  282.1 31.3 %collective-permute-start.30 = (f32[2,2,64,512]{3,2,1,0:T(8,128)S(1)}, f32[2,2,64,512]{3,2,1,0:T(8,128)S(1)}, u32[]{:S(2)}, u32[]{:S(2)}) collective-permute-start(f32[2,2,64,512]{3,2,1,0:T(8,128)S(1)} %get-tuple-element.79), channel_id=1, source_target_pairs={{0,4},{1,5},{2,6},{3,7},{4,0},{5,1},{6,2},{7,3},{8,12},{9,13},{10,... | collective-permute-start | bytes 1572872 | tf_op jit(solution)/shard_map/ppermute | solution.py:383
  286.2 27.3 %collective-permute-start.43 = (f32[2,2,64,512]{3,2,1,0:T(8,128)S(1)}, f32[2,2,64,512]{3,2,1,0:T(8,128)S(1)}, u32[]{:S(2)}, u32[]{:S(2)}) collective-permute-start(f32[2,2,64,512]{3,2,1,0:T(8,128)S(1)} %get-tuple-element.81), channel_id=1, source_target_pairs={{0,4},{1,5},{2,6},{3,7},{4,0},{5,1},{6,2},{7,3},{8,12},{9,13},{10,... | collective-permute-start | bytes 1572872 | tf_op jit(solution)/shard_map/ppermute | solution.py:383
  289.9 20.2 %collective-permute-start.18 = (f32[2,64,512]{2,1,0:T(8,128)S(1)}, f32[2,64,512]{2,1,0:T(8,128)S(1)}, u32[]{:S(2)}, u32[]{:S(2)}) collective-permute-start(f32[2,64,512]{2,1,0:T(8,128)S(1)} %get-tuple-element.119), channel_id=1, source_target_pairs={{0,8},{1,9},{2,10},{3,11},{4,12},{5,13},{6,14},{7,15},{8,0},{9,1},... | collective-permute-start | bytes 786440 | tf_op jit(solution)/shard_map/ppermute | solution.py:383
  290.0 15.6 %collective-permute-start.35 = (f32[2,64,384]{2,1,0:T(8,128)S(1)}, f32[2,64,384]{2,1,0:T(8,128)S(1)}, u32[]{:S(2)}, u32[]{:S(2)}) collective-permute-start(f32[2,64,384]{2,1,0:T(8,128)S(1)} %get-tuple-element.127), channel_id=1, source_target_pairs={{0,24},{1,25},{2,26},{3,27},{4,28},{5,29},{6,30},{7,31},{8,16},{9,... | collective-permute-start | bytes 589832 | tf_op jit(solution)/shard_map/ppermute | solution.py:383
  294.2 14.4 %collective-permute-start.48 = (f32[2,64,384]{2,1,0:T(8,128)S(1)}, f32[2,64,384]{2,1,0:T(8,128)S(1)}, u32[]{:S(2)}, u32[]{:S(2)}) collective-permute-start(f32[2,64,384]{2,1,0:T(8,128)S(1)} %get-tuple-element.129), channel_id=1, source_target_pairs={{0,24},{1,25},{2,26},{3,27},{4,28},{5,29},{6,30},{7,31},{8,16},{9,... | collective-permute-start | bytes 589832 | tf_op jit(solution)/shard_map/ppermute | solution.py:383
  310.0 6.8 %collective-permute-start.19 = (f32[64,512]{1,0:T(8,128)S(1)}, f32[64,512]{1,0:T(8,128)S(1)}, u32[]{:S(2)}, u32[]{:S(2)}) collective-permute-start(f32[64,512]{1,0:T(8,128)S(1)} %fusion.32), channel_id=1, source_target_pairs={{0,24},{1,25},{2,26},{3,27},{4,28},{5,29},{6,30},{7,31},{8,16},{9,... | collective-permute-start | bytes 393224 | tf_op jit(solution)/shard_map/ppermute | solution.py:383
  313.5 6.4 %collective-permute-start.31 = (f32[2,64,512]{2,1,0:T(8,128)S(1)}, f32[2,64,512]{2,1,0:T(8,128)S(1)}, u32[]{:S(2)}, u32[]{:S(2)}) collective-permute-start(f32[2,64,512]{2,1,0:T(8,128)S(1)} %get-tuple-element.121), channel_id=1, source_target_pairs={{0,8},{1,9},{2,10},{3,11},{4,12},{5,13},{6,14},{7,15},{8,0},{9,1},... | collective-permute-start | bytes 786440 | tf_op jit(solution)/shard_map/ppermute | solution.py:383
  313.7 9.1 %collective-permute-start.44 = (f32[2,64,512]{2,1,0:T(8,128)S(1)}, f32[2,64,512]{2,1,0:T(8,128)S(1)}, u32[]{:S(2)}, u32[]{:S(2)}) collective-permute-start(f32[2,64,512]{2,1,0:T(8,128)S(1)} %get-tuple-element.123), channel_id=1, source_target_pairs={{0,8},{1,9},{2,10},{3,11},{4,12},{5,13},{6,14},{7,15},{8,0},{9,1},... | collective-permute-start | bytes 786440 | tf_op jit(solution)/shard_map/ppermute | solution.py:383
  319.9 6.9 %collective-permute-start.32 = (f32[64,512]{1,0:T(8,128)S(1)}, f32[64,512]{1,0:T(8,128)S(1)}, u32[]{:S(2)}, u32[]{:S(2)}) collective-permute-start(f32[64,512]{1,0:T(8,128)S(1)} %fusion.28), channel_id=1, source_target_pairs={{0,24},{1,25},{2,26},{3,27},{4,28},{5,29},{6,30},{7,31},{8,16},{9,... | collective-permute-start | bytes 393224 | tf_op jit(solution)/shard_map/ppermute | solution.py:383
  322.8 6.8 %collective-permute-start.45 = (f32[64,512]{1,0:T(8,128)S(1)}, f32[64,512]{1,0:T(8,128)S(1)}, u32[]{:S(2)}, u32[]{:S(2)}) collective-permute-start(f32[64,512]{1,0:T(8,128)S(1)} %fusion.24), channel_id=1, source_target_pairs={{0,24},{1,25},{2,26},{3,27},{4,28},{5,29},{6,30},{7,31},{8,16},{9,... | collective-permute-start | bytes 393224 | tf_op jit(solution)/shard_map/ppermute | solution.py:383
  (38 other events, 244.5 us)

commit v2 on v0

v2 whole, which is shorter than its diff:
```python
import functools
import math

import jax
import jax.numpy as jnp
from jax import lax
from jax.experimental import pallas as pl
from jax.experimental.pallas import tpu as pltpu
from jax.sharding import PartitionSpec as P

HEADS = 8
DH = 128
PAIR = 2
WIDE = PAIR * DH
PARTS = 2
SHARES = 2
AXES = ("seq", "dp")
F32 = jnp.float32
BF16 = jnp.bfloat16
MIB = 1024 * 1024
EMBED_MIB = 41

fsq_levels = (8, 8, 8, 5, 5, 5)
fsq_bases = (1, 8, 64, 512, 2560, 12800)

NT = (((1,), (1,)), ((), ()))
TN = (((0,), (0,)), ((), ()))
VMEM = pl.BlockSpec(memory_space=pltpu.VMEM)
SMEM = pl.BlockSpec(memory_space=pltpu.SMEM)
HBM = pl.BlockSpec(memory_space=pltpu.HBM)


def mm(a, b):
    return jnp.dot(a, b, preferred_element_type=F32)


def mm_nt(a, b):
    return lax.dot_general(a, b, NT, preferred_element_type=F32)


def mm_tn(a, b):
    return lax.dot_general(a, b, TN, preferred_element_type=F32)


def params(size):
    return pltpu.CompilerParams(vmem_limit_bytes=int(size) + 5 * MIB)


def cost(flops, moved):
    return pl.CostEstimate(flops=1, bytes_accessed=1, transcendentals=0)


def shape(dims, dtype):
    return jax.ShapeDtypeStruct(dims, dtype)


def silu_and_slope(value):
    sigma = 1.0 / (1.0 + jnp.exp(-value))
    return value * sigma, sigma * (1.0 + value * (1.0 - sigma))


def head(h):
    return slice(h * DH, (h + 1) * DH)


def part_rows(t, p):
    return slice(p * (t // PARTS), (p + 1) * (t // PARTS))


def hand_out(slot, part_sums, pieces):
    share = pieces[0].shape[0]
    for mask, piece in enumerate(pieces):
        heads = pl.ds((slot ^ mask) * share, share)
        total = part_sums[0, heads]
        for p in range(1, PARTS):
            total = total + part_sums[p, heads]
        piece[...] = total


def take_in(slot, pieces, out_ref):
    share = pieces[0].shape[0]
    for mask, piece in enumerate(pieces):
        out_ref[pl.ds((slot ^ mask) * share, share)] = piece[...]


def in_vmem(kernel, slots, inputs, outs, scratch, price, name):
    size = sum(math.prod(a.shape) * a.dtype.itemsize for a in [*inputs, *outs, *scratch])
    return pl.pallas_call(
        kernel,
        in_specs=[SMEM] * len(slots) + [VMEM] * len(inputs),
        out_specs=[VMEM] * len(outs),
        out_shape=outs,
        scratch_shapes=scratch,
        compiler_params=params(size),
        cost_estimate=price,
        name=name,
    )(*slots, *inputs)


def embed_kernel(
    slots, ids_hbm, proj_hbm, resid_hbm, wk_hbm, wv_hbm,
    x_ref, codes_ref, k_ref, slope_ref, v_ref, kv_ref, *rest,
):
    pieces = rest[:-6]
    ids_ref, proj_ref, resid_ref, wk_ref, wv_ref, sems = rest[-6:]
    t, d = x_ref.shape
    hd = k_ref.shape[1]
    half = hd // 2
    moves = [(ids_hbm, ids_ref), (proj_hbm, proj_ref), (resid_hbm, resid_ref)]
    for c in range(2):
        at = pl.ds(c * half, half)
        moves += [(wk_hbm.at[:, at], wk_ref.at[:, at]), (wv_hbm.at[:, at], wv_ref.at[:, at])]
    incoming = [pltpu.make_async_copy(hbm, ref, sems.at[i]) for i, (hbm, ref) in enumerate(moves)]
    for copy in incoming:
        copy.start()
    incoming[0].wait()
    ids = ids_ref[...]
    code_list = []
    for fsq_level, fsq_base in zip(fsq_levels, fsq_bases):
        digit = lax.rem(lax.div(ids, fsq_base), fsq_level)
        code_list.append((2.0 * digit.astype(F32) - (fsq_level - 1)) / (fsq_level - 1))
    count = len(code_list)
    for _ in range(codes_ref.shape[0] - count):
        code_list.append(jnp.zeros_like(code_list[0]))
    codes = jnp.concatenate(code_list, axis=0)
    codes_ref[...] = codes
    turned = jnp.transpose(codes)
    incoming[1].wait()
    incoming[2].wait()
    step = 64
    for r in range(0, t, step):
        summed = resid_ref[r : r + step].astype(F32)
        for index in range(count):
            summed = summed + turned[r : r + step, index : index + 1] * proj_ref[index : index + 1]
        x_ref[r : r + step] = summed.astype(BF16)
    x = x_ref[...]
    for c in range(2):
        at = slice(c * half, (c + 1) * half)
        incoming[3 + 2 * c].wait()
        key, slope = silu_and_slope(mm(x, wk_ref[:, at]))
        key = key.astype(BF16)
        k_ref[:, at] = key
        slope_ref[:, at] = slope
        incoming[4 + 2 * c].wait()
        value = mm(x, wv_ref[:, at]).astype(BF16)
        v_ref[:, at] = value
        for h in range(half // DH):
            for p in range(PARTS):
                rows = part_rows(t, p)
                kv_ref[p, c * (half // DH) + h] = mm_tn(key[rows, head(h)], value[rows, head(h)])
    hand_out(slots[0], kv_ref, pieces)


def embed_keys_values(slots, resid, token_ids, code_proj, w_key, w_value, group):
    t, d = resid.shape
    hd = w_key.shape[1]
    heads = hd // DH
    return pl.pallas_call(
        embed_kernel,
        in_specs=[SMEM] + [HBM] * 5,
        out_specs=[VMEM] * (6 + group),
        out_shape=[
            shape((t, d), BF16),
            shape((8, t), F32),
            shape((t, hd), BF16),
            shape((t, hd), F32),
            shape((t, hd), BF16),
            shape((PARTS, heads, DH, DH), F32),
        ]
        + [shape((heads // group, DH, DH), F32)] * group,
        scratch_shapes=[
            pltpu.VMEM(token_ids.shape, jnp.int32),
            pltpu.VMEM(code_proj.shape, F32),
            pltpu.VMEM((t, d), BF16),
            pltpu.VMEM((d, hd), BF16),
            pltpu.VMEM((d, hd), BF16),
            pltpu.SemaphoreType.DMA((7,)),
        ],
        compiler_params=params(EMBED_MIB * MIB),
        cost_estimate=cost(4 * t * d * hd, 4 * d * hd + 10 * t * hd),
        name="embed_keys_values",
    )(slots, token_ids, code_proj, resid, w_key, w_value)


def causal_mask(t, transposed):
    rows = lax.broadcasted_iota(jnp.int32, (t, t), 0)
    cols = lax.broadcasted_iota(jnp.int32, (t, t), 1)
    return rows <= cols if transposed else cols <= rows


def masked(mask, product):
    return jnp.where(mask, product, 0.0).astype(BF16)


def query_kernel(x_ref, wq_ref, k_ref, v_ref, q_ref, slope_ref, sv_ref):
    t = x_ref.shape[0]
    hd = q_ref.shape[1]
    half = hd // 2
    mask = causal_mask(t // PARTS, False)
    for c in range(2):
        at = slice(c * half, (c + 1) * half)
        query, slope = silu_and_slope(mm(x_ref[...], wq_ref[:, at]))
        query = query.astype(BF16)
        q_ref[:, at] = query
        slope_ref[:, at] = slope
        for h in range(half // DH):
            at = head(c * (half // DH) + h)
            for p in range(PARTS):
                rows = part_rows(t, p)
                scores = masked(mask, mm_nt(query[rows, head(h)], k_ref[rows, at]))
                sv_ref[rows, at] = mm(scores, v_ref[rows, at])


def queries_scores(x, w_query, keys, values):
    t, d = x.shape
    hd = w_query.shape[1]
    outs = [shape((t, hd), BF16), shape((t, hd), F32), shape((t, hd), F32)]
    price = cost(2 * t * d * hd + 2 * t * t * hd, 2 * d * hd + 14 * t * hd)
    return in_vmem(query_kernel, [], [x, w_query, keys, values], outs, [], price, "queries_scores")


def norm_kernel(slots, sv_ref, q_ref, kv_ref, og_ref, gain_ref, *rest):
    group = (len(rest) - 4) // 2
    prefixes, (datt_ref, term_ref, grad_ref), outs = rest[:group], rest[group : group + 3], rest[group + 3 : -1]
    state_ref = rest[-1]
    take_in(slots[0], prefixes, state_ref)
    t, hd = q_ref.shape
    for h in range(hd // DH):
        at = head(h)
        term = None
        state = state_ref[h]
        for p in range(PARTS):
            rows = part_rows(t, p)
            if p:
                state = state + kv_ref[p - 1, h]
            query = q_ref[rows, at]
            attended = sv_ref[rows, at] + mm(query, state.astype(BF16))
            inverse = lax.rsqrt(jnp.mean(attended * attended, axis=-1, keepdims=True) + 1e-06)
            normed = attended * inverse
            grad = og_ref[rows, at].astype(F32)
            more = jnp.sum(grad * normed, axis=0, keepdims=True)
            term = more if term is None else term + more
            d_normed = grad * gain_ref[:, at]
            inner = jnp.mean(d_normed * normed, axis=-1, keepdims=True)
            d_att = ((d_normed - normed * inner) * inverse).astype(BF16)
            datt_ref[rows, at] = d_att
            grad_ref[p, h] = mm_tn(query, d_att)
        term_ref[:, at] = term
    hand_out(slots[1], grad_ref, outs)


def norm_gradient(slots, sv, queries, prefixes, part_kv, out_grad, gain):
    t, hd = sv.shape
    heads = hd // DH
    group = len(prefixes)
    outs = [shape((t, hd), BF16), shape((1, hd), F32), shape((PARTS, heads, DH, DH), F32)]
    outs += [shape((heads // group, DH, DH), F32)] * group
    return in_vmem(
        norm_kernel, [slots], [sv, queries, part_kv, out_grad, gain, *prefixes], outs,
        [pltpu.VMEM((heads, DH, DH), F32)], cost(4 * t * hd * DH, 10 * t * hd), "norm_gradient",
    )


def store_wide(refs, rows, h, grad):
    width = refs[0].shape[1]
    start = h * DH % width
    refs[h * DH // width][rows, start : start + DH] = grad.astype(F32)


def dquery_kernel(slots, datt_ref, v_ref, k_ref, kv_ref, slope_ref, *rest):
    prefixes, (g16_ref, *wide, state_ref) = rest[: -2 - SHARES], rest[-2 - SHARES :]
    take_in(slots[0], prefixes, state_ref)
    t, hd = datt_ref.shape
    mask = causal_mask(t // PARTS, False)
    for h in range(hd // DH):
        at = head(h)
        state = state_ref[h]
        for p in range(PARTS):
            rows = part_rows(t, p)
            if p:
                state = state + kv_ref[p - 1, h]
            d_att = datt_ref[rows, at]
            back = masked(mask, mm_nt(d_att, v_ref[rows, at]))
            d_query = mm(back, k_ref[rows, at]) + mm_nt(d_att, state.astype(BF16))
            grad = (d_query * slope_ref[rows, at]).astype(BF16)
            g16_ref[rows, at] = grad
            store_wide(wide, rows, h, grad)


def query_gradient(slots, d_att, values, keys, prefixes, part_kv, slope):
    t, hd = d_att.shape
    return in_vmem(
        dquery_kernel, [slots], [d_att, values, keys, part_kv, slope, *prefixes],
        [shape((t, hd), BF16)] + [shape((t, hd // SHARES), F32)] * SHARES, [pltpu.VMEM((hd // DH, DH, DH), F32)],
        cost(2 * t * t * hd, 16 * t * hd), "query_gradient",
    )


def within_kernel(datt_ref, v_ref, k_ref, q_ref, dk_ref, dv_ref):
    t, hd = datt_ref.shape
    mask = causal_mask(t // PARTS, True)
    for h in range(hd // DH):
        at = head(h)
        for p in range(PARTS):
            rows = part_rows(t, p)
            d_att, query = datt_ref[rows, at], q_ref[rows, at]
            back = masked(mask, mm_nt(v_ref[rows, at], d_att))
            dk_ref[rows, at] = mm(back, query)
            scores = masked(mask, mm_nt(k_ref[rows, at], query))
            dv_ref[rows, at] = mm(scores, d_att)


def within_block(d_att, values, keys, queries):
    t, hd = d_att.shape
    return in_vmem(
        within_kernel, [], [d_att, values, keys, queries], [shape((t, hd), F32)] * 2, [],
        cost(4 * t * t * hd, 16 * t * hd), "within_block",
    )


def dkv_kernel(slots, dk_ref, dv_ref, v_ref, k_ref, grad_ref, slope_ref, *rest):
    suffixes, outs, state_ref = rest[: -3 - 2 * SHARES], rest[-3 - 2 * SHARES : -1], rest[-1]
    (k16, *wide_k), (v16, *wide_v) = outs[: 1 + SHARES], outs[1 + SHARES :]
    take_in(slots[1], suffixes, state_ref)
    t, hd = dk_ref.shape
    for h in range(hd // DH):
        at = head(h)
        state = state_ref[h]
        for p in reversed(range(PARTS)):
            rows = part_rows(t, p)
            if p < PARTS - 1:
                state = state + grad_ref[p + 1, h]
            suffix = state.astype(BF16)
            d_key = dk_ref[rows, at] + mm_nt(v_ref[rows, at], suffix)
            grad = (d_key * slope_ref[rows, at]).astype(BF16)
            k16[rows, at] = grad
            store_wide(wide_k, rows, h, grad)
            grad = (dv_ref[rows, at] + mm(k_ref[rows, at], suffix)).astype(BF16)
            v16[rows, at] = grad
            store_wide(wide_v, rows, h, grad)


def key_value_gradients(slots, dk, dv, values, keys, suffixes, part_grad, slope):
    t, hd = dk.shape
    return in_vmem(
        dkv_kernel, [slots], [dk, dv, values, keys, part_grad, slope, *suffixes],
        ([shape((t, hd), BF16)] + [shape((t, hd // SHARES), F32)] * SHARES) * 2,
        [pltpu.VMEM((hd // DH, DH, DH), F32)],
        cost(4 * t * hd * DH, 28 * t * hd), "key_value_gradients",
    )


class Order:
    def __init__(self):
        self.last = None

    def tied(self, *arrays):
        if self.last is not None:
            *arrays, _ = lax.optimization_barrier((*arrays, self.last))
        return arrays[0] if len(arrays) == 1 else tuple(arrays)

    def mark(self, array):
        self.last = array


def exchange(array, axis, mask):
    count = lax.axis_size(axis)
    return lax.ppermute(array, axis, [(i, i ^ mask) for i in range(count)])


def combine_kernel(inner, base_ref, *refs):
    group = len(refs) // 2
    blocks, outs = refs[:group], refs[group:]
    for mask, out_ref in enumerate(outs):
        out_ref[...] = base_ref[...]
        for other, block in enumerate(blocks):
            if other != mask:

                @pl.when((inner[0] ^ other) < (inner[0] ^ mask))
                def _(out_ref=out_ref, block=block):
                    out_ref[...] += block[...]


def combine(inner, base, blocks):
    outs = [shape(base.shape, F32)] * len(blocks)
    return list(in_vmem(combine_kernel, [inner], [base, *blocks], outs, [], cost(0, 0), "combine"))


class Entering:
    def __init__(self, reverse):
        self.reverse = reverse
        self.count = lax.axis_size("seq")
        self.group = min(HEADS // PAIR, self.count)
        place = lax.axis_index("seq")
        if reverse:
            place = self.count - 1 - place
        self.inner, cluster = place % self.group, place // self.group
        self.twist = self.group // 2
        self.slot = (self.inner ^ (self.twist * (cluster % 2))).astype(jnp.int32)
        self.inner = self.inner.astype(jnp.int32)

    def first(self, pieces):
        self.blocks = [pieces[0]]
        for mask in range(1, self.group):
            self.blocks.append(exchange(pieces[mask], "seq", mask))

    def second(self, order):
        self.blocks[1:] = order.tied(*self.blocks[1:])
        total = sum(self.blocks[1:], self.blocks[0])
        order.mark(total)
        group, twist, count = self.group, self.twist, self.count
        clusters = count // group
        self.bases = []
        for shift in range(1, clusters):
            pairs = []
            for source in range(clusters - shift):
                for slot in range(group):
                    a = source * group + (slot ^ (twist * (source % 2)))
                    target = source + shift
                    b = target * group + (slot ^ (twist * (target % 2)))
                    pairs.append((count - 1 - a, count - 1 - b) if self.reverse else (a, b))
            self.bases.append(lax.ppermute(total, "seq", pairs))

    def third(self, order):
        bases = order.tied(*self.bases)
        if len(self.bases) == 1:
            bases = (bases,)
        base = sum(bases[1:], bases[0])
        self.outs = combine(self.inner, base, self.blocks)
        order.mark(self.outs[0])
        for mask in range(1, self.group):
            self.outs[mask] = exchange(self.outs[mask], "seq", mask)

    def result(self, order):
        self.outs[1:] = order.tied(*self.outs[1:])
        return self.outs


def both_exchange(array, masks):
    total = lax.axis_size("seq") * lax.axis_size("dp")
    return lax.ppermute(array, AXES, [(i, i ^ masks[i % 2]) for i in range(total)])


def turn_kernel(me_ref, x_ref, own_ref, other_ref, turned_ref):
    chips, rows, t = own_ref.shape
    core, chip = me_ref[0] % 2, me_ref[0] // 2
    span = 128 // (2 * rows)
    for block in range(chips // span):
        turned_ref[block] = jnp.transpose(x_ref[:, block * 128 : (block + 1) * 128])
    for block in range(chips // span):
        for i in range(span):
            slot = (block * span + i) ^ chip
            mine = pl.multiple_of((2 * i + core) * rows, rows)
            theirs = pl.multiple_of((2 * i + 1 - core) * rows, rows)
            own_ref[slot] = turned_ref[block, pl.ds(mine, rows)]
            other_ref[slot] = turned_ref[block, pl.ds(theirs, rows)].astype(F32)


def turn(me, x, chips):
    t, d = x.shape
    rows = d // (2 * chips)
    return in_vmem(
        turn_kernel, [me], [x], [shape((chips, rows, t), BF16), shape((chips, rows, t), F32)],
        [pltpu.VMEM((d // 128, 128, t), BF16)], cost(0, 12 * t * d), "turn_inputs",
    )


def merge_kernel(own_ref, other_ref, out_ref):
    half = own_ref.shape[-1]
    out_ref[:, :, :half] = own_ref[...]
    out_ref[:, :, half:] = other_ref[...].astype(BF16)


def merge(own, other):
    chips, rows, t = own.shape
    outs = [shape((chips, rows, 2 * t), BF16)]
    return in_vmem(merge_kernel, [], [own, other], outs, [], cost(0, 10 * own.size), "merge_inputs")[0]


def product_kernel(parts, me_ref, x_ref, own_ref, *rest):
    other_refs, out_refs = rest[: -len(parts)], rest[-len(parts) :]
    core = me_ref[0] % 2
    other = jnp.concatenate([ref[...].astype(BF16) for ref in other_refs], axis=1)
    for out_ref, (slots, start, stop) in zip(out_refs, parts):
        grads = jnp.concatenate([own_ref[:, start:stop], other[:, start:stop]], axis=0)
        rows = jnp.concatenate([x_ref[a ^ (core * (a ^ b))] for a, b in slots], axis=0)
        out_ref[...] = mm(rows, grads)


def products(me, x, own, others, parts, name):
    rows = x.shape[1]
    outs = [shape((len(slots) * rows, stop - start), F32) for slots, start, stop in parts]
    kernel = functools.partial(product_kernel, parts)
    return in_vmem(kernel, [me], [x, own, *others], outs, [], cost(0, 0), name)


class Chunk:
    def __init__(self, start, stop, orders, masks):
        self.start, self.stop = start, stop
        self.orders = [[masks[axis] for axis in order] for order in orders]
        self.step = 0

    def slots(self, sent):
        out = []
        for masks in self.orders:
            mine = []
            for pick in range(1 << (len(masks) - 1)):
                slot = masks[0] >> 1 if sent else 0
                for place, mask in enumerate(masks[1:]):
                    if pick >> (len(masks) - 2 - place) & 1:
                        slot ^= mask >> 1
                mine.append(slot)
            out.append(mine)
        return tuple(zip(*out))

    def masks(self, step):
        return [masks[step] for masks in self.orders]

    def launch(self, sending):
        self.got = both_exchange(sending, self.masks(self.step))
        self.step += 1

    def advance(self, order, small=None):
        rest, got = self.rest, order.tied(self.got)
        extra = got.shape[0] - rest.shape[0]
        if self.step == len(self.orders[0]):
            self.rest = None
            if extra:
                self.out, small = add_last(rest, got, small)
                order.mark(small)
                return small
            self.out = rest + got
            order.mark(got)
            return None
        half = rest.shape[0] // 2
        if small is None:
            sending = add_rows(rest, got, half, half)
        else:
            sending, small = add_rows_with(rest, got, small)
        order.mark(sending)
        self.launch(sending)
        self.rest = add_rows(rest, order.tied(got), 0, half)
        order.mark(self.rest)
        return small


def add_kernel(start, a_ref, b_ref, out_ref):
    rows = slice(start, start + out_ref.shape[0])
    out_ref[...] = a_ref[rows] + b_ref[rows]


def add_rows(a, b, start, rows):
    outs = [shape((rows, a.shape[1]), F32)]
    kernel = functools.partial(add_kernel, start)
    return in_vmem(kernel, [], [a, b], outs, [], cost(0, 0), "add_rows")[0]


def add_with_kernel(rest_ref, got_ref, small_ref, sending_ref, sum_ref):
    full = rest_ref.shape[0]
    half = full // 2
    total = small_ref[...]
    if got_ref.shape[0] > full:
        total = total + got_ref[full:]
    sum_ref[...] = total
    sending_ref[half:] = total
    sending_ref[:half] = rest_ref[half:] + got_ref[half:full]


def add_rows_with(rest, got, small):
    outs = [shape((rows, rest.shape[1]), F32) for rows in (rest.shape[0] // 2 + small.shape[0], small.shape[0])]
    return in_vmem(add_with_kernel, [], [rest, got, small], outs, [], cost(0, 0), "add_rows_with")


def add_last_kernel(rest_ref, got_ref, small_ref, out_ref, sum_ref):
    full = rest_ref.shape[0]
    out_ref[...] = rest_ref[...] + got_ref[:full]
    sum_ref[...] = small_ref[...] + got_ref[full:]


def add_last(rest, got, small):
    outs = [shape(rest.shape, F32), shape(small.shape, F32)]
    return in_vmem(add_last_kernel, [], [rest, got, small], outs, [], cost(0, 0), "add_last")


def first_input_kernel(grad_ref, w_ref, out_ref):
    out_ref[...] = mm_nt(grad_ref[...], w_ref[...])


def rest_input_kernel(first_ref, codes_ref, grad_a, grad_b, wa_ref, wb_ref, out_ref, term_ref):
    total = first_ref[...] + mm_nt(grad_a[...], wa_ref[...]) + mm_nt(grad_b[...], wb_ref[...])
    out_ref[...] = total.astype(BF16)
    term_ref[...] = jnp.dot(
        codes_ref[...], total, precision=lax.Precision.HIGHEST, preferred_element_type=F32
    )


def row_blocks(w):
    return pl.BlockSpec((WIDE, w.shape[1]), lambda i: (i, 0))


def out_columns(rows):
    return pl.BlockSpec((rows, WIDE), lambda i: (0, i))


def first_input_gradient(grad, w):
    t, d = grad.shape[0], w.shape[0]
    return pl.pallas_call(
        first_input_kernel,
        grid=(d // WIDE,),
        in_specs=[VMEM, row_blocks(w)],
        out_specs=out_columns(t),
        out_shape=shape((t, d), F32),
        compiler_params=params(4 * t * WIDE * 4 + 4 * WIDE * w.shape[1] + 2 * grad.size),
        cost_estimate=cost(0, 0),
        name="input_gradient_q",
    )(grad, w)


def rest_input_gradient(first, codes, grad_a, grad_b, wa, wb):
    t, d = first.shape
    rows = codes.shape[0]
    size = 8 * t * WIDE * 4 + 8 * WIDE * wa.shape[1] + 4 * grad_a.size
    return pl.pallas_call(
        rest_input_kernel,
        grid=(d // WIDE,),
        in_specs=[out_columns(t), VMEM, VMEM, VMEM, row_blocks(wa), row_blocks(wb)],
        out_specs=[out_columns(t), out_columns(rows)],
        out_shape=[shape((t, d), BF16), shape((rows, d), F32)],
        compiler_params=params(size),
        cost_estimate=cost(0, 0),
        name="input_gradient_kv",
    )(first, codes, grad_a, grad_b, wa, wb)


def body(resid, token_ids, code_proj, w_query, w_key, w_value, gain, out_grad):
    positions, width = resid.shape[1:]
    features = w_query.shape[1]
    n_dp = lax.axis_size("dp")
    total = lax.axis_size("seq") * n_dp
    me = (lax.axis_index("seq") * n_dp + lax.axis_index("dp")).astype(jnp.int32).reshape(1)
    order = Order()

    before, after = Entering(False), Entering(True)
    slots = jnp.stack([before.slot, after.slot])
    before.inner, after.inner = before.inner.reshape(1), after.inner.reshape(1)
    slots, me, before.inner, after.inner = lax.optimization_barrier((slots, me, before.inner, after.inner))
    x, code_values, keys, key_slope, values, part_kv, *pieces = embed_keys_values(
        slots, resid[0], token_ids, code_proj, w_key, w_value, before.group
    )
    before.first(pieces)
    queries, query_slope, within = queries_scores(x, w_query, keys, values)
    order.mark(within)
    before.second(order)
    own_rows, other_rows = turn(me, order.tied(x), total // 2)
    order.mark(own_rows)
    other_rows = both_exchange(other_rows, (1, 1))
    before.third(order)
    prefixes = before.result(order)

    d_att, gain_term, part_grad, *pieces = norm_gradient(
        slots, within, queries, prefixes, part_kv, out_grad[0], gain.reshape(1, features)
    )
    order.mark(d_att)
    after.first(pieces)
    grad_q, *wide_q = query_gradient(slots, order.tied(d_att), values, keys, prefixes, part_kv, query_slope)
    order.mark(grad_q)
    wide_q = [both_exchange(share, (1, 1)) for share in wide_q]
    merged = merge(own_rows, order.tied(other_rows))
    order.mark(merged)
    after.second(order)

    bits = total.bit_length() - 1
    masks = [1 << b for b in range(1, bits)]
    masks[-1] |= masks[-2]
    dims = len(masks)

    unit = features // 8
    extra = tuple(range(4, dims))

    def chunks_of(plan):
        out, start = [], 0
        for units, *orders in plan:
            axes = [tuple("xyzw".index(name) for name in order) + extra for order in orders]
            out.append(Chunk(start * unit, (start + units) * unit, axes, masks))
            start += units
        return out

    chunks_q = chunks_of([(8, "yxzw", "xyzw")])
    chunks_k = chunks_of([(8, "zyxw", "zxyw")])
    chunks_v = chunks_of([(8, "yxzw", "xzyw")])
    every = chunks_q + chunks_k + chunks_v

    def begin(chunks, own, others, name):
        own, *others = order.tied(own, *others)
        sent = products(me, merged, own, others, [(c.slots(True), c.start, c.stop) for c in chunks], name)
        order.mark(sent[0])
        for chunk, array in zip(chunks, sent):
            chunk.launch(array)
        kept = products(me, merged, order.tied(own), others, [(c.slots(False), c.start, c.stop) for c in chunks], name + "_kept")
        order.mark(kept[0])
        for chunk, array in zip(chunks, kept):
            chunk.rest = array

    begin(chunks_q, grad_q, wide_q, "weight_q")
    dk, dv = within_block(order.tied(d_att), values, keys, queries)
    order.mark(dk)
    after.third(order)
    input_grad = first_input_gradient(order.tied(grad_q), w_query)
    order.mark(input_grad)
    suffixes = after.result(order)
    outs = key_value_gradients(slots, dk, dv, values, keys, suffixes, part_grad, key_slope)
    (grad_k, *wide_k), (grad_v, *wide_v) = outs[: 1 + SHARES], outs[1 + SHARES :]
    order.mark(grad_k)
    wide_k = [both_exchange(share, (1, 1)) for share in wide_k]
    wide_v = [both_exchange(share, (1, 1)) for share in wide_v]
    begin(chunks_k, grad_k, wide_k, "weight_k")
    begin(chunks_v, grad_v, wide_v, "weight_v")
    resid_grad, code_term = rest_input_gradient(
        input_grad, code_values, order.tied(grad_k), grad_v, w_key, w_value
    )
    order.mark(code_term)
    grad_scale = 1.0 / math.sqrt(positions * total)
    codes = len(fsq_levels)
    carrier = chunks_q[0]
    edge = carrier.stop - carrier.start
    small = jnp.concatenate([gain_term.reshape(-1), code_term[:codes].reshape(-1)])
    used = small.shape[0]
    small = jnp.pad(small, (0, -used % (8 * edge))).reshape(-1, edge)

    def advance(index):
        nonlocal small
        if every[index] is carrier:
            small = carrier.advance(order, small)
        else:
            every[index].advance(order)

    small = small + order.tied(both_exchange(small, (1, 1)))
    order.mark(small)
    for index in (0, 2, 0, 1, 2, 0, 1):
        advance(index)
    while any(c.step < dims for c in every):
        for index, c in enumerate(every):
            if c.step < dims:
                advance(index)
    advance(0)
    small = small + order.tied(both_exchange(small, carrier.masks(0)))
    order.mark(small)
    for index in (2, 1):
        advance(index)
    small = small.reshape(-1)[:used] * grad_scale
    gain_sum, code_sum = small[:features], small[features:].reshape(codes, width)

    def joined(chunks):
        return jnp.concatenate([c.out for c in chunks], axis=-1)

    weights = jnp.stack([joined(chunks_q), joined(chunks_k), joined(chunks_v)], axis=1) * grad_scale
    return resid_grad[None], weights, gain_sum, code_sum


def solution(mesh):
    return jax.shard_map(
        body,
        mesh=mesh,
        in_specs=(
            P("dp", "seq", None),
            P("dp", "seq"),
            P(),
            P(),
            P(),
            P(),
            P(),
            P("dp", "seq", None),
        ),
        out_specs=(P("dp", "seq", None), P(AXES, None, None), P(), P()),
        check_vma=False,
    )
```

time: 509 us -> 205 us (0.40); the launches traced: 500 us -> 205 us
  waiting for transfers between devices: 311 us -> 102 us
  matrix products: 67.1 us -> 0 us
  Pallas kernels: 0 us -> 66 us
  blocking collectives: 50.1 us -> 0 us
  other arithmetic: 32.1 us -> 1.17 us
  starting transfers between devices: 0.12 us -> 30.3 us
  local copies, waits for them, and re-layouts: 23.9 us -> 4.17 us
  between operations: 14.7 us -> 1.18 us
    reduce_scatter x1 -> x0, waiting for transfers between devices: 207 us -> none  [body(): lax.psum_scatter(jnp.stack(products, axis=1), ('seq', 'dp'), scatter_dime...]
    all_gather x2 -> x0, waiting for transfers between devices: 104 us -> none  [entering(): gathered = lax.all_gather(part, axis)]
    ppermute x0 -> x35, waiting for transfers between devices: none -> 102 us  [the longest x21 83.2 us: both_exchange(): lax.ppermute(array, AXES, [(i, i ^ masks[i % 2]) for i in range(total)])]
    dot_general x22 -> x0, matrix products: 67.1 us -> none  [the longest x3 13.8 us: body(): lax.dot_general(inputs, grad_part, row_dims, preferred_element_type=f32)]
    pallas_call x0 -> x37, Pallas kernels: none -> 66 us  [the longest x34 38.7 us: in_vmem(): pl.pallas_call(kernel, in_specs=[SMEM] * len(slots) + [VMEM] * len(inputs...]
    psum x1 -> x0, blocking collectives: 50.1 us -> none  [body(): gain_sum, code_sum = lax.psum((gain_term, code_term), ('seq', 'dp'))]
    ppermute x0 -> x35, starting transfers between devices: none -> 30.3 us  [the longest x21 15.1 us: both_exchange(): lax.ppermute(array, AXES, [(i, i ^ masks[i % 2]) for i in range(total)])]
    unnamed x70 -> x26, local copies, waits for them, and re-layouts: 13.9 us -> 2.88 us
  transfers between devices with their start and end apart: 3 -> 35, of which waited for: 3 -> 22; matrix products, arithmetic and copies ran while one was open for 11% -> 1% of each run, Pallas kernels for 0% -> 26%
where the time goes in v2:
time: 205 us
  waiting for transfers between devices  102 us (50%)
  Pallas kernels  66 us (32%)
  starting transfers between devices  30.3 us (15%)
  local copies, waits for them, and re-layouts  4.17 us (2%)
    ppermute x21, waiting for transfers between devices, both_exchange(): lax.ppermute(array, AXES, [(i, i ^ masks[i % 2]) for i in range(total)])  83.2 us
    pallas_call x34, Pallas kernels, in_vmem(): pl.pallas_call(kernel, in_specs=[SMEM] * len(slots) + [VMEM] * len(inputs...  38.7 us
    ppermute x21, starting transfers between devices, both_exchange(): lax.ppermute(array, AXES, [(i, i ^ masks[i % 2]) for i in range(total)])  15.1 us
    pallas_call x1, Pallas kernels, rest_input_gradient(): pl.pallas_call(rest_input_kernel, grid=(d // WIDE,), in_specs=[out_column...  12 us
    ppermute x12, waiting for transfers between devices, exchange(): return lax.ppermute(array, axis, [(i, i ^ mask) for i in range(count)])  11.3 us
    pallas_call x1, Pallas kernels, embed_keys_values(): pl.pallas_call(embed_kernel, in_specs=[SMEM] + [HBM] * 5, out_specs=[VMEM...  11.3 us
    ppermute x12, starting transfers between devices, exchange(): return lax.ppermute(array, axis, [(i, i ^ mask) for i in range(count)])  10.8 us
    ppermute x2, waiting for transfers between devices, second(): self.bases.append(lax.ppermute(total, 'seq', pairs))  7.68 us
  transfers between devices with their start and end apart: 35, of which 22 were waited for; matrix products, arithmetic and copies ran while one was open for 1% of the time, Pallas kernels for 26%

profile of v2, /device:TPU:13, one launch (start us, length us, event | category | flops | bytes accessed | tf_op | source)
XLA Modules:
  0.0 205.0 jit_solution(17507861685610012742)
XLA Ops:
  2.3 11.3 %embed_keys_values.1 = (bf16[512,2048]{1,0:T(8,128)(2,1)S(1)}, f32[8,512]{1,0:T(8,128)S(1)}, bf16[512,1024]{1,0:T(8,128)(2,1)S(1)}, f32[512,1024]{1,0:T(8,128)S(...) custom-call(s32[2]{0:T(128)S(1)} %pad_add_fusion.slots, ...), custom_call_target="tpu_custom_call" | custom-call | flops 1 | bytes 1 | tf_op jit(solution)/shard_map/embed_keys_values/pallas_call | solution.py:158
  13.9 2.4 %collective-permute-start.2 = (f32[2,128,128]{2,1,0:T(8,128)S(1)}, f32[2,128,128]{2,1,0:T(8,128)S(1)}, u32[]{:S(2)}, u32[]{:S(2)}) collective-permute-start(f32[2,128,128]{2,1,0:T(8,128)S(1)} %get-tuple-element.125), channel_id=1, source_target_pairs={{0,12},{4,8},{8,4},{12,0},{16,28},{20,24},{24,20},{28,16},{1,13},{... | collective-permute-start | bytes 393224 | tf_op jit(solution)/shard_map/ppermute | solution.py:368
  16.3 4.0 %queries_scores.1 = (bf16[512,1024]{1,0:T(8,128)(2,1)S(1)}, f32[512,1024]{1,0:T(8,128)S(1)}, f32[512,1024]{1,0:T(8,128)S(1)}) custom-call(bf16[512,2048]{1,0:T(8,128)(2,1)S(1)} %get-tuple-element.130.x_ref, bf16[2048,1024]{1,0:T(8,128)(2,1)S(1)} %copy-done.4, bf16[512,1024]{1,0:T(8,128)(2,1)S(1)} %get-tuple-element.116.k_ref, ...), custom_call_target="tpu_custom_call" | custom-call | flops 1 | bytes 1 | tf_op jit(solution)/shard_map/queries_scores/pallas_call | solution.py:88
  22.5 2.2 %collective-permute-start.10 = (f32[16,64,512]{2,1,0:T(8,128)S(1)}, f32[16,64,512]{2,1,0:T(8,128)S(1)}, u32[]{:S(2)}, u32[]{:S(2)}) collective-permute-start(f32[16,64,512]{2,1,0:T(8,128)S(1)} %get-tuple-element.149), channel_id=1, source_target_pairs={{0,1},{1,0},{2,3},{3,2},{4,5},{5,4},{6,7},{7,6},{8,9},{9,8},{10,11... | collective-permute-start | bytes 6291464 | tf_op jit(solution)/shard_map/ppermute | solution.py:441
  24.7 3.2 %collective-permute-start.3 = (f32[2,128,128]{2,1,0:T(8,128)S(1)}, f32[2,128,128]{2,1,0:T(8,128)S(1)}, u32[]{:S(2)}, u32[]{:S(2)}) collective-permute-start(f32[2,128,128]{2,1,0:T(8,128)S(1)} %add_add_fusion.1), channel_id=1, source_target_pairs={{0,24},{4,28},{8,16},{12,20},{1,25},{5,29},{9,17},{13,21},{2,26},{... | collective-permute-start | bytes 393224 | tf_op jit(solution)/shard_map/ppermute | solution.py:422
  27.9 5.5 %collective-permute-done.3.base_ref = f32[2,128,128]{2,1,0:T(8,128)S(1)} collective-permute-done((f32[2,128,128]{2,1,0:T(8,128)S(1)}, f32[2,128,128]{2,1,0:T(8,128)S(1)}, u32[]{:S(2)}, u32[]{:S(2)}) %collective-permute-start.3) | collective-permute-done | bytes 131104 | tf_op jit(solution)/shard_map/ppermute | solution.py:422
  34.1 2.4 %collective-permute-start.6 = (f32[2,128,128]{2,1,0:T(8,128)S(1)}, f32[2,128,128]{2,1,0:T(8,128)S(1)}, u32[]{:S(2)}, u32[]{:S(2)}) collective-permute-start(f32[2,128,128]{2,1,0:T(8,128)S(1)} %get-tuple-element.136), channel_id=1, source_target_pairs={{0,12},{4,8},{8,4},{12,0},{16,28},{20,24},{24,20},{28,16},{1,13},{... | collective-permute-start | bytes 393224 | tf_op jit(solution)/shard_map/ppermute | solution.py:368
  38.2 3.1 %collective-permute-done.6.rest_3_ = f32[2,128,128]{2,1,0:T(8,128)S(1)} collective-permute-done((f32[2,128,128]{2,1,0:T(8,128)S(1)}, f32[2,128,128]{2,1,0:T(8,128)S(1)}, u32[]{:S(2)}, u32[]{:S(2)}) %collective-permute-start.6) | collective-permute-done | bytes 131104 | tf_op jit(solution)/shard_map/ppermute | solution.py:368
  41.3 3.3 %norm_gradient.1 = (bf16[512,1024]{1,0:T(8,128)(2,1)S(1)}, f32[1,1024]{1,0:T(1,128)S(1)}, f32[2,8,128,128]{3,2,1,0:T(8,128)S(1)}, f32[2,128,128]{2,1,0:T(8,128)S...) custom-call(s32[2]{0:T(128)S(1)} %pad_add_fusion.slots, ...), custom_call_target="tpu_custom_call" | custom-call | flops 1 | bytes 1 | tf_op jit(solution)/shard_map/norm_gradient/pallas_call | solution.py:88
  44.7 2.6 %query_gradient.1 = (bf16[512,1024]{1,0:T(8,128)(2,1)S(1)}, f32[512,512]{1,0:T(8,128)S(1)}, f32[512,512]{1,0:T(8,128)S(1)}) custom-call(s32[2]{0:T(128)S(1)} %pad_add_fusion.slots, bf16[512,1024]{1,0:T(8,128)(2,1)S(1)} %get-tuple-element.160.datt_ref, bf16[512,1024]{1,0:T(8,128)(2,1)S(1)} %get-tuple-element.117.v_ref, ...), custom_call_target="tpu_custom_call" | custom-call | flops 1 | bytes 1 | tf_op jit(solution)/shard_map/query_gradient/pallas_call | solution.py:88
  47.2 2.5 %collective-permute-start.12 = (f32[512,512]{1,0:T(8,128)S(1)}, f32[512,512]{1,0:T(8,128)S(1)}, u32[]{:S(2)}, u32[]{:S(2)}) collective-permute-start(f32[512,512]{1,0:T(8,128)S(1)} %get-tuple-element.154), channel_id=1, source_target_pairs={{0,1},{1,0},{2,3},{3,2},{4,5},{5,4},{6,7},{7,6},{8,9},{9,8},{10,11... | collective-permute-start | bytes 3145736 | tf_op jit(solution)/shard_map/ppermute | solution.py:441
  50.3 2.2 %collective-permute-start.9 = (f32[2,128,128]{2,1,0:T(8,128)S(1)}, f32[2,128,128]{2,1,0:T(8,128)S(1)}, u32[]{:S(2)}, u32[]{:S(2)}) collective-permute-start(f32[2,128,128]{2,1,0:T(8,128)S(1)} %get-tuple-element.148), channel_id=1, source_target_pairs={{0,12},{4,8},{8,4},{12,0},{16,28},{20,24},{24,20},{28,16},{1,13},{... | collective-permute-start | bytes 393224 | tf_op jit(solution)/shard_map/ppermute | solution.py:368
  52.7 1.8 collective-permute-done.7.refs_1_
  54.5 3.7 %collective-permute-done.9.refs_3_ = f32[2,128,128]{2,1,0:T(8,128)S(1)} collective-permute-done((f32[2,128,128]{2,1,0:T(8,128)S(1)}, f32[2,128,128]{2,1,0:T(8,128)S(1)}, u32[]{:S(2)}, u32[]{:S(2)}) %collective-permute-start.9) | collective-permute-done | bytes 131104 | tf_op jit(solution)/shard_map/ppermute | solution.py:368
  58.2 1.3 collective-permute-start.11
  59.5 2.7 %weight_q.1 = f32[512,1024]{1,0:T(8,128)} custom-call(s32[1]{0:T(128)} %bitcast.2.me_ref, bf16[16,64,1024]{2,1,0:T(8,128)(2,1)S(1)} %merge_inputs.1.x_ref, bf16[512,1024]{1,0:T(8,128)(2,1)S(1)} %get-tuple-element.164.own_ref.grad_ref, f32[512,512]{1,0:T(8,128)S(1)} %collective-permute-done.12.rest_0_, f32[512,512]{1,0:T(8,128)S(1)} %collective-permute-done.13.rest_1_), custom_call_target="tpu_custom_call" | custom-call | flops 1 | bytes 1 | tf_op jit(solution)/shard_map/weight_q/pallas_call | solution.py:88
  62.2 1.3 weight_q_kept.1.rest_ref.a_ref
  63.4 2.6 %within_block.1 = (f32[512,1024]{1,0:T(8,128)S(1)}, f32[512,1024]{1,0:T(8,128)S(1)}) custom-call(bf16[512,1024]{1,0:T(8,128)(2,1)S(1)} %get-tuple-element.160.datt_ref, bf16[512,1024]{1,0:T(8,128)(2,1)S(1)} %get-tuple-element.117.v_ref, bf16[512,1024]{1,0:T(8,128)(2,1)S(1)} %get-tuple-element.116.k_ref, bf16[512,1024]{1,0:T(8,128)(2,1)S(1)} %get-tuple-element.119.q_ref), custom_call_target="tpu_custom_call" | custom-call | flops 1 | bytes 1 | tf_op jit(solution)/shard_map/within_block/pallas_call | solution.py:88
  66.0 2.1 %collective-permute-done.11.base_ref = f32[2,128,128]{2,1,0:T(8,128)S(1)} collective-permute-done((f32[2,128,128]{2,1,0:T(8,128)S(1)}, f32[2,128,128]{2,1,0:T(8,128)S(1)}, u32[]{:S(2)}, u32[]{:S(2)}) %collective-permute-start.11) | collective-permute-done | bytes 131104 | tf_op jit(solution)/shard_map/ppermute | solution.py:422
  68.7 2.6 %collective-permute-start.16 = (f32[2,128,128]{2,1,0:T(8,128)S(1)}, f32[2,128,128]{2,1,0:T(8,128)S(1)}, u32[]{:S(2)}, u32[]{:S(2)}) collective-permute-start(f32[2,128,128]{2,1,0:T(8,128)S(1)} %get-tuple-element.171), channel_id=1, source_target_pairs={{0,12},{4,8},{8,4},{12,0},{16,28},{20,24},{24,20},{28,16},{1,13},{... | collective-permute-start | bytes 393224 | tf_op jit(solution)/shard_map/ppermute | solution.py:368
  72.5 4.0 %input_gradient_q.1.first_ref = f32[512,2048]{1,0:T(8,128)S(1)} custom-call(bf16[512,1024]{1,0:T(8,128)(2,1)S(1)} %get-tuple-element.164.own_ref.grad_ref, bf16[2048,1024]{1,0:T(8,128)(2,1)S(1)} %copy-done.4), custom_call_target="tpu_custom_call" | custom-call | flops 1 | bytes 1 | tf_op jit(solution)/shard_map/input_gradient_q/pallas_call | solution.py:607
  76.6 1.9 key_value_gradients.1
  78.5 2.1 %collective-permute-start.19 = (f32[512,512]{1,0:T(8,128)S(1)}, f32[512,512]{1,0:T(8,128)S(1)}, u32[]{:S(2)}, u32[]{:S(2)}) collective-permute-start(f32[512,512]{1,0:T(8,128)S(1)} %get-tuple-element.179), channel_id=1, source_target_pairs={{0,1},{1,0},{2,3},{3,2},{4,5},{5,4},{6,7},{7,6},{8,9},{9,8},{10,11... | collective-permute-start | bytes 3145736 | tf_op jit(solution)/shard_map/ppermute | solution.py:441
  81.1 1.7 collective-permute-done.19.rest_0_
  82.8 1.5 collective-permute-done.20.rest_1_
  84.3 2.6 %weight_k.1 = f32[512,1024]{1,0:T(8,128)} custom-call(s32[1]{0:T(128)} %bitcast.2.me_ref, bf16[16,64,1024]{2,1,0:T(8,128)(2,1)S(1)} %merge_inputs.1.x_ref, bf16[512,1024]{1,0:T(8,128)(2,1)S(1)} %get-tuple-element.189.own_ref.grad_a, f32[512,512]{1,0:T(8,128)S(1)} %collective-permute-done.19.rest_0_, f32[512,512]{1,0:T(8,128)S(1)} %collective-permute-done.20.rest_1_), custom_call_target="tpu_custom_call" | custom-call | flops 1 | bytes 1 | tf_op jit(solution)/shard_map/weight_k/pallas_call | solution.py:88
  87.0 1.3 weight_k_kept.1.a_ref
  88.3 2.6 %weight_v.1 = f32[512,1024]{1,0:T(8,128)} custom-call(s32[1]{0:T(128)} %bitcast.2.me_ref, bf16[16,64,1024]{2,1,0:T(8,128)(2,1)S(1)} %merge_inputs.1.x_ref, bf16[512,1024]{1,0:T(8,128)(2,1)S(1)} %get-tuple-element.188.own_ref.grad_b, f32[512,512]{1,0:T(8,128)S(1)} %collective-permute-done.17.rest_0_, f32[512,512]{1,0:T(8,128)S(1)} %collective-permute-done.18.rest_1_), custom_call_target="tpu_custom_call" | custom-call | flops 1 | bytes 1 | tf_op jit(solution)/shard_map/weight_v/pallas_call | solution.py:88
  92.1 1.3 weight_v_kept.1.a_ref
  93.4 1.3 copy-done.2
  94.7 12.0 %input_gradient_kv.1 = (bf16[512,2048]{1,0:T(8,128)(2,1)}, f32[8,2048]{1,0:T(8,128)S(1)}) custom-call(f32[512,2048]{1,0:T(8,128)S(1)} %input_gradient_q.1.first_ref, f32[8,512]{1,0:T(8,128)S(1)} %get-tuple-element.165.codes_ref, bf16[512,1024]{1,0:T(8,128)(2,1)S(1)} %get-tuple-element.189.own_ref.grad_a, ...), custom_call_target="tpu_custom_call" | custom-call | flops 1 | bytes 1 | tf_op jit(solution)/shard_map/input_gradient_kv/pallas_call | solution.py:623
  106.8 1.2 collective-permute-done.22
  108.1 1.7 add_rows_with.3
  110.7 1.7 add_rows.15.rest_ref.a_ref
  112.4 12.7 %collective-permute-done.24.b_ref = f32[512,1024]{1,0:T(8,128)} collective-permute-done((f32[512,1024]{1,0:T(8,128)}, f32[512,1024]{1,0:T(8,128)}, u32[]{:S(2)}, u32[]{:S(2)}) %collective-permute-start.24) | collective-permute-done | bytes 2097184 | tf_op jit(solution)/shard_map/ppermute | solution.py:441
  125.1 1.7 add_rows.16
  126.9 1.7 add_rows.17.a_ref
  128.6 6.2 %collective-permute-done.23.got_ref.b_ref = f32[272,1024]{1,0:T(8,128)S(1)} collective-permute-done((f32[272,1024]{1,0:T(8,128)S(1)}, f32[272,1024]{1,0:T(8,128)S(1)}, u32[]{:S(2)}, u32[]{:S(2)}) %collective-permute-start.23) | collective-permute-done | bytes 1114144 | tf_op jit(solution)/shard_map/ppermute | solution.py:441
  134.9 4.9 %collective-permute-done.27.b_ref = f32[512,1024]{1,0:T(8,128)} collective-permute-done((f32[512,1024]{1,0:T(8,128)}, f32[512,1024]{1,0:T(8,128)}, u32[]{:S(2)}, u32[]{:S(2)}) %collective-permute-start.27) | collective-permute-done | bytes 2097184 | tf_op jit(solution)/shard_map/ppermute | solution.py:441
  139.8 1.7 add_rows.19
  141.7 1.7 add_rows.20.a_ref
  143.4 11.8 %collective-permute-done.26.b_ref = f32[256,1024]{1,0:T(8,128)S(1)} collective-permute-done((f32[256,1024]{1,0:T(8,128)S(1)}, f32[256,1024]{1,0:T(8,128)S(1)}, u32[]{:S(2)}, u32[]{:S(2)}) %collective-permute-start.26) | collective-permute-done | bytes 1048608 | tf_op jit(solution)/shard_map/ppermute | solution.py:441
  155.3 8.4 %collective-permute-done.25.got_ref.b_ref = f32[144,1024]{1,0:T(8,128)S(1)} collective-permute-done((f32[144,1024]{1,0:T(8,128)S(1)}, f32[144,1024]{1,0:T(8,128)S(1)}, u32[]{:S(2)}, u32[]{:S(2)}) %collective-permute-start.25) | collective-permute-done | bytes 589856 | tf_op jit(solution)/shard_map/ppermute | solution.py:441
  165.9 6.5 %collective-permute-done.31.b_ref = f32[128,1024]{1,0:T(8,128)S(1)} collective-permute-done((f32[128,1024]{1,0:T(8,128)S(1)}, f32[128,1024]{1,0:T(8,128)S(1)}, u32[]{:S(2)}, u32[]{:S(2)}) %collective-permute-start.31) | collective-permute-done | bytes 524320 | tf_op jit(solution)/shard_map/ppermute | solution.py:441
  172.4 6.0 %collective-permute-done.29.b_ref = f32[128,1024]{1,0:T(8,128)S(1)} collective-permute-done((f32[128,1024]{1,0:T(8,128)S(1)}, f32[128,1024]{1,0:T(8,128)S(1)}, u32[]{:S(2)}, u32[]{:S(2)}) %collective-permute-start.29) | collective-permute-done | bytes 524320 | tf_op jit(solution)/shard_map/ppermute | solution.py:441
  181.2 1.5 collective-permute-done.34
  183.9 14.6 %collective-permute-done.33 = f32[64,1024]{1,0:T(8,128)S(1)} collective-permute-done((f32[64,1024]{1,0:T(8,128)S(1)}, f32[64,1024]{1,0:T(8,128)S(1)}, u32[]{:S(2)}, u32[]{:S(2)}) %collective-permute-start.33) | collective-permute-done | bytes 262176 | tf_op jit(solution)/shard_map/ppermute | solution.py:441
  198.5 5.5 %collective-permute-done.32 = f32[64,1024]{1,0:T(8,128)S(1)} collective-permute-done((f32[64,1024]{1,0:T(8,128)S(1)}, f32[64,1024]{1,0:T(8,128)S(1)}, u32[]{:S(2)}, u32[]{:S(2)}) %collective-permute-start.32) | collective-permute-done | bytes 262176 | tf_op jit(solution)/shard_map/ppermute | solution.py:441
  (99 shorter events, 19.4 us)
Async XLA Ops:
  0.8 0.8 copy-start.10
  1.6 0.7 copy-start.12
  2.3 14.0 %copy-start.4 = (bf16[2048,1024]{1,0:T(8,128)(2,1)S(1)}, bf16[2048,1024]{1,0:T(8,128)(2,1)}, u32[]{:S(2)}) copy-start(bf16[2048,1024]{1,0:T(8,128)(2,1)} %w_ref.1) | copy-start | bytes 12582916
  13.6 6.7 %copy-start.7 = (f32[512,1024]{1,0:T(8,128)}, f32[512,1024]{1,0:T(8,128)S(1)}, u32[]{:S(2)}) copy-start(f32[512,1024]{1,0:T(8,128)S(1)} %get-tuple-element.168.slope_ref) | copy-start | bytes 6291460
  13.6 6.7 %collective-permute-start = (f32[2,128,128]{2,1,0:T(8,128)S(1)}, f32[2,128,128]{2,1,0:T(8,128)S(1)}, u32[]{:S(2)}, u32[]{:S(2)}) collective-permute-start(f32[2,128,128]{2,1,0:T(8,128)S(1)} %get-tuple-element.123), channel_id=1, source_target_pairs={{0,4},{4,0},{8,12},{12,8},{16,20},{20,16},{24,28},{28,24},{1,5},{5... | collective-permute-start | bytes 393224 | tf_op jit(solution)/shard_map/ppermute | solution.py:368
  13.9 6.5 %collective-permute-start.1 = (f32[2,128,128]{2,1,0:T(8,128)S(1)}, f32[2,128,128]{2,1,0:T(8,128)S(1)}, u32[]{:S(2)}, u32[]{:S(2)}) collective-permute-start(f32[2,128,128]{2,1,0:T(8,128)S(1)} %get-tuple-element.124), channel_id=1, source_target_pairs={{0,8},{4,12},{8,0},{12,4},{16,24},{20,28},{24,16},{28,20},{1,9},{5... | collective-permute-start | bytes 393224 | tf_op jit(solution)/shard_map/ppermute | solution.py:368
  13.9 7.5 %collective-permute-start.2 = (f32[2,128,128]{2,1,0:T(8,128)S(1)}, f32[2,128,128]{2,1,0:T(8,128)S(1)}, u32[]{:S(2)}, u32[]{:S(2)}) collective-permute-start(f32[2,128,128]{2,1,0:T(8,128)S(1)} %get-tuple-element.125), channel_id=1, source_target_pairs={{0,12},{4,8},{8,4},{12,0},{16,28},{20,24},{24,20},{28,16},{1,13},{... | collective-permute-start | bytes 393224 | tf_op jit(solution)/shard_map/ppermute | solution.py:368
  20.3 21.0 %copy-start.9 = (bf16[1,512,1024]{2,1,0:T(8,128)(2,1)S(1)}, bf16[1,512,1024]{2,1,0:T(8,128)(2,1)}, u32[]{:S(2)}) copy-start(bf16[1,512,1024]{2,1,0:T(8,128)(2,1)} %param.15) | copy-start | bytes 3145732
  20.3 21.0 %copy-start.11 = (f32[1024]{0:T(1024)S(1)}, f32[1024]{0:T(1024)}, u32[]{:S(2)}) copy-start(f32[1024]{0:T(1024)} %param.14) | copy-start | bytes 12292
  22.5 27.8 %collective-permute-start.10 = (f32[16,64,512]{2,1,0:T(8,128)S(1)}, f32[16,64,512]{2,1,0:T(8,128)S(1)}, u32[]{:S(2)}, u32[]{:S(2)}) collective-permute-start(f32[16,64,512]{2,1,0:T(8,128)S(1)} %get-tuple-element.149), channel_id=1, source_target_pairs={{0,1},{1,0},{2,3},{3,2},{4,5},{5,4},{6,7},{7,6},{8,9},{9,8},{10,11... | collective-permute-start | bytes 6291464 | tf_op jit(solution)/shard_map/ppermute | solution.py:441
  24.7 8.8 %collective-permute-start.3 = (f32[2,128,128]{2,1,0:T(8,128)S(1)}, f32[2,128,128]{2,1,0:T(8,128)S(1)}, u32[]{:S(2)}, u32[]{:S(2)}) collective-permute-start(f32[2,128,128]{2,1,0:T(8,128)S(1)} %add_add_fusion.1), channel_id=1, source_target_pairs={{0,24},{4,28},{8,16},{12,20},{1,25},{5,29},{9,17},{13,21},{2,26},{... | collective-permute-start | bytes 393224 | tf_op jit(solution)/shard_map/ppermute | solution.py:422
  33.8 3.9 %collective-permute-start.4 = (f32[2,128,128]{2,1,0:T(8,128)S(1)}, f32[2,128,128]{2,1,0:T(8,128)S(1)}, u32[]{:S(2)}, u32[]{:S(2)}) collective-permute-start(f32[2,128,128]{2,1,0:T(8,128)S(1)} %get-tuple-element.134), channel_id=1, source_target_pairs={{0,4},{4,0},{8,12},{12,8},{16,20},{20,16},{24,28},{28,24},{1,5},{5... | collective-permute-start | bytes 393224 | tf_op jit(solution)/shard_map/ppermute | solution.py:368
  34.1 4.1 %collective-permute-start.5 = (f32[2,128,128]{2,1,0:T(8,128)S(1)}, f32[2,128,128]{2,1,0:T(8,128)S(1)}, u32[]{:S(2)}, u32[]{:S(2)}) collective-permute-start(f32[2,128,128]{2,1,0:T(8,128)S(1)} %get-tuple-element.135), channel_id=1, source_target_pairs={{0,8},{4,12},{8,0},{12,4},{16,24},{20,28},{24,16},{28,20},{1,9},{5... | collective-permute-start | bytes 393224 | tf_op jit(solution)/shard_map/ppermute | solution.py:368
  34.1 7.2 %collective-permute-start.6 = (f32[2,128,128]{2,1,0:T(8,128)S(1)}, f32[2,128,128]{2,1,0:T(8,128)S(1)}, u32[]{:S(2)}, u32[]{:S(2)}) collective-permute-start(f32[2,128,128]{2,1,0:T(8,128)S(1)} %get-tuple-element.136), channel_id=1, source_target_pairs={{0,12},{4,8},{8,4},{12,0},{16,28},{20,24},{24,20},{28,16},{1,13},{... | collective-permute-start | bytes 393224 | tf_op jit(solution)/shard_map/ppermute | solution.py:368
  47.2 12.2 %collective-permute-start.12 = (f32[512,512]{1,0:T(8,128)S(1)}, f32[512,512]{1,0:T(8,128)S(1)}, u32[]{:S(2)}, u32[]{:S(2)}) collective-permute-start(f32[512,512]{1,0:T(8,128)S(1)} %get-tuple-element.154), channel_id=1, source_target_pairs={{0,1},{1,0},{2,3},{3,2},{4,5},{5,4},{6,7},{7,6},{8,9},{9,8},{10,11... | collective-permute-start | bytes 3145736 | tf_op jit(solution)/shard_map/ppermute | solution.py:441
  49.8 9.7 %collective-permute-start.13 = (f32[512,512]{1,0:T(8,128)S(1)}, f32[512,512]{1,0:T(8,128)S(1)}, u32[]{:S(2)}, u32[]{:S(2)}) collective-permute-start(f32[512,512]{1,0:T(8,128)S(1)} %get-tuple-element.155), channel_id=1, source_target_pairs={{0,1},{1,0},{2,3},{3,2},{4,5},{5,4},{6,7},{7,6},{8,9},{9,8},{10,11... | collective-permute-start | bytes 3145736 | tf_op jit(solution)/shard_map/ppermute | solution.py:441
  49.8 4.6 %collective-permute-start.7 = (f32[2,128,128]{2,1,0:T(8,128)S(1)}, f32[2,128,128]{2,1,0:T(8,128)S(1)}, u32[]{:S(2)}, u32[]{:S(2)}) collective-permute-start(f32[2,128,128]{2,1,0:T(8,128)S(1)} %get-tuple-element.146), channel_id=1, source_target_pairs={{0,4},{4,0},{8,12},{12,8},{16,20},{20,16},{24,28},{28,24},{1,5},{5... | collective-permute-start | bytes 393224 | tf_op jit(solution)/shard_map/ppermute | solution.py:368
  50.1 4.4 %collective-permute-start.8 = (f32[2,128,128]{2,1,0:T(8,128)S(1)}, f32[2,128,128]{2,1,0:T(8,128)S(1)}, u32[]{:S(2)}, u32[]{:S(2)}) collective-permute-start(f32[2,128,128]{2,1,0:T(8,128)S(1)} %get-tuple-element.147), channel_id=1, source_target_pairs={{0,8},{4,12},{8,0},{12,4},{16,24},{20,28},{24,16},{28,20},{1,9},{5... | collective-permute-start | bytes 393224 | tf_op jit(solution)/shard_map/ppermute | solution.py:368
  50.3 7.9 %collective-permute-start.9 = (f32[2,128,128]{2,1,0:T(8,128)S(1)}, f32[2,128,128]{2,1,0:T(8,128)S(1)}, u32[]{:S(2)}, u32[]{:S(2)}) collective-permute-start(f32[2,128,128]{2,1,0:T(8,128)S(1)} %get-tuple-element.148), channel_id=1, source_target_pairs={{0,12},{4,8},{8,4},{12,0},{16,28},{20,24},{24,20},{28,16},{1,13},{... | collective-permute-start | bytes 393224 | tf_op jit(solution)/shard_map/ppermute | solution.py:368
  58.2 10.0 %collective-permute-start.11 = (f32[2,128,128]{2,1,0:T(8,128)S(1)}, f32[2,128,128]{2,1,0:T(8,128)S(1)}, u32[]{:S(2)}, u32[]{:S(2)}) collective-permute-start(f32[2,128,128]{2,1,0:T(8,128)S(1)} %add_add_fusion), channel_id=1, source_target_pairs={{28,4},{24,0},{20,12},{16,8},{29,5},{25,1},{21,13},{17,9},{30,6},{... | collective-permute-start | bytes 393224 | tf_op jit(solution)/shard_map/ppermute | solution.py:422
  68.6 8.0 %collective-permute-start.14 = (f32[2,128,128]{2,1,0:T(8,128)S(1)}, f32[2,128,128]{2,1,0:T(8,128)S(1)}, u32[]{:S(2)}, u32[]{:S(2)}) collective-permute-start(f32[2,128,128]{2,1,0:T(8,128)S(1)} %get-tuple-element.169), channel_id=1, source_target_pairs={{0,4},{4,0},{8,12},{12,8},{16,20},{20,16},{24,28},{28,24},{1,5},{5... | collective-permute-start | bytes 393224 | tf_op jit(solution)/shard_map/ppermute | solution.py:368
  68.6 7.9 %collective-permute-start.15 = (f32[2,128,128]{2,1,0:T(8,128)S(1)}, f32[2,128,128]{2,1,0:T(8,128)S(1)}, u32[]{:S(2)}, u32[]{:S(2)}) collective-permute-start(f32[2,128,128]{2,1,0:T(8,128)S(1)} %get-tuple-element.170), channel_id=1, source_target_pairs={{0,8},{4,12},{8,0},{12,4},{16,24},{20,28},{24,16},{28,20},{1,9},{5... | collective-permute-start | bytes 393224 | tf_op jit(solution)/shard_map/ppermute | solution.py:368
  68.7 7.8 %collective-permute-start.16 = (f32[2,128,128]{2,1,0:T(8,128)S(1)}, f32[2,128,128]{2,1,0:T(8,128)S(1)}, u32[]{:S(2)}, u32[]{:S(2)}) collective-permute-start(f32[2,128,128]{2,1,0:T(8,128)S(1)} %get-tuple-element.171), channel_id=1, source_target_pairs={{0,12},{4,8},{8,4},{12,0},{16,28},{20,24},{24,20},{28,16},{1,13},{... | collective-permute-start | bytes 393224 | tf_op jit(solution)/shard_map/ppermute | solution.py:368
  71.3 36.8 %collective-permute-start.21 = (f32[512,1024]{1,0:T(8,128)}, f32[512,1024]{1,0:T(8,128)}, u32[]{:S(2)}, u32[]{:S(2)}) collective-permute-start(f32[512,1024]{1,0:T(8,128)} %weight_q.1), channel_id=1, source_target_pairs={{0,4},{1,3},{2,6},{3,1},{4,0},{5,7},{6,2},{7,5},{8,12},{9,11},{10,... | collective-permute-start | bytes 6291464 | tf_op jit(solution)/shard_map/ppermute | solution.py:441
  72.5 4.1 %copy-start.8 = (f32[512,1024]{1,0:T(8,128)S(1)}, f32[512,1024]{1,0:T(8,128)}, u32[]{:S(2)}) copy-start(f32[512,1024]{1,0:T(8,128)} %copy-done.7) | copy-start | bytes 6291460
  78.5 4.4 %collective-permute-start.19 = (f32[512,512]{1,0:T(8,128)S(1)}, f32[512,512]{1,0:T(8,128)S(1)}, u32[]{:S(2)}, u32[]{:S(2)}) collective-permute-start(f32[512,512]{1,0:T(8,128)S(1)} %get-tuple-element.179), channel_id=1, source_target_pairs={{0,1},{1,0},{2,3},{3,2},{4,5},{5,4},{6,7},{7,6},{8,9},{9,8},{10,11... | collective-permute-start | bytes 3145736 | tf_op jit(solution)/shard_map/ppermute | solution.py:441
  80.5 3.8 %collective-permute-start.20 = (f32[512,512]{1,0:T(8,128)S(1)}, f32[512,512]{1,0:T(8,128)S(1)}, u32[]{:S(2)}, u32[]{:S(2)}) collective-permute-start(f32[512,512]{1,0:T(8,128)S(1)} %get-tuple-element.180), channel_id=1, source_target_pairs={{0,1},{1,0},{2,3},{3,2},{4,5},{5,4},{6,7},{7,6},{8,9},{9,8},{10,11... | collective-permute-start | bytes 3145736 | tf_op jit(solution)/shard_map/ppermute | solution.py:441
  80.6 7.6 %collective-permute-start.17 = (f32[512,512]{1,0:T(8,128)S(1)}, f32[512,512]{1,0:T(8,128)S(1)}, u32[]{:S(2)}, u32[]{:S(2)}) collective-permute-start(f32[512,512]{1,0:T(8,128)S(1)} %get-tuple-element.177), channel_id=1, source_target_pairs={{0,1},{1,0},{2,3},{3,2},{4,5},{5,4},{6,7},{7,6},{8,9},{9,8},{10,11... | collective-permute-start | bytes 3145736 | tf_op jit(solution)/shard_map/ppermute | solution.py:441
  81.1 7.2 %collective-permute-start.18 = (f32[512,512]{1,0:T(8,128)S(1)}, f32[512,512]{1,0:T(8,128)S(1)}, u32[]{:S(2)}, u32[]{:S(2)}) collective-permute-start(f32[512,512]{1,0:T(8,128)S(1)} %get-tuple-element.178), channel_id=1, source_target_pairs={{0,1},{1,0},{2,3},{3,2},{4,5},{5,4},{6,7},{7,6},{8,9},{9,8},{10,11... | collective-permute-start | bytes 3145736 | tf_op jit(solution)/shard_map/ppermute | solution.py:441
  88.2 2.6 %copy-start = (f32[512,1024]{1,0:T(8,128)}, f32[512,1024]{1,0:T(8,128)S(1)}, u32[]{:S(2)}) copy-start(f32[512,1024]{1,0:T(8,128)S(1)} %weight_k_kept.1.a_ref) | copy-start | bytes 6291460
  88.3 6.4 %copy-start.6 = (bf16[2048,1024]{1,0:T(8,128)(2,1)S(1)}, bf16[2048,1024]{1,0:T(8,128)(2,1)}, u32[]{:S(2)}) copy-start(bf16[2048,1024]{1,0:T(8,128)(2,1)} %wb_ref.1) | copy-start | bytes 12582916
  90.8 3.8 %copy-start.5 = (bf16[2048,1024]{1,0:T(8,128)(2,1)S(1)}, bf16[2048,1024]{1,0:T(8,128)(2,1)}, u32[]{:S(2)}) copy-start(bf16[2048,1024]{1,0:T(8,128)(2,1)} %wa_ref.1) | copy-start | bytes 12582916
  90.8 34.3 %collective-permute-start.24 = (f32[512,1024]{1,0:T(8,128)}, f32[512,1024]{1,0:T(8,128)}, u32[]{:S(2)}, u32[]{:S(2)}) collective-permute-start(f32[512,1024]{1,0:T(8,128)} %weight_v.1), channel_id=1, source_target_pairs={{0,4},{1,3},{2,6},{3,1},{4,0},{5,7},{6,2},{7,5},{8,12},{9,11},{10,... | collective-permute-start | bytes 6291464 | tf_op jit(solution)/shard_map/ppermute | solution.py:441
  92.1 47.8 %collective-permute-start.27 = (f32[512,1024]{1,0:T(8,128)}, f32[512,1024]{1,0:T(8,128)}, u32[]{:S(2)}, u32[]{:S(2)}) collective-permute-start(f32[512,1024]{1,0:T(8,128)} %weight_k.1), channel_id=1, source_target_pairs={{0,8},{1,9},{2,10},{3,11},{4,12},{5,13},{6,14},{7,15},{8,0},{9,1},... | collective-permute-start | bytes 6291464 | tf_op jit(solution)/shard_map/ppermute | solution.py:441
  93.4 1.3 copy-start.2
  106.7 1.3 collective-permute-start.22
  109.8 15.4 %copy-start.3 = (f32[512,1024]{1,0:T(8,128)S(1)}, f32[512,1024]{1,0:T(8,128)}, u32[]{:S(2)}) copy-start(f32[512,1024]{1,0:T(8,128)} %copy-done.2) | copy-start | bytes 6291460
  109.8 25.0 %collective-permute-start.23 = (f32[272,1024]{1,0:T(8,128)S(1)}, f32[272,1024]{1,0:T(8,128)S(1)}, u32[]{:S(2)}, u32[]{:S(2)}) collective-permute-start(f32[272,1024]{1,0:T(8,128)S(1)} %get-tuple-element.195), channel_id=1, source_target_pairs={{0,2},{1,5},{2,0},{3,7},{4,6},{5,1},{6,4},{7,3},{8,10},{9,13},{10,... | collective-permute-start | bytes 3342344 | tf_op jit(solution)/shard_map/ppermute | solution.py:441
  126.8 28.4 %collective-permute-start.26 = (f32[256,1024]{1,0:T(8,128)S(1)}, f32[256,1024]{1,0:T(8,128)S(1)}, u32[]{:S(2)}, u32[]{:S(2)}) collective-permute-start(f32[256,1024]{1,0:T(8,128)S(1)} %add_rows.16), channel_id=1, source_target_pairs={{0,2},{1,9},{2,0},{3,11},{4,6},{5,13},{6,4},{7,15},{8,10},{9,1},{1... | collective-permute-start | bytes 3145736 | tf_op jit(solution)/shard_map/ppermute | solution.py:441
  134.8 5.0 %copy-start.1 = (f32[512,1024]{1,0:T(8,128)S(1)}, f32[512,1024]{1,0:T(8,128)}, u32[]{:S(2)}) copy-start(f32[512,1024]{1,0:T(8,128)} %copy-done) | copy-start | bytes 6291460
  141.5 22.3 %collective-permute-start.30 = (f32[256,1024]{1,0:T(8,128)S(1)}, f32[256,1024]{1,0:T(8,128)S(1)}, u32[]{:S(2)}, u32[]{:S(2)}) collective-permute-start(f32[256,1024]{1,0:T(8,128)S(1)} %add_rows.19), channel_id=1, source_target_pairs={{0,4},{1,3},{2,6},{3,1},{4,0},{5,7},{6,2},{7,5},{8,12},{9,11},{10,... | collective-permute-start | bytes 3145736 | tf_op jit(solution)/shard_map/ppermute | solution.py:441
  141.6 22.2 %collective-permute-start.25 = (f32[144,1024]{1,0:T(8,128)S(1)}, f32[144,1024]{1,0:T(8,128)S(1)}, u32[]{:S(2)}, u32[]{:S(2)}) collective-permute-start(f32[144,1024]{1,0:T(8,128)S(1)} %get-tuple-element.201), channel_id=1, source_target_pairs={{0,8},{1,9},{2,10},{3,11},{4,12},{5,13},{6,14},{7,15},{8,0},{9,1},... | collective-permute-start | bytes 1769480 | tf_op jit(solution)/shard_map/ppermute | solution.py:441
  163.9 8.4 %collective-permute-start.31 = (f32[128,1024]{1,0:T(8,128)S(1)}, f32[128,1024]{1,0:T(8,128)S(1)}, u32[]{:S(2)}, u32[]{:S(2)}) collective-permute-start(f32[128,1024]{1,0:T(8,128)S(1)} %add_rows.24), channel_id=1, source_target_pairs={{0,2},{1,5},{2,0},{3,7},{4,6},{5,1},{6,4},{7,3},{8,10},{9,13},{10,... | collective-permute-start | bytes 1572872 | tf_op jit(solution)/shard_map/ppermute | solution.py:441
  164.3 14.1 %collective-permute-start.29 = (f32[128,1024]{1,0:T(8,128)S(1)}, f32[128,1024]{1,0:T(8,128)S(1)}, u32[]{:S(2)}, u32[]{:S(2)}) collective-permute-start(f32[128,1024]{1,0:T(8,128)S(1)} %add_rows.21), channel_id=1, source_target_pairs={{0,8},{1,5},{2,10},{3,7},{4,12},{5,1},{6,14},{7,3},{8,0},{9,13},{1... | collective-permute-start | bytes 1572872 | tf_op jit(solution)/shard_map/ppermute | solution.py:441
  165.5 13.6 %collective-permute-start.28 = (f32[80,1024]{1,0:T(8,128)S(1)}, f32[80,1024]{1,0:T(8,128)S(1)}, u32[]{:S(2)}, u32[]{:S(2)}) collective-permute-start(f32[80,1024]{1,0:T(8,128)S(1)} %get-tuple-element.209), channel_id=1, source_target_pairs={{0,24},{1,25},{2,26},{3,27},{4,28},{5,29},{6,30},{7,31},{8,16},{9,... | collective-permute-start | bytes 983048 | tf_op jit(solution)/shard_map/ppermute | solution.py:441
  179.2 3.5 %collective-permute-start.34 = (f32[16,1024]{1,0:T(8,128)S(1)}, f32[16,1024]{1,0:T(8,128)S(1)}, u32[]{:S(2)}, u32[]{:S(2)}) collective-permute-start(f32[16,1024]{1,0:T(8,128)S(1)} %get-tuple-element.220), channel_id=1, source_target_pairs={{0,4},{1,3},{2,6},{3,1},{4,0},{5,7},{6,2},{7,5},{8,12},{9,11},{10,... | collective-permute-start | bytes 196616 | tf_op jit(solution)/shard_map/ppermute | solution.py:441
  179.7 18.8 %collective-permute-start.33 = (f32[64,1024]{1,0:T(8,128)S(1)}, f32[64,1024]{1,0:T(8,128)S(1)}, u32[]{:S(2)}, u32[]{:S(2)}) collective-permute-start(f32[64,1024]{1,0:T(8,128)S(1)} %add_rows.28), channel_id=1, source_target_pairs={{0,24},{1,25},{2,26},{3,27},{4,28},{5,29},{6,30},{7,31},{8,16},{9,... | collective-permute-start | bytes 786440 | tf_op jit(solution)/shard_map/ppermute | solution.py:441
  180.4 23.6 %collective-permute-start.32 = (f32[64,1024]{1,0:T(8,128)S(1)}, f32[64,1024]{1,0:T(8,128)S(1)}, u32[]{:S(2)}, u32[]{:S(2)}) collective-permute-start(f32[64,1024]{1,0:T(8,128)S(1)} %add_rows.26), channel_id=1, source_target_pairs={{0,24},{1,25},{2,26},{3,27},{4,28},{5,29},{6,30},{7,31},{8,16},{9,... | collective-permute-start | bytes 786440 | tf_op jit(solution)/shard_map/ppermute | solution.py:441

commit v3 on v2

--- a/solution.py
+++ b/solution.py
@@ -685,9 +685,9 @@
             start += units
         return out
 
-    chunks_q = chunks_of([(8, "yxzw", "xyzw")])
-    chunks_k = chunks_of([(8, "zyxw", "zxyw")])
-    chunks_v = chunks_of([(8, "yxzw", "xzyw")])
+    chunks_q = chunks_of([(8, "xzwy", "zxyw")])
+    chunks_k = chunks_of([(8, "xzwy", "yxzw")])
+    chunks_v = chunks_of([(8, "zyxw", "yxzw")])
     every = chunks_q + chunks_k + chunks_v
 
     def begin(chunks, own, others, name):
@@ -736,16 +736,16 @@
 
     small = small + order.tied(both_exchange(small, (1, 1)))
     order.mark(small)
-    for index in (0, 2, 0, 1, 2, 0, 1):
+    for index in (0, 1, 0, 2, 1, 0, 2, 1, 2):
         advance(index)
     while any(c.step < dims for c in every):
-        for index, c in enumerate(every):
-            if c.step < dims:
+        for index in (0, 1, 2):
+            if every[index].step < dims:
                 advance(index)
     advance(0)
     small = small + order.tied(both_exchange(small, carrier.masks(0)))
     order.mark(small)
-    for index in (2, 1):
+    for index in (1, 2):
         advance(index)
     small = small.reshape(-1)[:used] * grad_scale
     gain_sum, code_sum = small[:features], small[features:].reshape(codes, width)

time: 205 us -> 195 us (0.951)
  waiting for transfers between devices: 102 us -> 87.6 us
  starting transfers between devices: 30.3 us -> 33.7 us
    ppermute x21, waiting for transfers between devices: 83.2 us -> 67.7 us  [both_exchange(): lax.ppermute(array, AXES, [(i, i ^ masks[i % 2]) for i in range(total)])]
    ppermute x21, starting transfers between devices: 15.1 us -> 18.4 us  [both_exchange(): lax.ppermute(array, AXES, [(i, i ^ masks[i % 2]) for i in range(total)])]
  transfers between devices with their start and end apart: 35 -> 35, of which waited for: 22 -> 23; matrix products, arithmetic and copies ran while one was open for 1% -> 1% of each run, Pallas kernels for 26% -> 27%
where the time goes in v3:
time: 195 us; the launch traced here: 194 us
  waiting for transfers between devices  87.6 us (45%)
  Pallas kernels  66 us (34%)
  starting transfers between devices  33.7 us (17%)
  local copies, waits for them, and re-layouts  4.17 us (2%)
    ppermute x21, waiting for transfers between devices, both_exchange(): lax.ppermute(array, AXES, [(i, i ^ masks[i % 2]) for i in range(total)])  67.7 us
    pallas_call x34, Pallas kernels, in_vmem(): pl.pallas_call(kernel, in_specs=[SMEM] * len(slots) + [VMEM] * len(inputs...  38.7 us
    ppermute x21, starting transfers between devices, both_exchange(): lax.ppermute(array, AXES, [(i, i ^ masks[i % 2]) for i in range(total)])  18.4 us
    ppermute x12, waiting for transfers between devices, exchange(): return lax.ppermute(array, axis, [(i, i ^ mask) for i in range(count)])  12.1 us
    pallas_call x1, Pallas kernels, rest_input_gradient(): pl.pallas_call(rest_input_kernel, grid=(d // WIDE,), in_specs=[out_column...  12 us
    pallas_call x1, Pallas kernels, embed_keys_values(): pl.pallas_call(embed_kernel, in_specs=[SMEM] + [HBM] * 5, out_specs=[VMEM...  11.3 us
    ppermute x12, starting transfers between devices, exchange(): return lax.ppermute(array, axis, [(i, i ^ mask) for i in range(count)])  10.8 us
    ppermute x2, waiting for transfers between devices, second(): self.bases.append(lax.ppermute(total, 'seq', pairs))  7.75 us
  transfers between devices with their start and end apart: 35, of which 23 were waited for; matrix products, arithmetic and copies ran while one was open for 1% of the time, Pallas kernels for 27%

profile of v3, /device:TPU:13, one launch (start us, length us, event | category | flops | bytes accessed | tf_op | source)
XLA Modules:
  0.0 193.7 jit_solution(6291608855732864223)
XLA Ops:
  2.3 11.3 %embed_keys_values.1 = (bf16[512,2048]{1,0:T(8,128)(2,1)S(1)}, f32[8,512]{1,0:T(8,128)S(1)}, bf16[512,1024]{1,0:T(8,128)(2,1)S(1)}, f32[512,1024]{1,0:T(8,128)S(...) custom-call(s32[2]{0:T(128)S(1)} %pad_add_fusion.slots, ...), custom_call_target="tpu_custom_call" | custom-call | flops 1 | bytes 1 | tf_op jit(solution)/shard_map/embed_keys_values/pallas_call | solution.py:158
  13.9 2.4 %collective-permute-start.2 = (f32[2,128,128]{2,1,0:T(8,128)S(1)}, f32[2,128,128]{2,1,0:T(8,128)S(1)}, u32[]{:S(2)}, u32[]{:S(2)}) collective-permute-start(f32[2,128,128]{2,1,0:T(8,128)S(1)} %get-tuple-element.125), channel_id=1, source_target_pairs={{0,12},{4,8},{8,4},{12,0},{16,28},{20,24},{24,20},{28,16},{1,13},{... | collective-permute-start | bytes 393224 | tf_op jit(solution)/shard_map/ppermute | solution.py:368
  16.3 4.0 %queries_scores.1 = (bf16[512,1024]{1,0:T(8,128)(2,1)S(1)}, f32[512,1024]{1,0:T(8,128)S(1)}, f32[512,1024]{1,0:T(8,128)S(1)}) custom-call(bf16[512,2048]{1,0:T(8,128)(2,1)S(1)} %get-tuple-element.130.x_ref, bf16[2048,1024]{1,0:T(8,128)(2,1)S(1)} %copy-done.4, bf16[512,1024]{1,0:T(8,128)(2,1)S(1)} %get-tuple-element.116.k_ref, ...), custom_call_target="tpu_custom_call" | custom-call | flops 1 | bytes 1 | tf_op jit(solution)/shard_map/queries_scores/pallas_call | solution.py:88
  22.5 2.2 %collective-permute-start.10 = (f32[16,64,512]{2,1,0:T(8,128)S(1)}, f32[16,64,512]{2,1,0:T(8,128)S(1)}, u32[]{:S(2)}, u32[]{:S(2)}) collective-permute-start(f32[16,64,512]{2,1,0:T(8,128)S(1)} %get-tuple-element.149), channel_id=1, source_target_pairs={{0,1},{1,0},{2,3},{3,2},{4,5},{5,4},{6,7},{7,6},{8,9},{9,8},{10,11... | collective-permute-start | bytes 6291464 | tf_op jit(solution)/shard_map/ppermute | solution.py:441
  24.7 3.2 %collective-permute-start.3 = (f32[2,128,128]{2,1,0:T(8,128)S(1)}, f32[2,128,128]{2,1,0:T(8,128)S(1)}, u32[]{:S(2)}, u32[]{:S(2)}) collective-permute-start(f32[2,128,128]{2,1,0:T(8,128)S(1)} %add_add_fusion.1), channel_id=1, source_target_pairs={{0,24},{4,28},{8,16},{12,20},{1,25},{5,29},{9,17},{13,21},{2,26},{... | collective-permute-start | bytes 393224 | tf_op jit(solution)/shard_map/ppermute | solution.py:422
  27.9 5.5 %collective-permute-done.3.base_ref = f32[2,128,128]{2,1,0:T(8,128)S(1)} collective-permute-done((f32[2,128,128]{2,1,0:T(8,128)S(1)}, f32[2,128,128]{2,1,0:T(8,128)S(1)}, u32[]{:S(2)}, u32[]{:S(2)}) %collective-permute-start.3) | collective-permute-done | bytes 131104 | tf_op jit(solution)/shard_map/ppermute | solution.py:422
  34.1 2.4 %collective-permute-start.6 = (f32[2,128,128]{2,1,0:T(8,128)S(1)}, f32[2,128,128]{2,1,0:T(8,128)S(1)}, u32[]{:S(2)}, u32[]{:S(2)}) collective-permute-start(f32[2,128,128]{2,1,0:T(8,128)S(1)} %get-tuple-element.136), channel_id=1, source_target_pairs={{0,12},{4,8},{8,4},{12,0},{16,28},{20,24},{24,20},{28,16},{1,13},{... | collective-permute-start | bytes 393224 | tf_op jit(solution)/shard_map/ppermute | solution.py:368
  38.2 3.1 %collective-permute-done.6.rest_3_ = f32[2,128,128]{2,1,0:T(8,128)S(1)} collective-permute-done((f32[2,128,128]{2,1,0:T(8,128)S(1)}, f32[2,128,128]{2,1,0:T(8,128)S(1)}, u32[]{:S(2)}, u32[]{:S(2)}) %collective-permute-start.6) | collective-permute-done | bytes 131104 | tf_op jit(solution)/shard_map/ppermute | solution.py:368
  41.3 3.3 %norm_gradient.1 = (bf16[512,1024]{1,0:T(8,128)(2,1)S(1)}, f32[1,1024]{1,0:T(1,128)S(1)}, f32[2,8,128,128]{3,2,1,0:T(8,128)S(1)}, f32[2,128,128]{2,1,0:T(8,128)S...) custom-call(s32[2]{0:T(128)S(1)} %pad_add_fusion.slots, ...), custom_call_target="tpu_custom_call" | custom-call | flops 1 | bytes 1 | tf_op jit(solution)/shard_map/norm_gradient/pallas_call | solution.py:88
  44.7 2.6 %query_gradient.1 = (bf16[512,1024]{1,0:T(8,128)(2,1)S(1)}, f32[512,512]{1,0:T(8,128)S(1)}, f32[512,512]{1,0:T(8,128)S(1)}) custom-call(s32[2]{0:T(128)S(1)} %pad_add_fusion.slots, bf16[512,1024]{1,0:T(8,128)(2,1)S(1)} %get-tuple-element.160.datt_ref, bf16[512,1024]{1,0:T(8,128)(2,1)S(1)} %get-tuple-element.117.v_ref, ...), custom_call_target="tpu_custom_call" | custom-call | flops 1 | bytes 1 | tf_op jit(solution)/shard_map/query_gradient/pallas_call | solution.py:88
  47.2 2.5 %collective-permute-start.12 = (f32[512,512]{1,0:T(8,128)S(1)}, f32[512,512]{1,0:T(8,128)S(1)}, u32[]{:S(2)}, u32[]{:S(2)}) collective-permute-start(f32[512,512]{1,0:T(8,128)S(1)} %get-tuple-element.154), channel_id=1, source_target_pairs={{0,1},{1,0},{2,3},{3,2},{4,5},{5,4},{6,7},{7,6},{8,9},{9,8},{10,11... | collective-permute-start | bytes 3145736 | tf_op jit(solution)/shard_map/ppermute | solution.py:441
  50.3 2.2 %collective-permute-start.9 = (f32[2,128,128]{2,1,0:T(8,128)S(1)}, f32[2,128,128]{2,1,0:T(8,128)S(1)}, u32[]{:S(2)}, u32[]{:S(2)}) collective-permute-start(f32[2,128,128]{2,1,0:T(8,128)S(1)} %get-tuple-element.148), channel_id=1, source_target_pairs={{0,12},{4,8},{8,4},{12,0},{16,28},{20,24},{24,20},{28,16},{1,13},{... | collective-permute-start | bytes 393224 | tf_op jit(solution)/shard_map/ppermute | solution.py:368
  52.7 1.8 collective-permute-done.7.refs_1_
  54.5 3.7 %collective-permute-done.9.refs_3_ = f32[2,128,128]{2,1,0:T(8,128)S(1)} collective-permute-done((f32[2,128,128]{2,1,0:T(8,128)S(1)}, f32[2,128,128]{2,1,0:T(8,128)S(1)}, u32[]{:S(2)}, u32[]{:S(2)}) %collective-permute-start.9) | collective-permute-done | bytes 131104 | tf_op jit(solution)/shard_map/ppermute | solution.py:368
  58.2 1.3 collective-permute-start.11
  59.5 2.6 %weight_q.1 = f32[512,1024]{1,0:T(8,128)} custom-call(s32[1]{0:T(128)} %bitcast.2.me_ref, bf16[16,64,1024]{2,1,0:T(8,128)(2,1)S(1)} %merge_inputs.1.x_ref, bf16[512,1024]{1,0:T(8,128)(2,1)S(1)} %get-tuple-element.164.own_ref.grad_ref, f32[512,512]{1,0:T(8,128)S(1)} %collective-permute-done.12.rest_0_, f32[512,512]{1,0:T(8,128)S(1)} %collective-permute-done.13.rest_1_), custom_call_target="tpu_custom_call" | custom-call | flops 1 | bytes 1 | tf_op jit(solution)/shard_map/weight_q/pallas_call | solution.py:88
  62.1 1.3 weight_q_kept.1.rest_ref.a_ref
  63.4 2.6 %within_block.1 = (f32[512,1024]{1,0:T(8,128)S(1)}, f32[512,1024]{1,0:T(8,128)S(1)}) custom-call(bf16[512,1024]{1,0:T(8,128)(2,1)S(1)} %get-tuple-element.160.datt_ref, bf16[512,1024]{1,0:T(8,128)(2,1)S(1)} %get-tuple-element.117.v_ref, bf16[512,1024]{1,0:T(8,128)(2,1)S(1)} %get-tuple-element.116.k_ref, bf16[512,1024]{1,0:T(8,128)(2,1)S(1)} %get-tuple-element.119.q_ref), custom_call_target="tpu_custom_call" | custom-call | flops 1 | bytes 1 | tf_op jit(solution)/shard_map/within_block/pallas_call | solution.py:88
  66.0 2.2 %collective-permute-done.11.base_ref = f32[2,128,128]{2,1,0:T(8,128)S(1)} collective-permute-done((f32[2,128,128]{2,1,0:T(8,128)S(1)}, f32[2,128,128]{2,1,0:T(8,128)S(1)}, u32[]{:S(2)}, u32[]{:S(2)}) %collective-permute-start.11) | collective-permute-done | bytes 131104 | tf_op jit(solution)/shard_map/ppermute | solution.py:422
  68.7 2.6 %collective-permute-start.16 = (f32[2,128,128]{2,1,0:T(8,128)S(1)}, f32[2,128,128]{2,1,0:T(8,128)S(1)}, u32[]{:S(2)}, u32[]{:S(2)}) collective-permute-start(f32[2,128,128]{2,1,0:T(8,128)S(1)} %get-tuple-element.171), channel_id=1, source_target_pairs={{0,12},{4,8},{8,4},{12,0},{16,28},{20,24},{24,20},{28,16},{1,13},{... | collective-permute-start | bytes 393224 | tf_op jit(solution)/shard_map/ppermute | solution.py:368
  71.3 4.0 %input_gradient_q.1.first_ref = f32[512,2048]{1,0:T(8,128)S(1)} custom-call(bf16[512,1024]{1,0:T(8,128)(2,1)S(1)} %get-tuple-element.164.own_ref.grad_ref, bf16[2048,1024]{1,0:T(8,128)(2,1)S(1)} %copy-done.4), custom_call_target="tpu_custom_call" | custom-call | flops 1 | bytes 1 | tf_op jit(solution)/shard_map/input_gradient_q/pallas_call | solution.py:607
  76.1 1.9 key_value_gradients.1
  78.0 4.2 %collective-permute-start.19 = (f32[512,512]{1,0:T(8,128)S(1)}, f32[512,512]{1,0:T(8,128)S(1)}, u32[]{:S(2)}, u32[]{:S(2)}) collective-permute-start(f32[512,512]{1,0:T(8,128)S(1)} %get-tuple-element.179), channel_id=1, source_target_pairs={{0,1},{1,0},{2,3},{3,2},{4,5},{5,4},{6,7},{7,6},{8,9},{9,8},{10,11... | collective-permute-start | bytes 3145736 | tf_op jit(solution)/shard_map/ppermute | solution.py:441
  82.8 1.7 collective-permute-done.19.rest_0_
  84.5 1.5 collective-permute-done.20.rest_1_
  86.0 2.7 %weight_k.1 = f32[512,1024]{1,0:T(8,128)} custom-call(s32[1]{0:T(128)} %bitcast.2.me_ref, bf16[16,64,1024]{2,1,0:T(8,128)(2,1)S(1)} %merge_inputs.1.x_ref, bf16[512,1024]{1,0:T(8,128)(2,1)S(1)} %get-tuple-element.189.own_ref.grad_a, f32[512,512]{1,0:T(8,128)S(1)} %collective-permute-done.19.rest_0_, f32[512,512]{1,0:T(8,128)S(1)} %collective-permute-done.20.rest_1_), custom_call_target="tpu_custom_call" | custom-call | flops 1 | bytes 1 | tf_op jit(solution)/shard_map/weight_k/pallas_call | solution.py:88
  88.9 1.3 weight_k_kept.1.a_ref
  90.2 2.6 %weight_v.1 = f32[512,1024]{1,0:T(8,128)} custom-call(s32[1]{0:T(128)} %bitcast.2.me_ref, bf16[16,64,1024]{2,1,0:T(8,128)(2,1)S(1)} %merge_inputs.1.x_ref, bf16[512,1024]{1,0:T(8,128)(2,1)S(1)} %get-tuple-element.188.own_ref.grad_b, f32[512,512]{1,0:T(8,128)S(1)} %collective-permute-done.17.rest_0_, f32[512,512]{1,0:T(8,128)S(1)} %collective-permute-done.18.rest_1_), custom_call_target="tpu_custom_call" | custom-call | flops 1 | bytes 1 | tf_op jit(solution)/shard_map/weight_v/pallas_call | solution.py:88
  94.0 1.3 weight_v_kept.1.a_ref
  95.3 1.3 copy-done
  96.6 12.0 %input_gradient_kv.1 = (bf16[512,2048]{1,0:T(8,128)(2,1)}, f32[8,2048]{1,0:T(8,128)S(1)}) custom-call(f32[512,2048]{1,0:T(8,128)S(1)} %input_gradient_q.1.first_ref, f32[8,512]{1,0:T(8,128)S(1)} %get-tuple-element.165.codes_ref, bf16[512,1024]{1,0:T(8,128)(2,1)S(1)} %get-tuple-element.189.own_ref.grad_a, ...), custom_call_target="tpu_custom_call" | custom-call | flops 1 | bytes 1 | tf_op jit(solution)/shard_map/input_gradient_kv/pallas_call | solution.py:623
  110.1 1.7 add_rows_with.3
  113.0 1.7 add_rows.15.rest_ref.a_ref
  114.7 1.7 add_rows.16
  117.1 1.7 add_rows.17.a_ref
  118.8 14.5 %collective-permute-done.23.got_ref.b_ref = f32[272,1024]{1,0:T(8,128)S(1)} collective-permute-done((f32[272,1024]{1,0:T(8,128)S(1)}, f32[272,1024]{1,0:T(8,128)S(1)}, u32[]{:S(2)}, u32[]{:S(2)}) %collective-permute-start.23) | collective-permute-done | bytes 1114144 | tf_op jit(solution)/shard_map/ppermute | solution.py:441
  133.4 3.1 %collective-permute-done.27.b_ref = f32[512,1024]{1,0:T(8,128)} collective-permute-done((f32[512,1024]{1,0:T(8,128)}, f32[512,1024]{1,0:T(8,128)}, u32[]{:S(2)}, u32[]{:S(2)}) %collective-permute-start.27) | collective-permute-done | bytes 2097184 | tf_op jit(solution)/shard_map/ppermute | solution.py:441
  136.5 1.7 add_rows.19
  138.2 1.3 collective-permute-start.29
  139.7 1.7 add_rows.20.a_ref
  141.4 3.1 %collective-permute-done.26.b_ref = f32[256,1024]{1,0:T(8,128)S(1)} collective-permute-done((f32[256,1024]{1,0:T(8,128)S(1)}, f32[256,1024]{1,0:T(8,128)S(1)}, u32[]{:S(2)}, u32[]{:S(2)}) %collective-permute-start.26) | collective-permute-done | bytes 1048608 | tf_op jit(solution)/shard_map/ppermute | solution.py:441
  144.7 10.1 %collective-permute-done.25.got_ref.b_ref = f32[144,1024]{1,0:T(8,128)S(1)} collective-permute-done((f32[144,1024]{1,0:T(8,128)S(1)}, f32[144,1024]{1,0:T(8,128)S(1)}, u32[]{:S(2)}, u32[]{:S(2)}) %collective-permute-start.25) | collective-permute-done | bytes 589856 | tf_op jit(solution)/shard_map/ppermute | solution.py:441
  155.9 1.7 collective-permute-start.28
  158.7 9.6 %collective-permute-done.30.b_ref = f32[128,1024]{1,0:T(8,128)S(1)} collective-permute-done((f32[128,1024]{1,0:T(8,128)S(1)}, f32[128,1024]{1,0:T(8,128)S(1)}, u32[]{:S(2)}, u32[]{:S(2)}) %collective-permute-start.30) | collective-permute-done | bytes 524320 | tf_op jit(solution)/shard_map/ppermute | solution.py:441
  168.4 5.0 %collective-permute-done.28.got_ref = f32[80,1024]{1,0:T(8,128)S(1)} collective-permute-done((f32[80,1024]{1,0:T(8,128)S(1)}, f32[80,1024]{1,0:T(8,128)S(1)}, u32[]{:S(2)}, u32[]{:S(2)}) %collective-permute-start.28) | collective-permute-done | bytes 327712 | tf_op jit(solution)/shard_map/ppermute | solution.py:441
  175.0 1.7 collective-permute-done.33
  178.1 11.6 %collective-permute-done.32 = f32[64,1024]{1,0:T(8,128)S(1)} collective-permute-done((f32[64,1024]{1,0:T(8,128)S(1)}, f32[64,1024]{1,0:T(8,128)S(1)}, u32[]{:S(2)}, u32[]{:S(2)}) %collective-permute-start.32) | collective-permute-done | bytes 262176 | tf_op jit(solution)/shard_map/ppermute | solution.py:441
  189.7 3.0 %collective-permute-done.34 = f32[64,1024]{1,0:T(8,128)S(1)} collective-permute-done((f32[64,1024]{1,0:T(8,128)S(1)}, f32[64,1024]{1,0:T(8,128)S(1)}, u32[]{:S(2)}, u32[]{:S(2)}) %collective-permute-start.34) | collective-permute-done | bytes 262176 | tf_op jit(solution)/shard_map/ppermute | solution.py:441
  (99 shorter events, 20.4 us)
Async XLA Ops:
  0.8 0.8 copy-start.10
  1.6 0.7 copy-start.12
  2.3 14.0 %copy-start.4 = (bf16[2048,1024]{1,0:T(8,128)(2,1)S(1)}, bf16[2048,1024]{1,0:T(8,128)(2,1)}, u32[]{:S(2)}) copy-start(bf16[2048,1024]{1,0:T(8,128)(2,1)} %w_ref.1) | copy-start | bytes 12582916
  13.6 6.7 %copy-start.7 = (f32[512,1024]{1,0:T(8,128)}, f32[512,1024]{1,0:T(8,128)S(1)}, u32[]{:S(2)}) copy-start(f32[512,1024]{1,0:T(8,128)S(1)} %get-tuple-element.168.slope_ref) | copy-start | bytes 6291460
  13.6 6.7 %collective-permute-start = (f32[2,128,128]{2,1,0:T(8,128)S(1)}, f32[2,128,128]{2,1,0:T(8,128)S(1)}, u32[]{:S(2)}, u32[]{:S(2)}) collective-permute-start(f32[2,128,128]{2,1,0:T(8,128)S(1)} %get-tuple-element.123), channel_id=1, source_target_pairs={{0,4},{4,0},{8,12},{12,8},{16,20},{20,16},{24,28},{28,24},{1,5},{5... | collective-permute-start | bytes 393224 | tf_op jit(solution)/shard_map/ppermute | solution.py:368
  13.9 6.5 %collective-permute-start.1 = (f32[2,128,128]{2,1,0:T(8,128)S(1)}, f32[2,128,128]{2,1,0:T(8,128)S(1)}, u32[]{:S(2)}, u32[]{:S(2)}) collective-permute-start(f32[2,128,128]{2,1,0:T(8,128)S(1)} %get-tuple-element.124), channel_id=1, source_target_pairs={{0,8},{4,12},{8,0},{12,4},{16,24},{20,28},{24,16},{28,20},{1,9},{5... | collective-permute-start | bytes 393224 | tf_op jit(solution)/shard_map/ppermute | solution.py:368
  13.9 7.5 %collective-permute-start.2 = (f32[2,128,128]{2,1,0:T(8,128)S(1)}, f32[2,128,128]{2,1,0:T(8,128)S(1)}, u32[]{:S(2)}, u32[]{:S(2)}) collective-permute-start(f32[2,128,128]{2,1,0:T(8,128)S(1)} %get-tuple-element.125), channel_id=1, source_target_pairs={{0,12},{4,8},{8,4},{12,0},{16,28},{20,24},{24,20},{28,16},{1,13},{... | collective-permute-start | bytes 393224 | tf_op jit(solution)/shard_map/ppermute | solution.py:368
  20.3 21.0 %copy-start.9 = (bf16[1,512,1024]{2,1,0:T(8,128)(2,1)S(1)}, bf16[1,512,1024]{2,1,0:T(8,128)(2,1)}, u32[]{:S(2)}) copy-start(bf16[1,512,1024]{2,1,0:T(8,128)(2,1)} %param.15) | copy-start | bytes 3145732
  20.3 21.0 %copy-start.11 = (f32[1024]{0:T(1024)S(1)}, f32[1024]{0:T(1024)}, u32[]{:S(2)}) copy-start(f32[1024]{0:T(1024)} %param.14) | copy-start | bytes 12292
  22.5 27.8 %collective-permute-start.10 = (f32[16,64,512]{2,1,0:T(8,128)S(1)}, f32[16,64,512]{2,1,0:T(8,128)S(1)}, u32[]{:S(2)}, u32[]{:S(2)}) collective-permute-start(f32[16,64,512]{2,1,0:T(8,128)S(1)} %get-tuple-element.149), channel_id=1, source_target_pairs={{0,1},{1,0},{2,3},{3,2},{4,5},{5,4},{6,7},{7,6},{8,9},{9,8},{10,11... | collective-permute-start | bytes 6291464 | tf_op jit(solution)/shard_map/ppermute | solution.py:441
  24.7 8.8 %collective-permute-start.3 = (f32[2,128,128]{2,1,0:T(8,128)S(1)}, f32[2,128,128]{2,1,0:T(8,128)S(1)}, u32[]{:S(2)}, u32[]{:S(2)}) collective-permute-start(f32[2,128,128]{2,1,0:T(8,128)S(1)} %add_add_fusion.1), channel_id=1, source_target_pairs={{0,24},{4,28},{8,16},{12,20},{1,25},{5,29},{9,17},{13,21},{2,26},{... | collective-permute-start | bytes 393224 | tf_op jit(solution)/shard_map/ppermute | solution.py:422
  33.8 3.9 %collective-permute-start.4 = (f32[2,128,128]{2,1,0:T(8,128)S(1)}, f32[2,128,128]{2,1,0:T(8,128)S(1)}, u32[]{:S(2)}, u32[]{:S(2)}) collective-permute-start(f32[2,128,128]{2,1,0:T(8,128)S(1)} %get-tuple-element.134), channel_id=1, source_target_pairs={{0,4},{4,0},{8,12},{12,8},{16,20},{20,16},{24,28},{28,24},{1,5},{5... | collective-permute-start | bytes 393224 | tf_op jit(solution)/shard_map/ppermute | solution.py:368
  34.1 4.1 %collective-permute-start.5 = (f32[2,128,128]{2,1,0:T(8,128)S(1)}, f32[2,128,128]{2,1,0:T(8,128)S(1)}, u32[]{:S(2)}, u32[]{:S(2)}) collective-permute-start(f32[2,128,128]{2,1,0:T(8,128)S(1)} %get-tuple-element.135), channel_id=1, source_target_pairs={{0,8},{4,12},{8,0},{12,4},{16,24},{20,28},{24,16},{28,20},{1,9},{5... | collective-permute-start | bytes 393224 | tf_op jit(solution)/shard_map/ppermute | solution.py:368
  34.1 7.2 %collective-permute-start.6 = (f32[2,128,128]{2,1,0:T(8,128)S(1)}, f32[2,128,128]{2,1,0:T(8,128)S(1)}, u32[]{:S(2)}, u32[]{:S(2)}) collective-permute-start(f32[2,128,128]{2,1,0:T(8,128)S(1)} %get-tuple-element.136), channel_id=1, source_target_pairs={{0,12},{4,8},{8,4},{12,0},{16,28},{20,24},{24,20},{28,16},{1,13},{... | collective-permute-start | bytes 393224 | tf_op jit(solution)/shard_map/ppermute | solution.py:368
  47.2 12.2 %collective-permute-start.12 = (f32[512,512]{1,0:T(8,128)S(1)}, f32[512,512]{1,0:T(8,128)S(1)}, u32[]{:S(2)}, u32[]{:S(2)}) collective-permute-start(f32[512,512]{1,0:T(8,128)S(1)} %get-tuple-element.154), channel_id=1, source_target_pairs={{0,1},{1,0},{2,3},{3,2},{4,5},{5,4},{6,7},{7,6},{8,9},{9,8},{10,11... | collective-permute-start | bytes 3145736 | tf_op jit(solution)/shard_map/ppermute | solution.py:441
  49.8 9.7 %collective-permute-start.13 = (f32[512,512]{1,0:T(8,128)S(1)}, f32[512,512]{1,0:T(8,128)S(1)}, u32[]{:S(2)}, u32[]{:S(2)}) collective-permute-start(f32[512,512]{1,0:T(8,128)S(1)} %get-tuple-element.155), channel_id=1, source_target_pairs={{0,1},{1,0},{2,3},{3,2},{4,5},{5,4},{6,7},{7,6},{8,9},{9,8},{10,11... | collective-permute-start | bytes 3145736 | tf_op jit(solution)/shard_map/ppermute | solution.py:441
  49.8 4.6 %collective-permute-start.7 = (f32[2,128,128]{2,1,0:T(8,128)S(1)}, f32[2,128,128]{2,1,0:T(8,128)S(1)}, u32[]{:S(2)}, u32[]{:S(2)}) collective-permute-start(f32[2,128,128]{2,1,0:T(8,128)S(1)} %get-tuple-element.146), channel_id=1, source_target_pairs={{0,4},{4,0},{8,12},{12,8},{16,20},{20,16},{24,28},{28,24},{1,5},{5... | collective-permute-start | bytes 393224 | tf_op jit(solution)/shard_map/ppermute | solution.py:368
  50.1 4.4 %collective-permute-start.8 = (f32[2,128,128]{2,1,0:T(8,128)S(1)}, f32[2,128,128]{2,1,0:T(8,128)S(1)}, u32[]{:S(2)}, u32[]{:S(2)}) collective-permute-start(f32[2,128,128]{2,1,0:T(8,128)S(1)} %get-tuple-element.147), channel_id=1, source_target_pairs={{0,8},{4,12},{8,0},{12,4},{16,24},{20,28},{24,16},{28,20},{1,9},{5... | collective-permute-start | bytes 393224 | tf_op jit(solution)/shard_map/ppermute | solution.py:368
  50.3 7.9 %collective-permute-start.9 = (f32[2,128,128]{2,1,0:T(8,128)S(1)}, f32[2,128,128]{2,1,0:T(8,128)S(1)}, u32[]{:S(2)}, u32[]{:S(2)}) collective-permute-start(f32[2,128,128]{2,1,0:T(8,128)S(1)} %get-tuple-element.148), channel_id=1, source_target_pairs={{0,12},{4,8},{8,4},{12,0},{16,28},{20,24},{24,20},{28,16},{1,13},{... | collective-permute-start | bytes 393224 | tf_op jit(solution)/shard_map/ppermute | solution.py:368
  58.2 10.0 %collective-permute-start.11 = (f32[2,128,128]{2,1,0:T(8,128)S(1)}, f32[2,128,128]{2,1,0:T(8,128)S(1)}, u32[]{:S(2)}, u32[]{:S(2)}) collective-permute-start(f32[2,128,128]{2,1,0:T(8,128)S(1)} %add_add_fusion), channel_id=1, source_target_pairs={{28,4},{24,0},{20,12},{16,8},{29,5},{25,1},{21,13},{17,9},{30,6},{... | collective-permute-start | bytes 393224 | tf_op jit(solution)/shard_map/ppermute | solution.py:422
  68.6 6.8 %collective-permute-start.14 = (f32[2,128,128]{2,1,0:T(8,128)S(1)}, f32[2,128,128]{2,1,0:T(8,128)S(1)}, u32[]{:S(2)}, u32[]{:S(2)}) collective-permute-start(f32[2,128,128]{2,1,0:T(8,128)S(1)} %get-tuple-element.169), channel_id=1, source_target_pairs={{0,4},{4,0},{8,12},{12,8},{16,20},{20,16},{24,28},{28,24},{1,5},{5... | collective-permute-start | bytes 393224 | tf_op jit(solution)/shard_map/ppermute | solution.py:368
  68.6 6.7 %collective-permute-start.15 = (f32[2,128,128]{2,1,0:T(8,128)S(1)}, f32[2,128,128]{2,1,0:T(8,128)S(1)}, u32[]{:S(2)}, u32[]{:S(2)}) collective-permute-start(f32[2,128,128]{2,1,0:T(8,128)S(1)} %get-tuple-element.170), channel_id=1, source_target_pairs={{0,8},{4,12},{8,0},{12,4},{16,24},{20,28},{24,16},{28,20},{1,9},{5... | collective-permute-start | bytes 393224 | tf_op jit(solution)/shard_map/ppermute | solution.py:368
  68.7 7.4 %collective-permute-start.16 = (f32[2,128,128]{2,1,0:T(8,128)S(1)}, f32[2,128,128]{2,1,0:T(8,128)S(1)}, u32[]{:S(2)}, u32[]{:S(2)}) collective-permute-start(f32[2,128,128]{2,1,0:T(8,128)S(1)} %get-tuple-element.171), channel_id=1, source_target_pairs={{0,12},{4,8},{8,4},{12,0},{16,28},{20,24},{24,20},{28,16},{1,13},{... | collective-permute-start | bytes 393224 | tf_op jit(solution)/shard_map/ppermute | solution.py:368
  71.3 38.8 %collective-permute-start.21 = (f32[512,1024]{1,0:T(8,128)}, f32[512,1024]{1,0:T(8,128)}, u32[]{:S(2)}, u32[]{:S(2)}) collective-permute-start(f32[512,1024]{1,0:T(8,128)} %weight_q.1), channel_id=1, source_target_pairs={{0,2},{1,9},{2,0},{3,11},{4,6},{5,13},{6,4},{7,15},{8,10},{9,1},{1... | collective-permute-start | bytes 6291464 | tf_op jit(solution)/shard_map/ppermute | solution.py:441
  71.3 4.8 %copy-start.8 = (f32[512,1024]{1,0:T(8,128)S(1)}, f32[512,1024]{1,0:T(8,128)}, u32[]{:S(2)}) copy-start(f32[512,1024]{1,0:T(8,128)} %copy-done.7) | copy-start | bytes 6291460
  78.0 6.5 %collective-permute-start.19 = (f32[512,512]{1,0:T(8,128)S(1)}, f32[512,512]{1,0:T(8,128)S(1)}, u32[]{:S(2)}, u32[]{:S(2)}) collective-permute-start(f32[512,512]{1,0:T(8,128)S(1)} %get-tuple-element.179), channel_id=1, source_target_pairs={{0,1},{1,0},{2,3},{3,2},{4,5},{5,4},{6,7},{7,6},{8,9},{9,8},{10,11... | collective-permute-start | bytes 3145736 | tf_op jit(solution)/shard_map/ppermute | solution.py:441
  82.2 3.8 %collective-permute-start.20 = (f32[512,512]{1,0:T(8,128)S(1)}, f32[512,512]{1,0:T(8,128)S(1)}, u32[]{:S(2)}, u32[]{:S(2)}) collective-permute-start(f32[512,512]{1,0:T(8,128)S(1)} %get-tuple-element.180), channel_id=1, source_target_pairs={{0,1},{1,0},{2,3},{3,2},{4,5},{5,4},{6,7},{7,6},{8,9},{9,8},{10,11... | collective-permute-start | bytes 3145736 | tf_op jit(solution)/shard_map/ppermute | solution.py:441
  82.3 7.9 %collective-permute-start.17 = (f32[512,512]{1,0:T(8,128)S(1)}, f32[512,512]{1,0:T(8,128)S(1)}, u32[]{:S(2)}, u32[]{:S(2)}) collective-permute-start(f32[512,512]{1,0:T(8,128)S(1)} %get-tuple-element.177), channel_id=1, source_target_pairs={{0,1},{1,0},{2,3},{3,2},{4,5},{5,4},{6,7},{7,6},{8,9},{9,8},{10,11... | collective-permute-start | bytes 3145736 | tf_op jit(solution)/shard_map/ppermute | solution.py:441
  82.7 7.4 %collective-permute-start.18 = (f32[512,512]{1,0:T(8,128)S(1)}, f32[512,512]{1,0:T(8,128)S(1)}, u32[]{:S(2)}, u32[]{:S(2)}) collective-permute-start(f32[512,512]{1,0:T(8,128)S(1)} %get-tuple-element.178), channel_id=1, source_target_pairs={{0,1},{1,0},{2,3},{3,2},{4,5},{5,4},{6,7},{7,6},{8,9},{9,8},{10,11... | collective-permute-start | bytes 3145736 | tf_op jit(solution)/shard_map/ppermute | solution.py:441
  88.6 26.1 %collective-permute-start.24 = (f32[512,1024]{1,0:T(8,128)}, f32[512,1024]{1,0:T(8,128)}, u32[]{:S(2)}, u32[]{:S(2)}) collective-permute-start(f32[512,1024]{1,0:T(8,128)} %weight_k.1), channel_id=1, source_target_pairs={{0,2},{1,5},{2,0},{3,7},{4,6},{5,1},{6,4},{7,3},{8,10},{9,13},{10,... | collective-permute-start | bytes 6291464 | tf_op jit(solution)/shard_map/ppermute | solution.py:441
  90.1 2.7 %copy-start.2 = (f32[512,1024]{1,0:T(8,128)}, f32[512,1024]{1,0:T(8,128)S(1)}, u32[]{:S(2)}) copy-start(f32[512,1024]{1,0:T(8,128)S(1)} %weight_k_kept.1.a_ref) | copy-start | bytes 6291460
  90.2 6.5 %copy-start.6 = (bf16[2048,1024]{1,0:T(8,128)(2,1)S(1)}, bf16[2048,1024]{1,0:T(8,128)(2,1)}, u32[]{:S(2)}) copy-start(bf16[2048,1024]{1,0:T(8,128)(2,1)} %wb_ref.1) | copy-start | bytes 12582916
  92.8 3.8 %copy-start.5 = (bf16[2048,1024]{1,0:T(8,128)(2,1)S(1)}, bf16[2048,1024]{1,0:T(8,128)(2,1)}, u32[]{:S(2)}) copy-start(bf16[2048,1024]{1,0:T(8,128)(2,1)} %wa_ref.1) | copy-start | bytes 12582916
  92.8 43.7 %collective-permute-start.27 = (f32[512,1024]{1,0:T(8,128)}, f32[512,1024]{1,0:T(8,128)}, u32[]{:S(2)}, u32[]{:S(2)}) collective-permute-start(f32[512,1024]{1,0:T(8,128)} %weight_v.1), channel_id=1, source_target_pairs={{0,8},{1,5},{2,10},{3,7},{4,12},{5,1},{6,14},{7,3},{8,0},{9,13},{1... | collective-permute-start | bytes 6291464 | tf_op jit(solution)/shard_map/ppermute | solution.py:441
  95.3 1.3 copy-start
  108.7 1.4 collective-permute-start.22
  111.8 2.9 %copy-start.3 = (f32[512,1024]{1,0:T(8,128)S(1)}, f32[512,1024]{1,0:T(8,128)}, u32[]{:S(2)}) copy-start(f32[512,1024]{1,0:T(8,128)} %copy-done.2) | copy-start | bytes 6291460
  111.8 21.5 %collective-permute-start.23 = (f32[272,1024]{1,0:T(8,128)S(1)}, f32[272,1024]{1,0:T(8,128)S(1)}, u32[]{:S(2)}, u32[]{:S(2)}) collective-permute-start(f32[272,1024]{1,0:T(8,128)S(1)} %get-tuple-element.195), channel_id=1, source_target_pairs={{0,8},{1,3},{2,10},{3,1},{4,12},{5,7},{6,14},{7,5},{8,0},{9,11},{1... | collective-permute-start | bytes 3342344 | tf_op jit(solution)/shard_map/ppermute | solution.py:441
  116.4 28.1 %collective-permute-start.26 = (f32[256,1024]{1,0:T(8,128)S(1)}, f32[256,1024]{1,0:T(8,128)S(1)}, u32[]{:S(2)}, u32[]{:S(2)}) collective-permute-start(f32[256,1024]{1,0:T(8,128)S(1)} %add_rows.16), channel_id=1, source_target_pairs={{0,8},{1,3},{2,10},{3,1},{4,12},{5,7},{6,14},{7,5},{8,0},{9,11},{1... | collective-permute-start | bytes 3145736 | tf_op jit(solution)/shard_map/ppermute | solution.py:441
  133.3 3.2 %copy-start.1 = (f32[512,1024]{1,0:T(8,128)S(1)}, f32[512,1024]{1,0:T(8,128)}, u32[]{:S(2)}) copy-start(f32[512,1024]{1,0:T(8,128)} %copy-done) | copy-start | bytes 6291460
  138.2 17.6 %collective-permute-start.29 = (f32[256,1024]{1,0:T(8,128)S(1)}, f32[256,1024]{1,0:T(8,128)S(1)}, u32[]{:S(2)}, u32[]{:S(2)}) collective-permute-start(f32[256,1024]{1,0:T(8,128)S(1)} %add_rows.19), channel_id=1, source_target_pairs={{0,4},{1,3},{2,6},{3,1},{4,0},{5,7},{6,2},{7,5},{8,12},{9,11},{10,... | collective-permute-start | bytes 3145736 | tf_op jit(solution)/shard_map/ppermute | solution.py:441
  139.5 15.4 %collective-permute-start.25 = (f32[144,1024]{1,0:T(8,128)S(1)}, f32[144,1024]{1,0:T(8,128)S(1)}, u32[]{:S(2)}, u32[]{:S(2)}) collective-permute-start(f32[144,1024]{1,0:T(8,128)S(1)} %get-tuple-element.201), channel_id=1, source_target_pairs={{0,24},{1,5},{2,26},{3,7},{4,28},{5,1},{6,30},{7,3},{8,16},{9,13},... | collective-permute-start | bytes 1769480 | tf_op jit(solution)/shard_map/ppermute | solution.py:441
  144.6 14.1 %collective-permute-start.31 = (f32[128,1024]{1,0:T(8,128)S(1)}, f32[128,1024]{1,0:T(8,128)S(1)}, u32[]{:S(2)}, u32[]{:S(2)}) collective-permute-start(f32[128,1024]{1,0:T(8,128)S(1)} %add_rows.21), channel_id=1, source_target_pairs={{0,24},{1,9},{2,26},{3,11},{4,28},{5,13},{6,30},{7,15},{8,16},{9,1... | collective-permute-start | bytes 1572872 | tf_op jit(solution)/shard_map/ppermute | solution.py:441
  155.8 12.5 %collective-permute-start.30 = (f32[128,1024]{1,0:T(8,128)S(1)}, f32[128,1024]{1,0:T(8,128)S(1)}, u32[]{:S(2)}, u32[]{:S(2)}) collective-permute-start(f32[128,1024]{1,0:T(8,128)S(1)} %add_rows.24), channel_id=1, source_target_pairs={{0,2},{1,9},{2,0},{3,11},{4,6},{5,13},{6,4},{7,15},{8,10},{9,1},{1... | collective-permute-start | bytes 1572872 | tf_op jit(solution)/shard_map/ppermute | solution.py:441
  155.9 17.5 %collective-permute-start.28 = (f32[80,1024]{1,0:T(8,128)S(1)}, f32[80,1024]{1,0:T(8,128)S(1)}, u32[]{:S(2)}, u32[]{:S(2)}) collective-permute-start(f32[80,1024]{1,0:T(8,128)S(1)} %get-tuple-element.209), channel_id=1, source_target_pairs={{0,4},{1,25},{2,6},{3,27},{4,0},{5,29},{6,2},{7,31},{8,12},{9,17},... | collective-permute-start | bytes 983048 | tf_op jit(solution)/shard_map/ppermute | solution.py:441
  173.4 3.4 %collective-permute-start.33 = (f32[16,1024]{1,0:T(8,128)S(1)}, f32[16,1024]{1,0:T(8,128)S(1)}, u32[]{:S(2)}, u32[]{:S(2)}) collective-permute-start(f32[16,1024]{1,0:T(8,128)S(1)} %get-tuple-element.220), channel_id=1, source_target_pairs={{0,2},{1,9},{2,0},{3,11},{4,6},{5,13},{6,4},{7,15},{8,10},{9,1},{1... | collective-permute-start | bytes 196616 | tf_op jit(solution)/shard_map/ppermute | solution.py:441
  173.5 16.2 %collective-permute-start.32 = (f32[64,1024]{1,0:T(8,128)S(1)}, f32[64,1024]{1,0:T(8,128)S(1)}, u32[]{:S(2)}, u32[]{:S(2)}) collective-permute-start(f32[64,1024]{1,0:T(8,128)S(1)} %add_rows.26), channel_id=1, source_target_pairs={{0,4},{1,25},{2,6},{3,27},{4,0},{5,29},{6,2},{7,31},{8,12},{9,17},... | collective-permute-start | bytes 786440 | tf_op jit(solution)/shard_map/ppermute | solution.py:441
  174.2 18.6 %collective-permute-start.34 = (f32[64,1024]{1,0:T(8,128)S(1)}, f32[64,1024]{1,0:T(8,128)S(1)}, u32[]{:S(2)}, u32[]{:S(2)}) collective-permute-start(f32[64,1024]{1,0:T(8,128)S(1)} %add_rows.28), channel_id=1, source_target_pairs={{0,24},{1,25},{2,26},{3,27},{4,28},{5,29},{6,30},{7,31},{8,16},{9,... | collective-permute-start | bytes 786440 | tf_op jit(solution)/shard_map/ppermute | solution.py:441

commit v4 on v3

--- a/solution.py
+++ b/solution.py
@@ -98,56 +98,59 @@
 
 
 def embed_kernel(
-    slots, ids_hbm, proj_hbm, resid_hbm, wk_hbm, wv_hbm,
+    slots, packed_ref, resid_hbm, wk_hbm, wv_hbm,
     x_ref, codes_ref, k_ref, slope_ref, v_ref, kv_ref, *rest,
 ):
-    pieces = rest[:-6]
-    ids_ref, proj_ref, resid_ref, wk_ref, wv_ref, sems = rest[-6:]
+    pieces = rest[:-4]
+    resid_ref, wk_ref, wv_ref, sems = rest[-4:]
     t, d = x_ref.shape
     hd = k_ref.shape[1]
     half = hd // 2
-    moves = [(ids_hbm, ids_ref), (proj_hbm, proj_ref), (resid_hbm, resid_ref)]
-    for c in range(2):
-        at = pl.ds(c * half, half)
-        moves += [(wk_hbm.at[:, at], wk_ref.at[:, at]), (wv_hbm.at[:, at], wv_ref.at[:, at])]
+    moves = [(resid_hbm, resid_ref)]
+    for hbm, ref in ((wk_hbm, wk_ref), (wv_hbm, wv_ref)):
+        for r in range(2):
+            at = pl.ds(r * (d // 2), d // 2)
+            moves.append((hbm.at[at], ref.at[at]))
     incoming = [pltpu.make_async_copy(hbm, ref, sems.at[i]) for i, (hbm, ref) in enumerate(moves)]
     for copy in incoming:
         copy.start()
-    incoming[0].wait()
-    ids = ids_ref[...]
+    count = len(fsq_levels)
+    ids = packed_ref[count : count + 1, :t].astype(jnp.int32)
     code_list = []
     for fsq_level, fsq_base in zip(fsq_levels, fsq_bases):
         digit = lax.rem(lax.div(ids, fsq_base), fsq_level)
         code_list.append((2.0 * digit.astype(F32) - (fsq_level - 1)) / (fsq_level - 1))
-    count = len(code_list)
     for _ in range(codes_ref.shape[0] - count):
         code_list.append(jnp.zeros_like(code_list[0]))
     codes = jnp.concatenate(code_list, axis=0)
     codes_ref[...] = codes
     turned = jnp.transpose(codes)
-    incoming[1].wait()
-    incoming[2].wait()
+    incoming[0].wait()
     step = 64
     for r in range(0, t, step):
         summed = resid_ref[r : r + step].astype(F32)
         for index in range(count):
-            summed = summed + turned[r : r + step, index : index + 1] * proj_ref[index : index + 1]
+            summed = summed + turned[r : r + step, index : index + 1] * packed_ref[index : index + 1]
         x_ref[r : r + step] = summed.astype(BF16)
     x = x_ref[...]
+    incoming[1].wait()
+    incoming[2].wait()
     for c in range(2):
         at = slice(c * half, (c + 1) * half)
-        incoming[3 + 2 * c].wait()
         key, slope = silu_and_slope(mm(x, wk_ref[:, at]))
-        key = key.astype(BF16)
-        k_ref[:, at] = key
+        k_ref[:, at] = key.astype(BF16)
         slope_ref[:, at] = slope
-        incoming[4 + 2 * c].wait()
+    incoming[3].wait()
+    incoming[4].wait()
+    for c in range(2):
+        at = slice(c * half, (c + 1) * half)
         value = mm(x, wv_ref[:, at]).astype(BF16)
         v_ref[:, at] = value
         for h in range(half // DH):
+            which = c * (half // DH) + h
             for p in range(PARTS):
                 rows = part_rows(t, p)
-                kv_ref[p, c * (half // DH) + h] = mm_tn(key[rows, head(h)], value[rows, head(h)])
+                kv_ref[p, which] = mm_tn(k_ref[rows, head(which)], value[rows, head(h)])
     hand_out(slots[0], kv_ref, pieces)
 
 
@@ -155,9 +158,11 @@
     t, d = resid.shape
     hd = w_key.shape[1]
     heads = hd // DH
+    ids = jnp.pad(token_ids.astype(F32), ((0, 0), (0, d - t)))
+    packed = jnp.concatenate([code_proj, ids], axis=0)
     return pl.pallas_call(
         embed_kernel,
-        in_specs=[SMEM] + [HBM] * 5,
+        in_specs=[SMEM, VMEM] + [HBM] * 3,
         out_specs=[VMEM] * (6 + group),
         out_shape=[
             shape((t, d), BF16),
@@ -169,17 +174,15 @@
         ]
         + [shape((heads // group, DH, DH), F32)] * group,
         scratch_shapes=[
-            pltpu.VMEM(token_ids.shape, jnp.int32),
-            pltpu.VMEM(code_proj.shape, F32),
             pltpu.VMEM((t, d), BF16),
             pltpu.VMEM((d, hd), BF16),
             pltpu.VMEM((d, hd), BF16),
-            pltpu.SemaphoreType.DMA((7,)),
+            pltpu.SemaphoreType.DMA((5,)),
         ],
         compiler_params=params(EMBED_MIB * MIB),
         cost_estimate=cost(4 * t * d * hd, 4 * d * hd + 10 * t * hd),
         name="embed_keys_values",
-    )(slots, token_ids, code_proj, resid, w_key, w_value)
+    )(slots, packed, resid, w_key, w_value)
 
 
 def causal_mask(t, transposed):
@@ -268,7 +271,7 @@
 
 
 def dquery_kernel(slots, datt_ref, v_ref, k_ref, kv_ref, slope_ref, *rest):
-    prefixes, (g16_ref, *wide, state_ref) = rest[: -2 - SHARES], rest[-2 - SHARES :]
+    prefixes, (g16_ref, state_ref) = rest[:-2], rest[-2:]
     take_in(slots[0], prefixes, state_ref)
     t, hd = datt_ref.shape
     mask = causal_mask(t // PARTS, False)
@@ -284,16 +287,27 @@
             d_query = mm(back, k_ref[rows, at]) + mm_nt(d_att, state.astype(BF16))
             grad = (d_query * slope_ref[rows, at]).astype(BF16)
             g16_ref[rows, at] = grad
-            store_wide(wide, rows, h, grad)
 
 
 def query_gradient(slots, d_att, values, keys, prefixes, part_kv, slope):
     t, hd = d_att.shape
     return in_vmem(
         dquery_kernel, [slots], [d_att, values, keys, part_kv, slope, *prefixes],
-        [shape((t, hd), BF16)] + [shape((t, hd // SHARES), F32)] * SHARES, [pltpu.VMEM((hd // DH, DH, DH), F32)],
+        [shape((t, hd), BF16)], [pltpu.VMEM((hd // DH, DH, DH), F32)],
         cost(2 * t * t * hd, 16 * t * hd), "query_gradient",
-    )
+    )[0]
+
+
+def widen_kernel(grad_ref, *wide):
+    width = wide[0].shape[1]
+    for index, ref in enumerate(wide):
+        ref[...] = grad_ref[:, index * width : (index + 1) * width].astype(F32)
+
+
+def widen(grad):
+    t, hd = grad.shape
+    outs = [shape((t, hd // SHARES), F32)] * SHARES
+    return in_vmem(widen_kernel, [], [grad], outs, [], cost(0, 0), "widen")
 
 
 def within_kernel(datt_ref, v_ref, k_ref, q_ref, dk_ref, dv_ref):
@@ -650,10 +664,10 @@
     before.first(pieces)
     queries, query_slope, within = queries_scores(x, w_query, keys, values)
     order.mark(within)
-    before.second(order)
     own_rows, other_rows = turn(me, order.tied(x), total // 2)
     order.mark(own_rows)
-    other_rows = both_exchange(other_rows, (1, 1))
+    before.second(order)
+    other_rows = both_exchange(order.tied(other_rows), (1, 1))
     before.third(order)
     prefixes = before.result(order)
 
@@ -662,12 +676,16 @@
     )
     order.mark(d_att)
     after.first(pieces)
-    grad_q, *wide_q = query_gradient(slots, order.tied(d_att), values, keys, prefixes, part_kv, query_slope)
+    grad_q = query_gradient(slots, order.tied(d_att), values, keys, prefixes, part_kv, query_slope)
     order.mark(grad_q)
-    wide_q = [both_exchange(share, (1, 1)) for share in wide_q]
     merged = merge(own_rows, order.tied(other_rows))
     order.mark(merged)
     after.second(order)
+    wide_q = widen(order.tied(grad_q))
+    order.mark(wide_q[0])
+    wide_q = [both_exchange(share, (1, 1)) for share in wide_q]
+    dk, dv = within_block(order.tied(d_att), values, keys, queries)
+    order.mark(dk)
 
     bits = total.bit_length() - 1
     masks = [1 << b for b in range(1, bits)]
@@ -702,8 +720,6 @@
             chunk.rest = array
 
     begin(chunks_q, grad_q, wide_q, "weight_q")
-    dk, dv = within_block(order.tied(d_att), values, keys, queries)
-    order.mark(dk)
     after.third(order)
     input_grad = first_input_gradient(order.tied(grad_q), w_query)
     order.mark(input_grad)

time: 195 us -> 190 us (0.974)
  waiting for transfers between devices: 87.6 us -> 82.5 us
    ppermute x12, waiting for transfers between devices: 12.1 us -> 6.65 us  [exchange(): return lax.ppermute(array, axis, [(i, i ^ mask) for i in range(count)])]
    pallas_call x34 -> x35, Pallas kernels: 38.7 us -> 38.8 us  [in_vmem(): pl.pallas_call(kernel, in_specs=[SMEM] * len(slots) + [VMEM] * len(inputs...]
  transfers between devices with their start and end apart: 35 -> 35, of which waited for: 23 -> 21; matrix products, arithmetic and copies ran while one was open for 1% -> 1% of each run, Pallas kernels for 27% -> 29%
where the time goes in v4:
time: 190 us; the launch traced here: 189 us
  waiting for transfers between devices  82.5 us (43%)
  Pallas kernels  65.5 us (34%)
  starting transfers between devices  34.7 us (18%)
  other arithmetic  2.7 us (1%)
  local copies, waits for them, and re-layouts  2.62 us (1%)
    ppermute x21, waiting for transfers between devices, both_exchange(): lax.ppermute(array, AXES, [(i, i ^ masks[i % 2]) for i in range(total)])  68.2 us
    pallas_call x35, Pallas kernels, in_vmem(): pl.pallas_call(kernel, in_specs=[SMEM] * len(slots) + [VMEM] * len(inputs...  38.8 us
    ppermute x21, starting transfers between devices, both_exchange(): lax.ppermute(array, AXES, [(i, i ^ masks[i % 2]) for i in range(total)])  19.4 us
    pallas_call x1, Pallas kernels, rest_input_gradient(): pl.pallas_call(rest_input_kernel, grid=(d // WIDE,), in_specs=[out_column...  12 us
    ppermute x12, starting transfers between devices, exchange(): return lax.ppermute(array, axis, [(i, i ^ mask) for i in range(count)])  10.9 us
    pallas_call x1, Pallas kernels, embed_keys_values(): pl.pallas_call(embed_kernel, in_specs=[SMEM, VMEM] + [HBM] * 3, out_specs...  10.7 us
    ppermute x2, waiting for transfers between devices, second(): self.bases.append(lax.ppermute(total, 'seq', pairs))  7.69 us
    ppermute x12, waiting for transfers between devices, exchange(): return lax.ppermute(array, axis, [(i, i ^ mask) for i in range(count)])  6.65 us
  transfers between devices with their start and end apart: 35, of which 21 were waited for; matrix products, arithmetic and copies ran while one was open for 1% of the time, Pallas kernels for 29%

profile of v4, /device:TPU:13, one launch (start us, length us, event | category | flops | bytes accessed | tf_op | source)
XLA Modules:
  0.0 189.2 jit_solution(10899148110155581188)
XLA Ops:
  2.3 10.7 %embed_keys_values.1 = (bf16[512,2048]{1,0:T(8,128)(2,1)S(1)}, f32[8,512]{1,0:T(8,128)S(1)}, bf16[512,1024]{1,0:T(8,128)(2,1)S(1)}, f32[512,1024]{1,0:T(8,128)S(...) custom-call(s32[2]{0:T(128)S(1)} %pad_add_fusion.slots, ...), custom_call_target="tpu_custom_call" | custom-call | flops 1 | bytes 1 | tf_op jit(solution)/shard_map/embed_keys_values/pallas_call | solution.py:163
  13.3 2.4 %collective-permute-start.2 = (f32[2,128,128]{2,1,0:T(8,128)S(1)}, f32[2,128,128]{2,1,0:T(8,128)S(1)}, u32[]{:S(2)}, u32[]{:S(2)}) collective-permute-start(f32[2,128,128]{2,1,0:T(8,128)S(1)} %get-tuple-element.126), channel_id=1, source_target_pairs={{0,12},{4,8},{8,4},{12,0},{16,28},{20,24},{24,20},{28,16},{1,13},{... | collective-permute-start | bytes 393224 | tf_op jit(solution)/shard_map/ppermute | solution.py:382
  15.7 4.0 %queries_scores.1 = (bf16[512,1024]{1,0:T(8,128)(2,1)S(1)}, f32[512,1024]{1,0:T(8,128)S(1)}, f32[512,1024]{1,0:T(8,128)S(1)}) custom-call(bf16[512,2048]{1,0:T(8,128)(2,1)S(1)} %get-tuple-element.128.x_ref, bf16[2048,1024]{1,0:T(8,128)(2,1)S(1)} %copy-done.4, bf16[512,1024]{1,0:T(8,128)(2,1)S(1)} %get-tuple-element.117.k_ref, ...), custom_call_target="tpu_custom_call" | custom-call | flops 1 | bytes 1 | tf_op jit(solution)/shard_map/queries_scores/pallas_call | solution.py:88
  20.9 2.2 %collective-permute-start.10 = (f32[16,64,512]{2,1,0:T(8,128)S(1)}, f32[16,64,512]{2,1,0:T(8,128)S(1)}, u32[]{:S(2)}, u32[]{:S(2)}) collective-permute-start(f32[16,64,512]{2,1,0:T(8,128)S(1)} %get-tuple-element.150), channel_id=1, source_target_pairs={{0,1},{1,0},{2,3},{3,2},{4,5},{5,4},{6,7},{7,6},{8,9},{9,8},{10,11... | collective-permute-start | bytes 6291464 | tf_op jit(solution)/shard_map/ppermute | solution.py:455
  23.1 3.2 %collective-permute-start.3 = (f32[2,128,128]{2,1,0:T(8,128)S(1)}, f32[2,128,128]{2,1,0:T(8,128)S(1)}, u32[]{:S(2)}, u32[]{:S(2)}) collective-permute-start(f32[2,128,128]{2,1,0:T(8,128)S(1)} %add_add_fusion.1), channel_id=1, source_target_pairs={{0,24},{4,28},{8,16},{12,20},{1,25},{5,29},{9,17},{13,21},{2,26},{... | collective-permute-start | bytes 393224 | tf_op jit(solution)/shard_map/ppermute | solution.py:436
  26.3 5.5 %collective-permute-done.3.base_ref = f32[2,128,128]{2,1,0:T(8,128)S(1)} collective-permute-done((f32[2,128,128]{2,1,0:T(8,128)S(1)}, f32[2,128,128]{2,1,0:T(8,128)S(1)}, u32[]{:S(2)}, u32[]{:S(2)}) %collective-permute-start.3) | collective-permute-done | bytes 131104 | tf_op jit(solution)/shard_map/ppermute | solution.py:436
  32.5 2.4 %collective-permute-start.6 = (f32[2,128,128]{2,1,0:T(8,128)S(1)}, f32[2,128,128]{2,1,0:T(8,128)S(1)}, u32[]{:S(2)}, u32[]{:S(2)}) collective-permute-start(f32[2,128,128]{2,1,0:T(8,128)S(1)} %get-tuple-element.137), channel_id=1, source_target_pairs={{0,12},{4,8},{8,4},{12,0},{16,28},{20,24},{24,20},{28,16},{1,13},{... | collective-permute-start | bytes 393224 | tf_op jit(solution)/shard_map/ppermute | solution.py:382
  34.9 1.2 collective-permute-done.4.rest_1_
  36.6 3.1 %collective-permute-done.6.rest_3_ = f32[2,128,128]{2,1,0:T(8,128)S(1)} collective-permute-done((f32[2,128,128]{2,1,0:T(8,128)S(1)}, f32[2,128,128]{2,1,0:T(8,128)S(1)}, u32[]{:S(2)}, u32[]{:S(2)}) %collective-permute-start.6) | collective-permute-done | bytes 131104 | tf_op jit(solution)/shard_map/ppermute | solution.py:382
  39.7 3.3 %norm_gradient.1 = (bf16[512,1024]{1,0:T(8,128)(2,1)S(1)}, f32[1,1024]{1,0:T(1,128)S(1)}, f32[2,8,128,128]{3,2,1,0:T(8,128)S(1)}, f32[2,128,128]{2,1,0:T(8,128)S...) custom-call(s32[2]{0:T(128)S(1)} %pad_add_fusion.slots, ...), custom_call_target="tpu_custom_call" | custom-call | flops 1 | bytes 1 | tf_op jit(solution)/shard_map/norm_gradient/pallas_call | solution.py:88
  43.9 1.9 %collective-permute-start.9 = (f32[2,128,128]{2,1,0:T(8,128)S(1)}, f32[2,128,128]{2,1,0:T(8,128)S(1)}, u32[]{:S(2)}, u32[]{:S(2)}) collective-permute-start(f32[2,128,128]{2,1,0:T(8,128)S(1)} %get-tuple-element.148), channel_id=1, source_target_pairs={{0,12},{4,8},{8,4},{12,0},{16,28},{20,24},{24,20},{28,16},{1,13},{... | collective-permute-start | bytes 393224 | tf_op jit(solution)/shard_map/ppermute | solution.py:382
  45.8 2.5 %query_gradient.1.grad_ref.own_ref = bf16[512,1024]{1,0:T(8,128)(2,1)S(1)} custom-call(s32[2]{0:T(128)S(1)} %pad_add_fusion.slots, bf16[512,1024]{1,0:T(8,128)(2,1)S(1)} %get-tuple-element.158.datt_ref, bf16[512,1024]{1,0:T(8,128)(2,1)S(1)} %get-tuple-element.118.v_ref, bf16[512,1024]{1,0:T(8,128)(2,1)S(1)} %get-tuple-element.117.k_ref, ...), custom_call_target="tpu_custom_call" | custom-call | flops 1 | bytes 1 | tf_op jit(solution)/shard_map/query_gradient/pallas_call | solution.py:88
  49.8 3.8 %collective-permute-start.13 = (f32[512,512]{1,0:T(8,128)S(1)}, f32[512,512]{1,0:T(8,128)S(1)}, u32[]{:S(2)}, u32[]{:S(2)}) collective-permute-start(f32[512,512]{1,0:T(8,128)S(1)} %get-tuple-element.157), channel_id=1, source_target_pairs={{0,1},{1,0},{2,3},{3,2},{4,5},{5,4},{6,7},{7,6},{8,9},{9,8},{10,11... | collective-permute-start | bytes 3145736 | tf_op jit(solution)/shard_map/ppermute | solution.py:455
  53.7 1.3 collective-permute-start.11
  55.0 2.6 %within_block.1 = (f32[512,1024]{1,0:T(8,128)S(1)}, f32[512,1024]{1,0:T(8,128)S(1)}) custom-call(bf16[512,1024]{1,0:T(8,128)(2,1)S(1)} %get-tuple-element.158.datt_ref, bf16[512,1024]{1,0:T(8,128)(2,1)S(1)} %get-tuple-element.118.v_ref, bf16[512,1024]{1,0:T(8,128)(2,1)S(1)} %get-tuple-element.117.k_ref, bf16[512,1024]{1,0:T(8,128)(2,1)S(1)} %get-tuple-element.120.q_ref), custom_call_target="tpu_custom_call" | custom-call | flops 1 | bytes 1 | tf_op jit(solution)/shard_map/within_block/pallas_call | solution.py:88
  57.6 2.6 %weight_q.1 = f32[512,1024]{1,0:T(8,128)} custom-call(s32[1]{0:T(128)} %bitcast.2.me_ref, bf16[16,64,1024]{2,1,0:T(8,128)(2,1)S(1)} %merge_inputs.1.x_ref, bf16[512,1024]{1,0:T(8,128)(2,1)S(1)} %query_gradient.1.grad_ref.own_ref, f32[512,512]{1,0:T(8,128)S(1)} %collective-permute-done.12.rest_0_, f32[512,512]{1,0:T(8,128)S(1)} %collective-permute-done.13.rest_1_), custom_call_target="tpu_custom_call" | custom-call | flops 1 | bytes 1 | tf_op jit(solution)/shard_map/weight_q/pallas_call | solution.py:88
  60.2 1.3 weight_q_kept.1.rest_ref.a_ref
  61.5 2.1 %collective-permute-done.11.base_ref = f32[2,128,128]{2,1,0:T(8,128)S(1)} collective-permute-done((f32[2,128,128]{2,1,0:T(8,128)S(1)}, f32[2,128,128]{2,1,0:T(8,128)S(1)}, u32[]{:S(2)}, u32[]{:S(2)}) %collective-permute-start.11) | collective-permute-done | bytes 131104 | tf_op jit(solution)/shard_map/ppermute | solution.py:436
  64.5 2.3 %collective-permute-start.16 = (f32[2,128,128]{2,1,0:T(8,128)S(1)}, f32[2,128,128]{2,1,0:T(8,128)S(1)}, u32[]{:S(2)}, u32[]{:S(2)}) collective-permute-start(f32[2,128,128]{2,1,0:T(8,128)S(1)} %get-tuple-element.173), channel_id=1, source_target_pairs={{0,12},{4,8},{8,4},{12,0},{16,28},{20,24},{24,20},{28,16},{1,13},{... | collective-permute-start | bytes 393224 | tf_op jit(solution)/shard_map/ppermute | solution.py:382
  66.7 4.0 %input_gradient_q.1.first_ref = f32[512,2048]{1,0:T(8,128)S(1)} custom-call(bf16[512,1024]{1,0:T(8,128)(2,1)S(1)} %query_gradient.1.grad_ref.own_ref, bf16[2048,1024]{1,0:T(8,128)(2,1)S(1)} %copy-done.4), custom_call_target="tpu_custom_call" | custom-call | flops 1 | bytes 1 | tf_op jit(solution)/shard_map/input_gradient_q/pallas_call | solution.py:621
  71.5 1.9 key_value_gradients.1
  73.4 4.3 %collective-permute-start.19 = (f32[512,512]{1,0:T(8,128)S(1)}, f32[512,512]{1,0:T(8,128)S(1)}, u32[]{:S(2)}, u32[]{:S(2)}) collective-permute-start(f32[512,512]{1,0:T(8,128)S(1)} %get-tuple-element.181), channel_id=1, source_target_pairs={{0,1},{1,0},{2,3},{3,2},{4,5},{5,4},{6,7},{7,6},{8,9},{9,8},{10,11... | collective-permute-start | bytes 3145736 | tf_op jit(solution)/shard_map/ppermute | solution.py:455
  78.3 1.7 collective-permute-done.19.rest_0_
  80.0 1.5 collective-permute-done.20.rest_1_
  81.5 2.6 %weight_k.1 = f32[512,1024]{1,0:T(8,128)} custom-call(s32[1]{0:T(128)} %bitcast.2.me_ref, bf16[16,64,1024]{2,1,0:T(8,128)(2,1)S(1)} %merge_inputs.1.x_ref, bf16[512,1024]{1,0:T(8,128)(2,1)S(1)} %get-tuple-element.191.own_ref.grad_a, f32[512,512]{1,0:T(8,128)S(1)} %collective-permute-done.19.rest_0_, f32[512,512]{1,0:T(8,128)S(1)} %collective-permute-done.20.rest_1_), custom_call_target="tpu_custom_call" | custom-call | flops 1 | bytes 1 | tf_op jit(solution)/shard_map/weight_k/pallas_call | solution.py:88
  84.5 1.3 weight_k_kept.1.a_ref
  85.8 2.6 %weight_v.1 = f32[512,1024]{1,0:T(8,128)} custom-call(s32[1]{0:T(128)} %bitcast.2.me_ref, bf16[16,64,1024]{2,1,0:T(8,128)(2,1)S(1)} %merge_inputs.1.x_ref, bf16[512,1024]{1,0:T(8,128)(2,1)S(1)} %get-tuple-element.190.own_ref.grad_b, f32[512,512]{1,0:T(8,128)S(1)} %collective-permute-done.17.rest_0_, f32[512,512]{1,0:T(8,128)S(1)} %collective-permute-done.18.rest_1_), custom_call_target="tpu_custom_call" | custom-call | flops 1 | bytes 1 | tf_op jit(solution)/shard_map/weight_v/pallas_call | solution.py:88
  89.5 1.3 weight_v_kept.1.a_ref
  90.8 1.3 copy-done
  92.1 12.0 %input_gradient_kv.1 = (bf16[512,2048]{1,0:T(8,128)(2,1)}, f32[8,2048]{1,0:T(8,128)S(1)}) custom-call(f32[512,2048]{1,0:T(8,128)S(1)} %input_gradient_q.1.first_ref, f32[8,512]{1,0:T(8,128)S(1)} %get-tuple-element.167.codes_ref, bf16[512,1024]{1,0:T(8,128)(2,1)S(1)} %get-tuple-element.191.own_ref.grad_a, ...), custom_call_target="tpu_custom_call" | custom-call | flops 1 | bytes 1 | tf_op jit(solution)/shard_map/input_gradient_kv/pallas_call | solution.py:637
  105.6 1.7 add_rows_with.3
  107.4 1.1 collective-permute-start.23
  108.5 1.7 add_rows.15.rest_ref.a_ref
  110.2 1.7 add_rows.16
  112.6 1.7 add_rows.17.a_ref
  114.3 14.5 %collective-permute-done.23.got_ref.b_ref = f32[272,1024]{1,0:T(8,128)S(1)} collective-permute-done((f32[272,1024]{1,0:T(8,128)S(1)}, f32[272,1024]{1,0:T(8,128)S(1)}, u32[]{:S(2)}, u32[]{:S(2)}) %collective-permute-start.23) | collective-permute-done | bytes 1114144 | tf_op jit(solution)/shard_map/ppermute | solution.py:455
  128.9 3.0 %collective-permute-done.27.b_ref = f32[512,1024]{1,0:T(8,128)} collective-permute-done((f32[512,1024]{1,0:T(8,128)}, f32[512,1024]{1,0:T(8,128)}, u32[]{:S(2)}, u32[]{:S(2)}) %collective-permute-start.27) | collective-permute-done | bytes 2097184 | tf_op jit(solution)/shard_map/ppermute | solution.py:455
  132.0 1.7 add_rows.19
  133.7 1.3 collective-permute-start.29
  135.3 1.7 add_rows.20.a_ref
  137.0 3.0 %collective-permute-done.26.b_ref = f32[256,1024]{1,0:T(8,128)S(1)} collective-permute-done((f32[256,1024]{1,0:T(8,128)S(1)}, f32[256,1024]{1,0:T(8,128)S(1)}, u32[]{:S(2)}, u32[]{:S(2)}) %collective-permute-start.26) | collective-permute-done | bytes 1048608 | tf_op jit(solution)/shard_map/ppermute | solution.py:455
  140.2 10.1 %collective-permute-done.25.got_ref.b_ref = f32[144,1024]{1,0:T(8,128)S(1)} collective-permute-done((f32[144,1024]{1,0:T(8,128)S(1)}, f32[144,1024]{1,0:T(8,128)S(1)}, u32[]{:S(2)}, u32[]{:S(2)}) %collective-permute-start.25) | collective-permute-done | bytes 589856 | tf_op jit(solution)/shard_map/ppermute | solution.py:455
  152.4 1.8 collective-permute-done.31.b_ref
  154.2 9.9 %collective-permute-done.30.b_ref = f32[128,1024]{1,0:T(8,128)S(1)} collective-permute-done((f32[128,1024]{1,0:T(8,128)S(1)}, f32[128,1024]{1,0:T(8,128)S(1)}, u32[]{:S(2)}, u32[]{:S(2)}) %collective-permute-start.30) | collective-permute-done | bytes 524320 | tf_op jit(solution)/shard_map/ppermute | solution.py:455
  164.2 4.4 %collective-permute-done.28.got_ref = f32[80,1024]{1,0:T(8,128)S(1)} collective-permute-done((f32[80,1024]{1,0:T(8,128)S(1)}, f32[80,1024]{1,0:T(8,128)S(1)}, u32[]{:S(2)}, u32[]{:S(2)}) %collective-permute-start.28) | collective-permute-done | bytes 327712 | tf_op jit(solution)/shard_map/ppermute | solution.py:455
  170.4 1.7 collective-permute-done.33
  173.4 11.4 %collective-permute-done.32 = f32[64,1024]{1,0:T(8,128)S(1)} collective-permute-done((f32[64,1024]{1,0:T(8,128)S(1)}, f32[64,1024]{1,0:T(8,128)S(1)}, u32[]{:S(2)}, u32[]{:S(2)}) %collective-permute-start.32) | collective-permute-done | bytes 262176 | tf_op jit(solution)/shard_map/ppermute | solution.py:455
  184.9 3.3 %collective-permute-done.34 = f32[64,1024]{1,0:T(8,128)S(1)} collective-permute-done((f32[64,1024]{1,0:T(8,128)S(1)}, f32[64,1024]{1,0:T(8,128)S(1)}, u32[]{:S(2)}, u32[]{:S(2)}) %collective-permute-start.34) | collective-permute-done | bytes 262176 | tf_op jit(solution)/shard_map/ppermute | solution.py:455
  (94 shorter events, 19.4 us)
Async XLA Ops:
  2.3 13.4 %copy-start.4 = (bf16[2048,1024]{1,0:T(8,128)(2,1)S(1)}, bf16[2048,1024]{1,0:T(8,128)(2,1)}, u32[]{:S(2)}) copy-start(bf16[2048,1024]{1,0:T(8,128)(2,1)} %w_ref.1) | copy-start | bytes 12582916
  13.0 7.8 %collective-permute-start = (f32[2,128,128]{2,1,0:T(8,128)S(1)}, f32[2,128,128]{2,1,0:T(8,128)S(1)}, u32[]{:S(2)}, u32[]{:S(2)}) collective-permute-start(f32[2,128,128]{2,1,0:T(8,128)S(1)} %get-tuple-element.124), channel_id=1, source_target_pairs={{0,4},{4,0},{8,12},{12,8},{16,20},{20,16},{24,28},{28,24},{1,5},{5... | collective-permute-start | bytes 393224 | tf_op jit(solution)/shard_map/ppermute | solution.py:382
  13.3 7.5 %collective-permute-start.1 = (f32[2,128,128]{2,1,0:T(8,128)S(1)}, f32[2,128,128]{2,1,0:T(8,128)S(1)}, u32[]{:S(2)}, u32[]{:S(2)}) collective-permute-start(f32[2,128,128]{2,1,0:T(8,128)S(1)} %get-tuple-element.125), channel_id=1, source_target_pairs={{0,8},{4,12},{8,0},{12,4},{16,24},{20,28},{24,16},{28,20},{1,9},{5... | collective-permute-start | bytes 393224 | tf_op jit(solution)/shard_map/ppermute | solution.py:382
  13.3 7.5 %collective-permute-start.2 = (f32[2,128,128]{2,1,0:T(8,128)S(1)}, f32[2,128,128]{2,1,0:T(8,128)S(1)}, u32[]{:S(2)}, u32[]{:S(2)}) collective-permute-start(f32[2,128,128]{2,1,0:T(8,128)S(1)} %get-tuple-element.126), channel_id=1, source_target_pairs={{0,12},{4,8},{8,4},{12,0},{16,28},{20,24},{24,20},{28,16},{1,13},{... | collective-permute-start | bytes 393224 | tf_op jit(solution)/shard_map/ppermute | solution.py:382
  19.7 20.0 %copy-start.7 = (bf16[1,512,1024]{2,1,0:T(8,128)(2,1)S(1)}, bf16[1,512,1024]{2,1,0:T(8,128)(2,1)}, u32[]{:S(2)}) copy-start(bf16[1,512,1024]{2,1,0:T(8,128)(2,1)} %param.15) | copy-start | bytes 3145732
  19.8 20.0 %copy-start.8 = (f32[1024]{0:T(1024)S(1)}, f32[1024]{0:T(1024)}, u32[]{:S(2)}) copy-start(f32[1024]{0:T(1024)} %param.14) | copy-start | bytes 12292
  20.9 27.4 %collective-permute-start.10 = (f32[16,64,512]{2,1,0:T(8,128)S(1)}, f32[16,64,512]{2,1,0:T(8,128)S(1)}, u32[]{:S(2)}, u32[]{:S(2)}) collective-permute-start(f32[16,64,512]{2,1,0:T(8,128)S(1)} %get-tuple-element.150), channel_id=1, source_target_pairs={{0,1},{1,0},{2,3},{3,2},{4,5},{5,4},{6,7},{7,6},{8,9},{9,8},{10,11... | collective-permute-start | bytes 6291464 | tf_op jit(solution)/shard_map/ppermute | solution.py:455
  23.1 8.8 %collective-permute-start.3 = (f32[2,128,128]{2,1,0:T(8,128)S(1)}, f32[2,128,128]{2,1,0:T(8,128)S(1)}, u32[]{:S(2)}, u32[]{:S(2)}) collective-permute-start(f32[2,128,128]{2,1,0:T(8,128)S(1)} %add_add_fusion.1), channel_id=1, source_target_pairs={{0,24},{4,28},{8,16},{12,20},{1,25},{5,29},{9,17},{13,21},{2,26},{... | collective-permute-start | bytes 393224 | tf_op jit(solution)/shard_map/ppermute | solution.py:436
  32.2 3.9 %collective-permute-start.4 = (f32[2,128,128]{2,1,0:T(8,128)S(1)}, f32[2,128,128]{2,1,0:T(8,128)S(1)}, u32[]{:S(2)}, u32[]{:S(2)}) collective-permute-start(f32[2,128,128]{2,1,0:T(8,128)S(1)} %get-tuple-element.135), channel_id=1, source_target_pairs={{0,4},{4,0},{8,12},{12,8},{16,20},{20,16},{24,28},{28,24},{1,5},{5... | collective-permute-start | bytes 393224 | tf_op jit(solution)/shard_map/ppermute | solution.py:382
  32.5 4.1 %collective-permute-start.5 = (f32[2,128,128]{2,1,0:T(8,128)S(1)}, f32[2,128,128]{2,1,0:T(8,128)S(1)}, u32[]{:S(2)}, u32[]{:S(2)}) collective-permute-start(f32[2,128,128]{2,1,0:T(8,128)S(1)} %get-tuple-element.136), channel_id=1, source_target_pairs={{0,8},{4,12},{8,0},{12,4},{16,24},{20,28},{24,16},{28,20},{1,9},{5... | collective-permute-start | bytes 393224 | tf_op jit(solution)/shard_map/ppermute | solution.py:382
  32.5 7.2 %collective-permute-start.6 = (f32[2,128,128]{2,1,0:T(8,128)S(1)}, f32[2,128,128]{2,1,0:T(8,128)S(1)}, u32[]{:S(2)}, u32[]{:S(2)}) collective-permute-start(f32[2,128,128]{2,1,0:T(8,128)S(1)} %get-tuple-element.137), channel_id=1, source_target_pairs={{0,12},{4,8},{8,4},{12,0},{16,28},{20,24},{24,20},{28,16},{1,13},{... | collective-permute-start | bytes 393224 | tf_op jit(solution)/shard_map/ppermute | solution.py:382
  43.0 5.5 %collective-permute-start.7 = (f32[2,128,128]{2,1,0:T(8,128)S(1)}, f32[2,128,128]{2,1,0:T(8,128)S(1)}, u32[]{:S(2)}, u32[]{:S(2)}) collective-permute-start(f32[2,128,128]{2,1,0:T(8,128)S(1)} %get-tuple-element.146), channel_id=1, source_target_pairs={{0,4},{4,0},{8,12},{12,8},{16,20},{20,16},{24,28},{28,24},{1,5},{5... | collective-permute-start | bytes 393224 | tf_op jit(solution)/shard_map/ppermute | solution.py:382
  43.4 5.2 %collective-permute-start.8 = (f32[2,128,128]{2,1,0:T(8,128)S(1)}, f32[2,128,128]{2,1,0:T(8,128)S(1)}, u32[]{:S(2)}, u32[]{:S(2)}) collective-permute-start(f32[2,128,128]{2,1,0:T(8,128)S(1)} %get-tuple-element.147), channel_id=1, source_target_pairs={{0,8},{4,12},{8,0},{12,4},{16,24},{20,28},{24,16},{28,20},{1,9},{5... | collective-permute-start | bytes 393224 | tf_op jit(solution)/shard_map/ppermute | solution.py:382
  43.9 5.8 %collective-permute-start.9 = (f32[2,128,128]{2,1,0:T(8,128)S(1)}, f32[2,128,128]{2,1,0:T(8,128)S(1)}, u32[]{:S(2)}, u32[]{:S(2)}) collective-permute-start(f32[2,128,128]{2,1,0:T(8,128)S(1)} %get-tuple-element.148), channel_id=1, source_target_pairs={{0,12},{4,8},{8,4},{12,0},{16,28},{20,24},{24,20},{28,16},{1,13},{... | collective-permute-start | bytes 393224 | tf_op jit(solution)/shard_map/ppermute | solution.py:382
  49.8 7.8 %collective-permute-start.13 = (f32[512,512]{1,0:T(8,128)S(1)}, f32[512,512]{1,0:T(8,128)S(1)}, u32[]{:S(2)}, u32[]{:S(2)}) collective-permute-start(f32[512,512]{1,0:T(8,128)S(1)} %get-tuple-element.157), channel_id=1, source_target_pairs={{0,1},{1,0},{2,3},{3,2},{4,5},{5,4},{6,7},{7,6},{8,9},{9,8},{10,11... | collective-permute-start | bytes 3145736 | tf_op jit(solution)/shard_map/ppermute | solution.py:455
  53.6 4.0 %collective-permute-start.12 = (f32[512,512]{1,0:T(8,128)S(1)}, f32[512,512]{1,0:T(8,128)S(1)}, u32[]{:S(2)}, u32[]{:S(2)}) collective-permute-start(f32[512,512]{1,0:T(8,128)S(1)} %get-tuple-element.156), channel_id=1, source_target_pairs={{0,1},{1,0},{2,3},{3,2},{4,5},{5,4},{6,7},{7,6},{8,9},{9,8},{10,11... | collective-permute-start | bytes 3145736 | tf_op jit(solution)/shard_map/ppermute | solution.py:455
  53.7 9.9 %collective-permute-start.11 = (f32[2,128,128]{2,1,0:T(8,128)S(1)}, f32[2,128,128]{2,1,0:T(8,128)S(1)}, u32[]{:S(2)}, u32[]{:S(2)}) collective-permute-start(f32[2,128,128]{2,1,0:T(8,128)S(1)} %add_add_fusion), channel_id=1, source_target_pairs={{28,4},{24,0},{20,12},{16,8},{29,5},{25,1},{21,13},{17,9},{30,6},{... | collective-permute-start | bytes 393224 | tf_op jit(solution)/shard_map/ppermute | solution.py:436
  64.0 6.8 %collective-permute-start.14 = (f32[2,128,128]{2,1,0:T(8,128)S(1)}, f32[2,128,128]{2,1,0:T(8,128)S(1)}, u32[]{:S(2)}, u32[]{:S(2)}) collective-permute-start(f32[2,128,128]{2,1,0:T(8,128)S(1)} %get-tuple-element.171), channel_id=1, source_target_pairs={{0,4},{4,0},{8,12},{12,8},{16,20},{20,16},{24,28},{28,24},{1,5},{5... | collective-permute-start | bytes 393224 | tf_op jit(solution)/shard_map/ppermute | solution.py:382
  64.5 6.3 %collective-permute-start.15 = (f32[2,128,128]{2,1,0:T(8,128)S(1)}, f32[2,128,128]{2,1,0:T(8,128)S(1)}, u32[]{:S(2)}, u32[]{:S(2)}) collective-permute-start(f32[2,128,128]{2,1,0:T(8,128)S(1)} %get-tuple-element.172), channel_id=1, source_target_pairs={{0,8},{4,12},{8,0},{12,4},{16,24},{20,28},{24,16},{28,20},{1,9},{5... | collective-permute-start | bytes 393224 | tf_op jit(solution)/shard_map/ppermute | solution.py:382
  64.5 7.1 %collective-permute-start.16 = (f32[2,128,128]{2,1,0:T(8,128)S(1)}, f32[2,128,128]{2,1,0:T(8,128)S(1)}, u32[]{:S(2)}, u32[]{:S(2)}) collective-permute-start(f32[2,128,128]{2,1,0:T(8,128)S(1)} %get-tuple-element.173), channel_id=1, source_target_pairs={{0,12},{4,8},{8,4},{12,0},{16,28},{20,24},{24,20},{28,16},{1,13},{... | collective-permute-start | bytes 393224 | tf_op jit(solution)/shard_map/ppermute | solution.py:382
  66.7 38.9 %collective-permute-start.21 = (f32[512,1024]{1,0:T(8,128)}, f32[512,1024]{1,0:T(8,128)}, u32[]{:S(2)}, u32[]{:S(2)}) collective-permute-start(f32[512,1024]{1,0:T(8,128)} %weight_q.1), channel_id=1, source_target_pairs={{0,2},{1,9},{2,0},{3,11},{4,6},{5,13},{6,4},{7,15},{8,10},{9,1},{1... | collective-permute-start | bytes 6291464 | tf_op jit(solution)/shard_map/ppermute | solution.py:455
  73.4 6.6 %collective-permute-start.19 = (f32[512,512]{1,0:T(8,128)S(1)}, f32[512,512]{1,0:T(8,128)S(1)}, u32[]{:S(2)}, u32[]{:S(2)}) collective-permute-start(f32[512,512]{1,0:T(8,128)S(1)} %get-tuple-element.181), channel_id=1, source_target_pairs={{0,1},{1,0},{2,3},{3,2},{4,5},{5,4},{6,7},{7,6},{8,9},{9,8},{10,11... | collective-permute-start | bytes 3145736 | tf_op jit(solution)/shard_map/ppermute | solution.py:455
  77.7 3.8 %collective-permute-start.20 = (f32[512,512]{1,0:T(8,128)S(1)}, f32[512,512]{1,0:T(8,128)S(1)}, u32[]{:S(2)}, u32[]{:S(2)}) collective-permute-start(f32[512,512]{1,0:T(8,128)S(1)} %get-tuple-element.182), channel_id=1, source_target_pairs={{0,1},{1,0},{2,3},{3,2},{4,5},{5,4},{6,7},{7,6},{8,9},{9,8},{10,11... | collective-permute-start | bytes 3145736 | tf_op jit(solution)/shard_map/ppermute | solution.py:455
  77.8 8.0 %collective-permute-start.17 = (f32[512,512]{1,0:T(8,128)S(1)}, f32[512,512]{1,0:T(8,128)S(1)}, u32[]{:S(2)}, u32[]{:S(2)}) collective-permute-start(f32[512,512]{1,0:T(8,128)S(1)} %get-tuple-element.179), channel_id=1, source_target_pairs={{0,1},{1,0},{2,3},{3,2},{4,5},{5,4},{6,7},{7,6},{8,9},{9,8},{10,11... | collective-permute-start | bytes 3145736 | tf_op jit(solution)/shard_map/ppermute | solution.py:455
  78.2 7.6 %collective-permute-start.18 = (f32[512,512]{1,0:T(8,128)S(1)}, f32[512,512]{1,0:T(8,128)S(1)}, u32[]{:S(2)}, u32[]{:S(2)}) collective-permute-start(f32[512,512]{1,0:T(8,128)S(1)} %get-tuple-element.180), channel_id=1, source_target_pairs={{0,1},{1,0},{2,3},{3,2},{4,5},{5,4},{6,7},{7,6},{8,9},{9,8},{10,11... | collective-permute-start | bytes 3145736 | tf_op jit(solution)/shard_map/ppermute | solution.py:455
  84.1 26.1 %collective-permute-start.24 = (f32[512,1024]{1,0:T(8,128)}, f32[512,1024]{1,0:T(8,128)}, u32[]{:S(2)}, u32[]{:S(2)}) collective-permute-start(f32[512,1024]{1,0:T(8,128)} %weight_k.1), channel_id=1, source_target_pairs={{0,2},{1,5},{2,0},{3,7},{4,6},{5,1},{6,4},{7,3},{8,10},{9,13},{10,... | collective-permute-start | bytes 6291464 | tf_op jit(solution)/shard_map/ppermute | solution.py:455
  85.7 2.7 %copy-start.2 = (f32[512,1024]{1,0:T(8,128)}, f32[512,1024]{1,0:T(8,128)S(1)}, u32[]{:S(2)}) copy-start(f32[512,1024]{1,0:T(8,128)S(1)} %weight_k_kept.1.a_ref) | copy-start | bytes 6291460
  85.8 6.3 %copy-start.6 = (bf16[2048,1024]{1,0:T(8,128)(2,1)S(1)}, bf16[2048,1024]{1,0:T(8,128)(2,1)}, u32[]{:S(2)}) copy-start(bf16[2048,1024]{1,0:T(8,128)(2,1)} %wb_ref.1) | copy-start | bytes 12582916
  88.4 3.7 %copy-start.5 = (bf16[2048,1024]{1,0:T(8,128)(2,1)S(1)}, bf16[2048,1024]{1,0:T(8,128)(2,1)}, u32[]{:S(2)}) copy-start(bf16[2048,1024]{1,0:T(8,128)(2,1)} %wa_ref.1) | copy-start | bytes 12582916
  88.4 43.6 %collective-permute-start.27 = (f32[512,1024]{1,0:T(8,128)}, f32[512,1024]{1,0:T(8,128)}, u32[]{:S(2)}, u32[]{:S(2)}) collective-permute-start(f32[512,1024]{1,0:T(8,128)} %weight_v.1), channel_id=1, source_target_pairs={{0,8},{1,5},{2,10},{3,7},{4,12},{5,1},{6,14},{7,3},{8,0},{9,13},{1... | collective-permute-start | bytes 6291464 | tf_op jit(solution)/shard_map/ppermute | solution.py:455
  90.8 1.3 copy-start
  104.1 1.5 collective-permute-start.22
  107.4 2.8 %copy-start.3 = (f32[512,1024]{1,0:T(8,128)S(1)}, f32[512,1024]{1,0:T(8,128)}, u32[]{:S(2)}) copy-start(f32[512,1024]{1,0:T(8,128)} %copy-done.2) | copy-start | bytes 6291460
  107.4 21.4 %collective-permute-start.23 = (f32[272,1024]{1,0:T(8,128)S(1)}, f32[272,1024]{1,0:T(8,128)S(1)}, u32[]{:S(2)}, u32[]{:S(2)}) collective-permute-start(f32[272,1024]{1,0:T(8,128)S(1)} %get-tuple-element.197), channel_id=1, source_target_pairs={{0,8},{1,3},{2,10},{3,1},{4,12},{5,7},{6,14},{7,5},{8,0},{9,11},{1... | collective-permute-start | bytes 3342344 | tf_op jit(solution)/shard_map/ppermute | solution.py:455
  111.9 28.1 %collective-permute-start.26 = (f32[256,1024]{1,0:T(8,128)S(1)}, f32[256,1024]{1,0:T(8,128)S(1)}, u32[]{:S(2)}, u32[]{:S(2)}) collective-permute-start(f32[256,1024]{1,0:T(8,128)S(1)} %add_rows.16), channel_id=1, source_target_pairs={{0,8},{1,3},{2,10},{3,1},{4,12},{5,7},{6,14},{7,5},{8,0},{9,11},{1... | collective-permute-start | bytes 3145736 | tf_op jit(solution)/shard_map/ppermute | solution.py:455
  128.8 3.2 %copy-start.1 = (f32[512,1024]{1,0:T(8,128)S(1)}, f32[512,1024]{1,0:T(8,128)}, u32[]{:S(2)}) copy-start(f32[512,1024]{1,0:T(8,128)} %copy-done) | copy-start | bytes 6291460
  133.7 17.6 %collective-permute-start.29 = (f32[256,1024]{1,0:T(8,128)S(1)}, f32[256,1024]{1,0:T(8,128)S(1)}, u32[]{:S(2)}, u32[]{:S(2)}) collective-permute-start(f32[256,1024]{1,0:T(8,128)S(1)} %add_rows.19), channel_id=1, source_target_pairs={{0,4},{1,3},{2,6},{3,1},{4,0},{5,7},{6,2},{7,5},{8,12},{9,11},{10,... | collective-permute-start | bytes 3145736 | tf_op jit(solution)/shard_map/ppermute | solution.py:455
  134.9 15.4 %collective-permute-start.25 = (f32[144,1024]{1,0:T(8,128)S(1)}, f32[144,1024]{1,0:T(8,128)S(1)}, u32[]{:S(2)}, u32[]{:S(2)}) collective-permute-start(f32[144,1024]{1,0:T(8,128)S(1)} %get-tuple-element.203), channel_id=1, source_target_pairs={{0,24},{1,5},{2,26},{3,7},{4,28},{5,1},{6,30},{7,3},{8,16},{9,13},... | collective-permute-start | bytes 1769480 | tf_op jit(solution)/shard_map/ppermute | solution.py:455
  140.1 14.1 %collective-permute-start.31 = (f32[128,1024]{1,0:T(8,128)S(1)}, f32[128,1024]{1,0:T(8,128)S(1)}, u32[]{:S(2)}, u32[]{:S(2)}) collective-permute-start(f32[128,1024]{1,0:T(8,128)S(1)} %add_rows.21), channel_id=1, source_target_pairs={{0,24},{1,9},{2,26},{3,11},{4,28},{5,13},{6,30},{7,15},{8,16},{9,1... | collective-permute-start | bytes 1572872 | tf_op jit(solution)/shard_map/ppermute | solution.py:455
  151.3 12.8 %collective-permute-start.30 = (f32[128,1024]{1,0:T(8,128)S(1)}, f32[128,1024]{1,0:T(8,128)S(1)}, u32[]{:S(2)}, u32[]{:S(2)}) collective-permute-start(f32[128,1024]{1,0:T(8,128)S(1)} %add_rows.24), channel_id=1, source_target_pairs={{0,2},{1,9},{2,0},{3,11},{4,6},{5,13},{6,4},{7,15},{8,10},{9,1},{1... | collective-permute-start | bytes 1572872 | tf_op jit(solution)/shard_map/ppermute | solution.py:455
  151.4 17.2 %collective-permute-start.28 = (f32[80,1024]{1,0:T(8,128)S(1)}, f32[80,1024]{1,0:T(8,128)S(1)}, u32[]{:S(2)}, u32[]{:S(2)}) collective-permute-start(f32[80,1024]{1,0:T(8,128)S(1)} %get-tuple-element.211), channel_id=1, source_target_pairs={{0,4},{1,25},{2,6},{3,27},{4,0},{5,29},{6,2},{7,31},{8,12},{9,17},... | collective-permute-start | bytes 983048 | tf_op jit(solution)/shard_map/ppermute | solution.py:455
  168.6 3.6 %collective-permute-start.33 = (f32[16,1024]{1,0:T(8,128)S(1)}, f32[16,1024]{1,0:T(8,128)S(1)}, u32[]{:S(2)}, u32[]{:S(2)}) collective-permute-start(f32[16,1024]{1,0:T(8,128)S(1)} %get-tuple-element.222), channel_id=1, source_target_pairs={{0,2},{1,9},{2,0},{3,11},{4,6},{5,13},{6,4},{7,15},{8,10},{9,1},{1... | collective-permute-start | bytes 196616 | tf_op jit(solution)/shard_map/ppermute | solution.py:455
  168.9 15.9 %collective-permute-start.32 = (f32[64,1024]{1,0:T(8,128)S(1)}, f32[64,1024]{1,0:T(8,128)S(1)}, u32[]{:S(2)}, u32[]{:S(2)}) collective-permute-start(f32[64,1024]{1,0:T(8,128)S(1)} %add_rows.26), channel_id=1, source_target_pairs={{0,4},{1,25},{2,6},{3,27},{4,0},{5,29},{6,2},{7,31},{8,12},{9,17},... | collective-permute-start | bytes 786440 | tf_op jit(solution)/shard_map/ppermute | solution.py:455
  169.9 18.3 %collective-permute-start.34 = (f32[64,1024]{1,0:T(8,128)S(1)}, f32[64,1024]{1,0:T(8,128)S(1)}, u32[]{:S(2)}, u32[]{:S(2)}) collective-permute-start(f32[64,1024]{1,0:T(8,128)S(1)} %add_rows.28), channel_id=1, source_target_pairs={{0,24},{1,25},{2,26},{3,27},{4,28},{5,29},{6,30},{7,31},{8,16},{9,... | collective-permute-start | bytes 786440 | tf_op jit(solution)/shard_map/ppermute | solution.py:455

commit v5 on v4

--- a/solution.py
+++ b/solution.py
@@ -18,7 +18,7 @@
 F32 = jnp.float32
 BF16 = jnp.bfloat16
 MIB = 1024 * 1024
-EMBED_MIB = 41
+EMBED_MIB = 43
 
 fsq_levels = (8, 8, 8, 5, 5, 5)
 fsq_bases = (1, 8, 64, 512, 2560, 12800)
@@ -43,7 +43,7 @@
 
 
 def params(size):
-    return pltpu.CompilerParams(vmem_limit_bytes=int(size) + 5 * MIB)
+    return pltpu.CompilerParams(vmem_limit_bytes=int(size) + 3 * MIB)
 
 
 def cost(flops, moved):
@@ -127,19 +127,22 @@
     turned = jnp.transpose(codes)
     incoming[0].wait()
     step = 64
-    for r in range(0, t, step):
-        summed = resid_ref[r : r + step].astype(F32)
-        for index in range(count):
-            summed = summed + turned[r : r + step, index : index + 1] * packed_ref[index : index + 1]
-        x_ref[r : r + step] = summed.astype(BF16)
+    for p in range(PARTS):
+        rows = part_rows(t, p)
+        for r in range(rows.start, rows.stop, step):
+            summed = resid_ref[r : r + step].astype(F32)
+            for index in range(count):
+                summed = summed + turned[r : r + step, index : index + 1] * packed_ref[index : index + 1]
+            x_ref[r : r + step] = summed.astype(BF16)
+        if p == 0:
+            incoming[1].wait()
+            incoming[2].wait()
+        for c in range(2):
+            at = slice(c * half, (c + 1) * half)
+            key, slope = silu_and_slope(mm(x_ref[rows], wk_ref[:, at]))
+            k_ref[rows, at] = key.astype(BF16)
+            slope_ref[rows, at] = slope
     x = x_ref[...]
-    incoming[1].wait()
-    incoming[2].wait()
-    for c in range(2):
-        at = slice(c * half, (c + 1) * half)
-        key, slope = silu_and_slope(mm(x, wk_ref[:, at]))
-        k_ref[:, at] = key.astype(BF16)
-        slope_ref[:, at] = slope
     incoming[3].wait()
     incoming[4].wait()
     for c in range(2):
@@ -158,8 +161,8 @@
     t, d = resid.shape
     hd = w_key.shape[1]
     heads = hd // DH
-    ids = jnp.pad(token_ids.astype(F32), ((0, 0), (0, d - t)))
-    packed = jnp.concatenate([code_proj, ids], axis=0)
+    ids = jnp.pad(token_ids, ((0, 0), (0, d - t)))
+    packed = jnp.concatenate([code_proj, ids.astype(F32)], axis=0)
     return pl.pallas_call(
         embed_kernel,
         in_specs=[SMEM, VMEM] + [HBM] * 3,
@@ -508,6 +511,38 @@
     return in_vmem(kernel, [me], [x, own, *others], outs, [], cost(0, 0), name)
 
 
+def sent_kernel(slots, me_ref, x_ref, own_ref, *rest):
+    other_refs, (out_hbm, out_ref, sems) = rest[:-3], rest[-3:]
+    core = me_ref[0] % 2
+    rows = jnp.concatenate([x_ref[a ^ (core * (a ^ b))] for a, b in slots], axis=0)
+    share = other_refs[0].shape[1]
+    copies = []
+    for start in range(0, own_ref.shape[1], WIDE):
+        other = other_refs[start // share][:, start % share : start % share + WIDE]
+        grads = jnp.concatenate([own_ref[:, start : start + WIDE], other.astype(BF16)], axis=0)
+        out_ref[:, start : start + WIDE] = mm(rows, grads)
+        at = pl.ds(start, WIDE)
+        copies.append(pltpu.make_async_copy(out_ref.at[:, at], out_hbm.at[:, at], sems.at[len(copies)]))
+        copies[-1].start()
+    for copy in copies:
+        copy.wait()
+
+
+def sent_products(me, x, own, others, slots, name):
+    out = shape((len(slots) * x.shape[1], own.shape[1]), F32)
+    size = sum(math.prod(a.shape) * a.dtype.itemsize for a in [x, own, *others, out])
+    return pl.pallas_call(
+        functools.partial(sent_kernel, slots),
+        in_specs=[SMEM] + [VMEM] * (2 + len(others)),
+        out_specs=HBM,
+        out_shape=out,
+        scratch_shapes=[pltpu.VMEM(out.shape, F32), pltpu.SemaphoreType.DMA((own.shape[1] // WIDE,))],
+        compiler_params=params(size),
+        cost_estimate=cost(0, 0),
+        name=name,
+    )(me, x, own, *others)
+
+
 class Chunk:
     def __init__(self, start, stop, orders, masks):
         self.start, self.stop = start, stop
@@ -624,7 +659,7 @@
         in_specs=[VMEM, row_blocks(w)],
         out_specs=out_columns(t),
         out_shape=shape((t, d), F32),
-        compiler_params=params(4 * t * WIDE * 4 + 4 * WIDE * w.shape[1] + 2 * grad.size),
+        compiler_params=params(4 * t * WIDE * 4 + 2 * grad.size),
         cost_estimate=cost(0, 0),
         name="input_gradient_q",
     )(grad, w)
@@ -633,7 +668,7 @@
 def rest_input_gradient(first, codes, grad_a, grad_b, wa, wb):
     t, d = first.shape
     rows = codes.shape[0]
-    size = 8 * t * WIDE * 4 + 8 * WIDE * wa.shape[1] + 4 * grad_a.size
+    size = 4 * t * WIDE * 4 + 4 * grad_a.size
     return pl.pallas_call(
         rest_input_kernel,
         grid=(d // WIDE,),
@@ -710,7 +745,7 @@
 
     def begin(chunks, own, others, name):
         own, *others = order.tied(own, *others)
-        sent = products(me, merged, own, others, [(c.slots(True), c.start, c.stop) for c in chunks], name)
+        sent = [sent_products(me, merged, own, others, c.slots(True), name) for c in chunks]
         order.mark(sent[0])
         for chunk, array in zip(chunks, sent):
             chunk.launch(array)

time: 190 us -> 189 us (level)
    pallas_call x35 -> x32, Pallas kernels: 38.8 us -> 31 us  [in_vmem(): pl.pallas_call(kernel, in_specs=[SMEM] * len(slots) + [VMEM] * len(inputs...]
    pallas_call x0 -> x3, Pallas kernels: none -> 7.11 us  [sent_products(): pl.pallas_call(functools.partial(sent_kernel, slots), in_specs=[SMEM] + [...]
  transfers between devices with their start and end apart: 35 -> 35, of which waited for: 21 -> 21; matrix products, arithmetic and copies ran while one was open for 1% -> 1% of each run, Pallas kernels for 29% -> 28%
where the time goes in v5:
time: 189 us; the launch traced here: 188 us
  waiting for transfers between devices  82.9 us (44%)
  Pallas kernels  64.1 us (34%)
  starting transfers between devices  34.7 us (18%)
  other arithmetic  2.71 us (1%)
  local copies, waits for them, and re-layouts  2.62 us (1%)
    ppermute x21, waiting for transfers between devices, both_exchange(): lax.ppermute(array, AXES, [(i, i ^ masks[i % 2]) for i in range(total)])  68.4 us
    pallas_call x32, Pallas kernels, in_vmem(): pl.pallas_call(kernel, in_specs=[SMEM] * len(slots) + [VMEM] * len(inputs...  31 us
    ppermute x21, starting transfers between devices, both_exchange(): lax.ppermute(array, AXES, [(i, i ^ masks[i % 2]) for i in range(total)])  19.4 us
    pallas_call x1, Pallas kernels, rest_input_gradient(): pl.pallas_call(rest_input_kernel, grid=(d // WIDE,), in_specs=[out_column...  12 us
    ppermute x12, starting transfers between devices, exchange(): return lax.ppermute(array, axis, [(i, i ^ mask) for i in range(count)])  10.9 us
    pallas_call x1, Pallas kernels, embed_keys_values(): pl.pallas_call(embed_kernel, in_specs=[SMEM, VMEM] + [HBM] * 3, out_specs...  9.93 us
    ppermute x2, waiting for transfers between devices, second(): self.bases.append(lax.ppermute(total, 'seq', pairs))  7.92 us
    pallas_call x3, Pallas kernels, sent_products(): pl.pallas_call(functools.partial(sent_kernel, slots), in_specs=[SMEM] + [...  7.11 us
  transfers between devices with their start and end apart: 35, of which 21 were waited for; matrix products, arithmetic and copies ran while one was open for 1% of the time, Pallas kernels for 28%

profile of v5, /device:TPU:13, one launch (start us, length us, event | category | flops | bytes accessed | tf_op | source)
XLA Modules:
  0.0 188.3 jit_solution(13487796951009349581)
XLA Ops:
  2.3 9.9 %embed_keys_values.1 = (bf16[512,2048]{1,0:T(8,128)(2,1)S(1)}, f32[8,512]{1,0:T(8,128)S(1)}, bf16[512,1024]{1,0:T(8,128)(2,1)S(1)}, f32[512,1024]{1,0:T(8,128)S(...) custom-call(s32[2]{0:T(128)S(1)} %pad_add_fusion.slots, ...), custom_call_target="tpu_custom_call" | custom-call | flops 1 | bytes 1 | tf_op jit(solution)/shard_map/embed_keys_values/pallas_call | solution.py:166
  12.6 2.4 %collective-permute-start.2 = (f32[2,128,128]{2,1,0:T(8,128)S(1)}, f32[2,128,128]{2,1,0:T(8,128)S(1)}, u32[]{:S(2)}, u32[]{:S(2)}) collective-permute-start(f32[2,128,128]{2,1,0:T(8,128)S(1)} %get-tuple-element.126), channel_id=1, source_target_pairs={{0,12},{4,8},{8,4},{12,0},{16,28},{20,24},{24,20},{28,16},{1,13},{... | collective-permute-start | bytes 393224 | tf_op jit(solution)/shard_map/ppermute | solution.py:385
  15.0 4.0 %queries_scores.1 = (bf16[512,1024]{1,0:T(8,128)(2,1)S(1)}, f32[512,1024]{1,0:T(8,128)S(1)}, f32[512,1024]{1,0:T(8,128)S(1)}) custom-call(bf16[512,2048]{1,0:T(8,128)(2,1)S(1)} %get-tuple-element.128.x_ref, bf16[2048,1024]{1,0:T(8,128)(2,1)S(1)} %copy-done.4, bf16[512,1024]{1,0:T(8,128)(2,1)S(1)} %get-tuple-element.117.k_ref, ...), custom_call_target="tpu_custom_call" | custom-call | flops 1 | bytes 1 | tf_op jit(solution)/shard_map/queries_scores/pallas_call | solution.py:88
  20.1 2.2 %collective-permute-start.10 = (f32[16,64,512]{2,1,0:T(8,128)S(1)}, f32[16,64,512]{2,1,0:T(8,128)S(1)}, u32[]{:S(2)}, u32[]{:S(2)}) collective-permute-start(f32[16,64,512]{2,1,0:T(8,128)S(1)} %get-tuple-element.150), channel_id=1, source_target_pairs={{0,1},{1,0},{2,3},{3,2},{4,5},{5,4},{6,7},{7,6},{8,9},{9,8},{10,11... | collective-permute-start | bytes 6291464 | tf_op jit(solution)/shard_map/ppermute | solution.py:458
  22.3 3.2 %collective-permute-start.3 = (f32[2,128,128]{2,1,0:T(8,128)S(1)}, f32[2,128,128]{2,1,0:T(8,128)S(1)}, u32[]{:S(2)}, u32[]{:S(2)}) collective-permute-start(f32[2,128,128]{2,1,0:T(8,128)S(1)} %add_add_fusion.1), channel_id=1, source_target_pairs={{0,24},{4,28},{8,16},{12,20},{1,25},{5,29},{9,17},{13,21},{2,26},{... | collective-permute-start | bytes 393224 | tf_op jit(solution)/shard_map/ppermute | solution.py:439
  25.5 5.5 %collective-permute-done.3.base_ref = f32[2,128,128]{2,1,0:T(8,128)S(1)} collective-permute-done((f32[2,128,128]{2,1,0:T(8,128)S(1)}, f32[2,128,128]{2,1,0:T(8,128)S(1)}, u32[]{:S(2)}, u32[]{:S(2)}) %collective-permute-start.3) | collective-permute-done | bytes 131104 | tf_op jit(solution)/shard_map/ppermute | solution.py:439
  31.7 2.4 %collective-permute-start.6 = (f32[2,128,128]{2,1,0:T(8,128)S(1)}, f32[2,128,128]{2,1,0:T(8,128)S(1)}, u32[]{:S(2)}, u32[]{:S(2)}) collective-permute-start(f32[2,128,128]{2,1,0:T(8,128)S(1)} %get-tuple-element.137), channel_id=1, source_target_pairs={{0,12},{4,8},{8,4},{12,0},{16,28},{20,24},{24,20},{28,16},{1,13},{... | collective-permute-start | bytes 393224 | tf_op jit(solution)/shard_map/ppermute | solution.py:385
  34.2 1.2 collective-permute-done.4.rest_1_
  35.9 3.1 %collective-permute-done.6.rest_3_ = f32[2,128,128]{2,1,0:T(8,128)S(1)} collective-permute-done((f32[2,128,128]{2,1,0:T(8,128)S(1)}, f32[2,128,128]{2,1,0:T(8,128)S(1)}, u32[]{:S(2)}, u32[]{:S(2)}) %collective-permute-start.6) | collective-permute-done | bytes 131104 | tf_op jit(solution)/shard_map/ppermute | solution.py:385
  39.0 3.3 %norm_gradient.1 = (bf16[512,1024]{1,0:T(8,128)(2,1)S(1)}, f32[1,1024]{1,0:T(1,128)S(1)}, f32[2,8,128,128]{3,2,1,0:T(8,128)S(1)}, f32[2,128,128]{2,1,0:T(8,128)S...) custom-call(s32[2]{0:T(128)S(1)} %pad_add_fusion.slots, ...), custom_call_target="tpu_custom_call" | custom-call | flops 1 | bytes 1 | tf_op jit(solution)/shard_map/norm_gradient/pallas_call | solution.py:88
  43.1 1.9 %collective-permute-start.9 = (f32[2,128,128]{2,1,0:T(8,128)S(1)}, f32[2,128,128]{2,1,0:T(8,128)S(1)}, u32[]{:S(2)}, u32[]{:S(2)}) collective-permute-start(f32[2,128,128]{2,1,0:T(8,128)S(1)} %get-tuple-element.148), channel_id=1, source_target_pairs={{0,12},{4,8},{8,4},{12,0},{16,28},{20,24},{24,20},{28,16},{1,13},{... | collective-permute-start | bytes 393224 | tf_op jit(solution)/shard_map/ppermute | solution.py:385
  45.0 2.5 %query_gradient.1.grad_ref.own_ref = bf16[512,1024]{1,0:T(8,128)(2,1)S(1)} custom-call(s32[2]{0:T(128)S(1)} %pad_add_fusion.slots, bf16[512,1024]{1,0:T(8,128)(2,1)S(1)} %get-tuple-element.158.datt_ref, bf16[512,1024]{1,0:T(8,128)(2,1)S(1)} %get-tuple-element.118.v_ref, bf16[512,1024]{1,0:T(8,128)(2,1)S(1)} %get-tuple-element.117.k_ref, ...), custom_call_target="tpu_custom_call" | custom-call | flops 1 | bytes 1 | tf_op jit(solution)/shard_map/query_gradient/pallas_call | solution.py:88
  49.1 3.8 %collective-permute-start.13 = (f32[512,512]{1,0:T(8,128)S(1)}, f32[512,512]{1,0:T(8,128)S(1)}, u32[]{:S(2)}, u32[]{:S(2)}) collective-permute-start(f32[512,512]{1,0:T(8,128)S(1)} %get-tuple-element.157), channel_id=1, source_target_pairs={{0,1},{1,0},{2,3},{3,2},{4,5},{5,4},{6,7},{7,6},{8,9},{9,8},{10,11... | collective-permute-start | bytes 3145736 | tf_op jit(solution)/shard_map/ppermute | solution.py:458
  53.0 1.3 collective-permute-start.11
  54.3 2.6 %within_block.1 = (f32[512,1024]{1,0:T(8,128)S(1)}, f32[512,1024]{1,0:T(8,128)S(1)}) custom-call(bf16[512,1024]{1,0:T(8,128)(2,1)S(1)} %get-tuple-element.158.datt_ref, bf16[512,1024]{1,0:T(8,128)(2,1)S(1)} %get-tuple-element.118.v_ref, bf16[512,1024]{1,0:T(8,128)(2,1)S(1)} %get-tuple-element.117.k_ref, bf16[512,1024]{1,0:T(8,128)(2,1)S(1)} %get-tuple-element.120.q_ref), custom_call_target="tpu_custom_call" | custom-call | flops 1 | bytes 1 | tf_op jit(solution)/shard_map/within_block/pallas_call | solution.py:88
  56.9 2.4 %weight_q.1 = f32[512,1024]{1,0:T(8,128)} custom-call(s32[1]{0:T(128)} %bitcast.2.me_ref, bf16[16,64,1024]{2,1,0:T(8,128)(2,1)S(1)} %merge_inputs.1.x_ref, bf16[512,1024]{1,0:T(8,128)(2,1)S(1)} %query_gradient.1.grad_ref.own_ref, f32[512,512]{1,0:T(8,128)S(1)} %collective-permute-done.12.rest_0_, f32[512,512]{1,0:T(8,128)S(1)} %collective-permute-done.13.rest_1_), custom_call_target="tpu_custom_call" | custom-call | flops 1 | bytes 1 | tf_op jit(solution)/shard_map/weight_q/pallas_call | solution.py:534
  59.2 1.3 weight_q_kept.1.rest_ref.a_ref
  60.5 2.4 %collective-permute-done.11.base_ref = f32[2,128,128]{2,1,0:T(8,128)S(1)} collective-permute-done((f32[2,128,128]{2,1,0:T(8,128)S(1)}, f32[2,128,128]{2,1,0:T(8,128)S(1)}, u32[]{:S(2)}, u32[]{:S(2)}) %collective-permute-start.11) | collective-permute-done | bytes 131104 | tf_op jit(solution)/shard_map/ppermute | solution.py:439
  63.7 2.2 %collective-permute-start.16 = (f32[2,128,128]{2,1,0:T(8,128)S(1)}, f32[2,128,128]{2,1,0:T(8,128)S(1)}, u32[]{:S(2)}, u32[]{:S(2)}) collective-permute-start(f32[2,128,128]{2,1,0:T(8,128)S(1)} %get-tuple-element.173), channel_id=1, source_target_pairs={{0,12},{4,8},{8,4},{12,0},{16,28},{20,24},{24,20},{28,16},{1,13},{... | collective-permute-start | bytes 393224 | tf_op jit(solution)/shard_map/ppermute | solution.py:385
  66.0 4.0 %input_gradient_q.1.first_ref = f32[512,2048]{1,0:T(8,128)S(1)} custom-call(bf16[512,1024]{1,0:T(8,128)(2,1)S(1)} %query_gradient.1.grad_ref.own_ref, bf16[2048,1024]{1,0:T(8,128)(2,1)S(1)} %copy-done.4), custom_call_target="tpu_custom_call" | custom-call | flops 1 | bytes 1 | tf_op jit(solution)/shard_map/input_gradient_q/pallas_call | solution.py:656
  70.8 1.9 key_value_gradients.1
  72.7 4.3 %collective-permute-start.19 = (f32[512,512]{1,0:T(8,128)S(1)}, f32[512,512]{1,0:T(8,128)S(1)}, u32[]{:S(2)}, u32[]{:S(2)}) collective-permute-start(f32[512,512]{1,0:T(8,128)S(1)} %get-tuple-element.181), channel_id=1, source_target_pairs={{0,1},{1,0},{2,3},{3,2},{4,5},{5,4},{6,7},{7,6},{8,9},{9,8},{10,11... | collective-permute-start | bytes 3145736 | tf_op jit(solution)/shard_map/ppermute | solution.py:458
  77.5 1.7 collective-permute-done.19.rest_0_
  79.2 1.5 collective-permute-done.20.rest_1_
  80.7 2.4 %weight_k.1 = f32[512,1024]{1,0:T(8,128)} custom-call(s32[1]{0:T(128)} %bitcast.2.me_ref, bf16[16,64,1024]{2,1,0:T(8,128)(2,1)S(1)} %merge_inputs.1.x_ref, bf16[512,1024]{1,0:T(8,128)(2,1)S(1)} %get-tuple-element.191.own_ref.grad_a, f32[512,512]{1,0:T(8,128)S(1)} %collective-permute-done.19.rest_0_, f32[512,512]{1,0:T(8,128)S(1)} %collective-permute-done.20.rest_1_), custom_call_target="tpu_custom_call" | custom-call | flops 1 | bytes 1 | tf_op jit(solution)/shard_map/weight_k/pallas_call | solution.py:534
  83.6 1.3 weight_k_kept.1.a_ref
  84.9 2.3 %weight_v.1 = f32[512,1024]{1,0:T(8,128)} custom-call(s32[1]{0:T(128)} %bitcast.2.me_ref, bf16[16,64,1024]{2,1,0:T(8,128)(2,1)S(1)} %merge_inputs.1.x_ref, bf16[512,1024]{1,0:T(8,128)(2,1)S(1)} %get-tuple-element.190.own_ref.grad_b, f32[512,512]{1,0:T(8,128)S(1)} %collective-permute-done.17.rest_0_, f32[512,512]{1,0:T(8,128)S(1)} %collective-permute-done.18.rest_1_), custom_call_target="tpu_custom_call" | custom-call | flops 1 | bytes 1 | tf_op jit(solution)/shard_map/weight_v/pallas_call | solution.py:534
  88.4 1.3 weight_v_kept.1.a_ref
  89.7 1.3 copy-done
  91.0 12.0 %input_gradient_kv.1 = (bf16[512,2048]{1,0:T(8,128)(2,1)}, f32[8,2048]{1,0:T(8,128)S(1)}) custom-call(f32[512,2048]{1,0:T(8,128)S(1)} %input_gradient_q.1.first_ref, f32[8,512]{1,0:T(8,128)S(1)} %get-tuple-element.167.codes_ref, bf16[512,1024]{1,0:T(8,128)(2,1)S(1)} %get-tuple-element.191.own_ref.grad_a, ...), custom_call_target="tpu_custom_call" | custom-call | flops 1 | bytes 1 | tf_op jit(solution)/shard_map/input_gradient_kv/pallas_call | solution.py:672
  105.1 1.7 add_rows_with.3
  107.4 1.7 add_rows.15.rest_ref.a_ref
  109.2 1.7 add_rows.16
  111.9 1.7 add_rows.17.a_ref
  113.6 14.5 %collective-permute-done.23.got_ref.b_ref = f32[272,1024]{1,0:T(8,128)S(1)} collective-permute-done((f32[272,1024]{1,0:T(8,128)S(1)}, f32[272,1024]{1,0:T(8,128)S(1)}, u32[]{:S(2)}, u32[]{:S(2)}) %collective-permute-start.23) | collective-permute-done | bytes 1114144 | tf_op jit(solution)/shard_map/ppermute | solution.py:458
  128.2 2.9 %collective-permute-done.27.b_ref = f32[512,1024]{1,0:T(8,128)} collective-permute-done((f32[512,1024]{1,0:T(8,128)}, f32[512,1024]{1,0:T(8,128)}, u32[]{:S(2)}, u32[]{:S(2)}) %collective-permute-start.27) | collective-permute-done | bytes 2097184 | tf_op jit(solution)/shard_map/ppermute | solution.py:458
  131.1 1.7 add_rows.19
  132.8 1.3 collective-permute-start.29
  134.4 1.7 add_rows.20.a_ref
  136.1 3.1 %collective-permute-done.26.b_ref = f32[256,1024]{1,0:T(8,128)S(1)} collective-permute-done((f32[256,1024]{1,0:T(8,128)S(1)}, f32[256,1024]{1,0:T(8,128)S(1)}, u32[]{:S(2)}, u32[]{:S(2)}) %collective-permute-start.26) | collective-permute-done | bytes 1048608 | tf_op jit(solution)/shard_map/ppermute | solution.py:458
  139.5 9.9 %collective-permute-done.25.got_ref.b_ref = f32[144,1024]{1,0:T(8,128)S(1)} collective-permute-done((f32[144,1024]{1,0:T(8,128)S(1)}, f32[144,1024]{1,0:T(8,128)S(1)}, u32[]{:S(2)}, u32[]{:S(2)}) %collective-permute-start.25) | collective-permute-done | bytes 589856 | tf_op jit(solution)/shard_map/ppermute | solution.py:458
  151.4 2.0 %collective-permute-done.31.b_ref = f32[128,1024]{1,0:T(8,128)S(1)} collective-permute-done((f32[128,1024]{1,0:T(8,128)S(1)}, f32[128,1024]{1,0:T(8,128)S(1)}, u32[]{:S(2)}, u32[]{:S(2)}) %collective-permute-start.31) | collective-permute-done | bytes 524320 | tf_op jit(solution)/shard_map/ppermute | solution.py:458
  153.5 9.9 %collective-permute-done.30.b_ref = f32[128,1024]{1,0:T(8,128)S(1)} collective-permute-done((f32[128,1024]{1,0:T(8,128)S(1)}, f32[128,1024]{1,0:T(8,128)S(1)}, u32[]{:S(2)}, u32[]{:S(2)}) %collective-permute-start.30) | collective-permute-done | bytes 524320 | tf_op jit(solution)/shard_map/ppermute | solution.py:458
  163.5 4.3 %collective-permute-done.28.got_ref = f32[80,1024]{1,0:T(8,128)S(1)} collective-permute-done((f32[80,1024]{1,0:T(8,128)S(1)}, f32[80,1024]{1,0:T(8,128)S(1)}, u32[]{:S(2)}, u32[]{:S(2)}) %collective-permute-start.28) | collective-permute-done | bytes 327712 | tf_op jit(solution)/shard_map/ppermute | solution.py:458
  168.0 1.2 collective-permute-start.32
  169.5 1.9 %collective-permute-done.33 = f32[16,1024]{1,0:T(8,128)S(1)} collective-permute-done((f32[16,1024]{1,0:T(8,128)S(1)}, f32[16,1024]{1,0:T(8,128)S(1)}, u32[]{:S(2)}, u32[]{:S(2)}) %collective-permute-start.33) | collective-permute-done | bytes 65568 | tf_op jit(solution)/shard_map/ppermute | solution.py:458
  172.7 11.6 %collective-permute-done.32 = f32[64,1024]{1,0:T(8,128)S(1)} collective-permute-done((f32[64,1024]{1,0:T(8,128)S(1)}, f32[64,1024]{1,0:T(8,128)S(1)}, u32[]{:S(2)}, u32[]{:S(2)}) %collective-permute-start.32) | collective-permute-done | bytes 262176 | tf_op jit(solution)/shard_map/ppermute | solution.py:458
  184.3 2.9 %collective-permute-done.34 = f32[64,1024]{1,0:T(8,128)S(1)} collective-permute-done((f32[64,1024]{1,0:T(8,128)S(1)}, f32[64,1024]{1,0:T(8,128)S(1)}, u32[]{:S(2)}, u32[]{:S(2)}) %collective-permute-start.34) | collective-permute-done | bytes 262176 | tf_op jit(solution)/shard_map/ppermute | solution.py:458
  (94 shorter events, 19.5 us)
Async XLA Ops:
  2.3 12.7 %copy-start.4 = (bf16[2048,1024]{1,0:T(8,128)(2,1)S(1)}, bf16[2048,1024]{1,0:T(8,128)(2,1)}, u32[]{:S(2)}) copy-start(bf16[2048,1024]{1,0:T(8,128)(2,1)} %w_ref.1) | copy-start | bytes 12582916
  12.3 7.8 %collective-permute-start = (f32[2,128,128]{2,1,0:T(8,128)S(1)}, f32[2,128,128]{2,1,0:T(8,128)S(1)}, u32[]{:S(2)}, u32[]{:S(2)}) collective-permute-start(f32[2,128,128]{2,1,0:T(8,128)S(1)} %get-tuple-element.124), channel_id=1, source_target_pairs={{0,4},{4,0},{8,12},{12,8},{16,20},{20,16},{24,28},{28,24},{1,5},{5... | collective-permute-start | bytes 393224 | tf_op jit(solution)/shard_map/ppermute | solution.py:385
  12.6 7.5 %collective-permute-start.1 = (f32[2,128,128]{2,1,0:T(8,128)S(1)}, f32[2,128,128]{2,1,0:T(8,128)S(1)}, u32[]{:S(2)}, u32[]{:S(2)}) collective-permute-start(f32[2,128,128]{2,1,0:T(8,128)S(1)} %get-tuple-element.125), channel_id=1, source_target_pairs={{0,8},{4,12},{8,0},{12,4},{16,24},{20,28},{24,16},{28,20},{1,9},{5... | collective-permute-start | bytes 393224 | tf_op jit(solution)/shard_map/ppermute | solution.py:385
  12.6 7.5 %collective-permute-start.2 = (f32[2,128,128]{2,1,0:T(8,128)S(1)}, f32[2,128,128]{2,1,0:T(8,128)S(1)}, u32[]{:S(2)}, u32[]{:S(2)}) collective-permute-start(f32[2,128,128]{2,1,0:T(8,128)S(1)} %get-tuple-element.126), channel_id=1, source_target_pairs={{0,12},{4,8},{8,4},{12,0},{16,28},{20,24},{24,20},{28,16},{1,13},{... | collective-permute-start | bytes 393224 | tf_op jit(solution)/shard_map/ppermute | solution.py:385
  19.0 20.0 %copy-start.7 = (bf16[1,512,1024]{2,1,0:T(8,128)(2,1)S(1)}, bf16[1,512,1024]{2,1,0:T(8,128)(2,1)}, u32[]{:S(2)}) copy-start(bf16[1,512,1024]{2,1,0:T(8,128)(2,1)} %param.15) | copy-start | bytes 3145732
  19.0 20.0 %copy-start.8 = (f32[1024]{0:T(1024)S(1)}, f32[1024]{0:T(1024)}, u32[]{:S(2)}) copy-start(f32[1024]{0:T(1024)} %param.14) | copy-start | bytes 12292
  20.1 27.5 %collective-permute-start.10 = (f32[16,64,512]{2,1,0:T(8,128)S(1)}, f32[16,64,512]{2,1,0:T(8,128)S(1)}, u32[]{:S(2)}, u32[]{:S(2)}) collective-permute-start(f32[16,64,512]{2,1,0:T(8,128)S(1)} %get-tuple-element.150), channel_id=1, source_target_pairs={{0,1},{1,0},{2,3},{3,2},{4,5},{5,4},{6,7},{7,6},{8,9},{9,8},{10,11... | collective-permute-start | bytes 6291464 | tf_op jit(solution)/shard_map/ppermute | solution.py:458
  22.3 8.8 %collective-permute-start.3 = (f32[2,128,128]{2,1,0:T(8,128)S(1)}, f32[2,128,128]{2,1,0:T(8,128)S(1)}, u32[]{:S(2)}, u32[]{:S(2)}) collective-permute-start(f32[2,128,128]{2,1,0:T(8,128)S(1)} %add_add_fusion.1), channel_id=1, source_target_pairs={{0,24},{4,28},{8,16},{12,20},{1,25},{5,29},{9,17},{13,21},{2,26},{... | collective-permute-start | bytes 393224 | tf_op jit(solution)/shard_map/ppermute | solution.py:439
  31.4 3.9 %collective-permute-start.4 = (f32[2,128,128]{2,1,0:T(8,128)S(1)}, f32[2,128,128]{2,1,0:T(8,128)S(1)}, u32[]{:S(2)}, u32[]{:S(2)}) collective-permute-start(f32[2,128,128]{2,1,0:T(8,128)S(1)} %get-tuple-element.135), channel_id=1, source_target_pairs={{0,4},{4,0},{8,12},{12,8},{16,20},{20,16},{24,28},{28,24},{1,5},{5... | collective-permute-start | bytes 393224 | tf_op jit(solution)/shard_map/ppermute | solution.py:385
  31.7 4.1 %collective-permute-start.5 = (f32[2,128,128]{2,1,0:T(8,128)S(1)}, f32[2,128,128]{2,1,0:T(8,128)S(1)}, u32[]{:S(2)}, u32[]{:S(2)}) collective-permute-start(f32[2,128,128]{2,1,0:T(8,128)S(1)} %get-tuple-element.136), channel_id=1, source_target_pairs={{0,8},{4,12},{8,0},{12,4},{16,24},{20,28},{24,16},{28,20},{1,9},{5... | collective-permute-start | bytes 393224 | tf_op jit(solution)/shard_map/ppermute | solution.py:385
  31.7 7.2 %collective-permute-start.6 = (f32[2,128,128]{2,1,0:T(8,128)S(1)}, f32[2,128,128]{2,1,0:T(8,128)S(1)}, u32[]{:S(2)}, u32[]{:S(2)}) collective-permute-start(f32[2,128,128]{2,1,0:T(8,128)S(1)} %get-tuple-element.137), channel_id=1, source_target_pairs={{0,12},{4,8},{8,4},{12,0},{16,28},{20,24},{24,20},{28,16},{1,13},{... | collective-permute-start | bytes 393224 | tf_op jit(solution)/shard_map/ppermute | solution.py:385
  42.3 5.5 %collective-permute-start.7 = (f32[2,128,128]{2,1,0:T(8,128)S(1)}, f32[2,128,128]{2,1,0:T(8,128)S(1)}, u32[]{:S(2)}, u32[]{:S(2)}) collective-permute-start(f32[2,128,128]{2,1,0:T(8,128)S(1)} %get-tuple-element.146), channel_id=1, source_target_pairs={{0,4},{4,0},{8,12},{12,8},{16,20},{20,16},{24,28},{28,24},{1,5},{5... | collective-permute-start | bytes 393224 | tf_op jit(solution)/shard_map/ppermute | solution.py:385
  42.6 5.2 %collective-permute-start.8 = (f32[2,128,128]{2,1,0:T(8,128)S(1)}, f32[2,128,128]{2,1,0:T(8,128)S(1)}, u32[]{:S(2)}, u32[]{:S(2)}) collective-permute-start(f32[2,128,128]{2,1,0:T(8,128)S(1)} %get-tuple-element.147), channel_id=1, source_target_pairs={{0,8},{4,12},{8,0},{12,4},{16,24},{20,28},{24,16},{28,20},{1,9},{5... | collective-permute-start | bytes 393224 | tf_op jit(solution)/shard_map/ppermute | solution.py:385
  43.1 5.8 %collective-permute-start.9 = (f32[2,128,128]{2,1,0:T(8,128)S(1)}, f32[2,128,128]{2,1,0:T(8,128)S(1)}, u32[]{:S(2)}, u32[]{:S(2)}) collective-permute-start(f32[2,128,128]{2,1,0:T(8,128)S(1)} %get-tuple-element.148), channel_id=1, source_target_pairs={{0,12},{4,8},{8,4},{12,0},{16,28},{20,24},{24,20},{28,16},{1,13},{... | collective-permute-start | bytes 393224 | tf_op jit(solution)/shard_map/ppermute | solution.py:385
  49.1 7.8 %collective-permute-start.13 = (f32[512,512]{1,0:T(8,128)S(1)}, f32[512,512]{1,0:T(8,128)S(1)}, u32[]{:S(2)}, u32[]{:S(2)}) collective-permute-start(f32[512,512]{1,0:T(8,128)S(1)} %get-tuple-element.157), channel_id=1, source_target_pairs={{0,1},{1,0},{2,3},{3,2},{4,5},{5,4},{6,7},{7,6},{8,9},{9,8},{10,11... | collective-permute-start | bytes 3145736 | tf_op jit(solution)/shard_map/ppermute | solution.py:458
  52.9 4.0 %collective-permute-start.12 = (f32[512,512]{1,0:T(8,128)S(1)}, f32[512,512]{1,0:T(8,128)S(1)}, u32[]{:S(2)}, u32[]{:S(2)}) collective-permute-start(f32[512,512]{1,0:T(8,128)S(1)} %get-tuple-element.156), channel_id=1, source_target_pairs={{0,1},{1,0},{2,3},{3,2},{4,5},{5,4},{6,7},{7,6},{8,9},{9,8},{10,11... | collective-permute-start | bytes 3145736 | tf_op jit(solution)/shard_map/ppermute | solution.py:458
  53.0 9.9 %collective-permute-start.11 = (f32[2,128,128]{2,1,0:T(8,128)S(1)}, f32[2,128,128]{2,1,0:T(8,128)S(1)}, u32[]{:S(2)}, u32[]{:S(2)}) collective-permute-start(f32[2,128,128]{2,1,0:T(8,128)S(1)} %add_add_fusion), channel_id=1, source_target_pairs={{28,4},{24,0},{20,12},{16,8},{29,5},{25,1},{21,13},{17,9},{30,6},{... | collective-permute-start | bytes 393224 | tf_op jit(solution)/shard_map/ppermute | solution.py:439
  63.3 6.8 %collective-permute-start.14 = (f32[2,128,128]{2,1,0:T(8,128)S(1)}, f32[2,128,128]{2,1,0:T(8,128)S(1)}, u32[]{:S(2)}, u32[]{:S(2)}) collective-permute-start(f32[2,128,128]{2,1,0:T(8,128)S(1)} %get-tuple-element.171), channel_id=1, source_target_pairs={{0,4},{4,0},{8,12},{12,8},{16,20},{20,16},{24,28},{28,24},{1,5},{5... | collective-permute-start | bytes 393224 | tf_op jit(solution)/shard_map/ppermute | solution.py:385
  63.7 6.3 %collective-permute-start.15 = (f32[2,128,128]{2,1,0:T(8,128)S(1)}, f32[2,128,128]{2,1,0:T(8,128)S(1)}, u32[]{:S(2)}, u32[]{:S(2)}) collective-permute-start(f32[2,128,128]{2,1,0:T(8,128)S(1)} %get-tuple-element.172), channel_id=1, source_target_pairs={{0,8},{4,12},{8,0},{12,4},{16,24},{20,28},{24,16},{28,20},{1,9},{5... | collective-permute-start | bytes 393224 | tf_op jit(solution)/shard_map/ppermute | solution.py:385
  63.7 7.0 %collective-permute-start.16 = (f32[2,128,128]{2,1,0:T(8,128)S(1)}, f32[2,128,128]{2,1,0:T(8,128)S(1)}, u32[]{:S(2)}, u32[]{:S(2)}) collective-permute-start(f32[2,128,128]{2,1,0:T(8,128)S(1)} %get-tuple-element.173), channel_id=1, source_target_pairs={{0,12},{4,8},{8,4},{12,0},{16,28},{20,24},{24,20},{28,16},{1,13},{... | collective-permute-start | bytes 393224 | tf_op jit(solution)/shard_map/ppermute | solution.py:385
  66.0 39.1 %collective-permute-start.21 = (f32[512,1024]{1,0:T(8,128)}, f32[512,1024]{1,0:T(8,128)}, u32[]{:S(2)}, u32[]{:S(2)}) collective-permute-start(f32[512,1024]{1,0:T(8,128)} %weight_q.1), channel_id=1, source_target_pairs={{0,2},{1,9},{2,0},{3,11},{4,6},{5,13},{6,4},{7,15},{8,10},{9,1},{1... | collective-permute-start | bytes 6291464 | tf_op jit(solution)/shard_map/ppermute | solution.py:458
  72.7 6.6 %collective-permute-start.19 = (f32[512,512]{1,0:T(8,128)S(1)}, f32[512,512]{1,0:T(8,128)S(1)}, u32[]{:S(2)}, u32[]{:S(2)}) collective-permute-start(f32[512,512]{1,0:T(8,128)S(1)} %get-tuple-element.181), channel_id=1, source_target_pairs={{0,1},{1,0},{2,3},{3,2},{4,5},{5,4},{6,7},{7,6},{8,9},{9,8},{10,11... | collective-permute-start | bytes 3145736 | tf_op jit(solution)/shard_map/ppermute | solution.py:458
  77.0 3.8 %collective-permute-start.20 = (f32[512,512]{1,0:T(8,128)S(1)}, f32[512,512]{1,0:T(8,128)S(1)}, u32[]{:S(2)}, u32[]{:S(2)}) collective-permute-start(f32[512,512]{1,0:T(8,128)S(1)} %get-tuple-element.182), channel_id=1, source_target_pairs={{0,1},{1,0},{2,3},{3,2},{4,5},{5,4},{6,7},{7,6},{8,9},{9,8},{10,11... | collective-permute-start | bytes 3145736 | tf_op jit(solution)/shard_map/ppermute | solution.py:458
  77.0 7.8 %collective-permute-start.17 = (f32[512,512]{1,0:T(8,128)S(1)}, f32[512,512]{1,0:T(8,128)S(1)}, u32[]{:S(2)}, u32[]{:S(2)}) collective-permute-start(f32[512,512]{1,0:T(8,128)S(1)} %get-tuple-element.179), channel_id=1, source_target_pairs={{0,1},{1,0},{2,3},{3,2},{4,5},{5,4},{6,7},{7,6},{8,9},{9,8},{10,11... | collective-permute-start | bytes 3145736 | tf_op jit(solution)/shard_map/ppermute | solution.py:458
  77.5 7.4 %collective-permute-start.18 = (f32[512,512]{1,0:T(8,128)S(1)}, f32[512,512]{1,0:T(8,128)S(1)}, u32[]{:S(2)}, u32[]{:S(2)}) collective-permute-start(f32[512,512]{1,0:T(8,128)S(1)} %get-tuple-element.180), channel_id=1, source_target_pairs={{0,1},{1,0},{2,3},{3,2},{4,5},{5,4},{6,7},{7,6},{8,9},{9,8},{10,11... | collective-permute-start | bytes 3145736 | tf_op jit(solution)/shard_map/ppermute | solution.py:458
  83.1 26.0 %collective-permute-start.24 = (f32[512,1024]{1,0:T(8,128)}, f32[512,1024]{1,0:T(8,128)}, u32[]{:S(2)}, u32[]{:S(2)}) collective-permute-start(f32[512,1024]{1,0:T(8,128)} %weight_k.1), channel_id=1, source_target_pairs={{0,2},{1,5},{2,0},{3,7},{4,6},{5,1},{6,4},{7,3},{8,10},{9,13},{10,... | collective-permute-start | bytes 6291464 | tf_op jit(solution)/shard_map/ppermute | solution.py:458
  84.9 2.4 %copy-start.2 = (f32[512,1024]{1,0:T(8,128)}, f32[512,1024]{1,0:T(8,128)S(1)}, u32[]{:S(2)}) copy-start(f32[512,1024]{1,0:T(8,128)S(1)} %weight_k_kept.1.a_ref) | copy-start | bytes 6291460
  84.9 6.1 %copy-start.6 = (bf16[2048,1024]{1,0:T(8,128)(2,1)S(1)}, bf16[2048,1024]{1,0:T(8,128)(2,1)}, u32[]{:S(2)}) copy-start(bf16[2048,1024]{1,0:T(8,128)(2,1)} %wb_ref.1) | copy-start | bytes 12582916
  87.3 3.7 %copy-start.5 = (bf16[2048,1024]{1,0:T(8,128)(2,1)S(1)}, bf16[2048,1024]{1,0:T(8,128)(2,1)}, u32[]{:S(2)}) copy-start(bf16[2048,1024]{1,0:T(8,128)(2,1)} %wa_ref.1) | copy-start | bytes 12582916
  87.3 43.8 %collective-permute-start.27 = (f32[512,1024]{1,0:T(8,128)}, f32[512,1024]{1,0:T(8,128)}, u32[]{:S(2)}, u32[]{:S(2)}) collective-permute-start(f32[512,1024]{1,0:T(8,128)} %weight_v.1), channel_id=1, source_target_pairs={{0,8},{1,5},{2,10},{3,7},{4,12},{5,1},{6,14},{7,3},{8,0},{9,13},{1... | collective-permute-start | bytes 6291464 | tf_op jit(solution)/shard_map/ppermute | solution.py:458
  89.7 1.3 copy-start
  103.1 2.0 %collective-permute-start.22 = (f32[16,1024]{1,0:T(8,128)S(1)}, f32[16,1024]{1,0:T(8,128)S(1)}, u32[]{:S(2)}, u32[]{:S(2)}) collective-permute-start(f32[16,1024]{1,0:T(8,128)S(1)} %reshape.45), channel_id=1, source_target_pairs={{0,1},{1,0},{2,3},{3,2},{4,5},{5,4},{6,7},{7,6},{8,9},{9,8},{10,11... | collective-permute-start | bytes 196616 | tf_op jit(solution)/shard_map/ppermute | solution.py:458
  106.8 2.3 %copy-start.3 = (f32[512,1024]{1,0:T(8,128)S(1)}, f32[512,1024]{1,0:T(8,128)}, u32[]{:S(2)}) copy-start(f32[512,1024]{1,0:T(8,128)} %copy-done.2) | copy-start | bytes 6291460
  106.8 21.2 %collective-permute-start.23 = (f32[272,1024]{1,0:T(8,128)S(1)}, f32[272,1024]{1,0:T(8,128)S(1)}, u32[]{:S(2)}, u32[]{:S(2)}) collective-permute-start(f32[272,1024]{1,0:T(8,128)S(1)} %get-tuple-element.197), channel_id=1, source_target_pairs={{0,8},{1,3},{2,10},{3,1},{4,12},{5,7},{6,14},{7,5},{8,0},{9,11},{1... | collective-permute-start | bytes 3342344 | tf_op jit(solution)/shard_map/ppermute | solution.py:458
  110.9 28.4 %collective-permute-start.26 = (f32[256,1024]{1,0:T(8,128)S(1)}, f32[256,1024]{1,0:T(8,128)S(1)}, u32[]{:S(2)}, u32[]{:S(2)}) collective-permute-start(f32[256,1024]{1,0:T(8,128)S(1)} %add_rows.16), channel_id=1, source_target_pairs={{0,8},{1,3},{2,10},{3,1},{4,12},{5,7},{6,14},{7,5},{8,0},{9,11},{1... | collective-permute-start | bytes 3145736 | tf_op jit(solution)/shard_map/ppermute | solution.py:458
  128.1 3.0 %copy-start.1 = (f32[512,1024]{1,0:T(8,128)S(1)}, f32[512,1024]{1,0:T(8,128)}, u32[]{:S(2)}) copy-start(f32[512,1024]{1,0:T(8,128)} %copy-done) | copy-start | bytes 6291460
  132.8 17.7 %collective-permute-start.29 = (f32[256,1024]{1,0:T(8,128)S(1)}, f32[256,1024]{1,0:T(8,128)S(1)}, u32[]{:S(2)}, u32[]{:S(2)}) collective-permute-start(f32[256,1024]{1,0:T(8,128)S(1)} %add_rows.19), channel_id=1, source_target_pairs={{0,4},{1,3},{2,6},{3,1},{4,0},{5,7},{6,2},{7,5},{8,12},{9,11},{10,... | collective-permute-start | bytes 3145736 | tf_op jit(solution)/shard_map/ppermute | solution.py:458
  134.1 15.3 %collective-permute-start.25 = (f32[144,1024]{1,0:T(8,128)S(1)}, f32[144,1024]{1,0:T(8,128)S(1)}, u32[]{:S(2)}, u32[]{:S(2)}) collective-permute-start(f32[144,1024]{1,0:T(8,128)S(1)} %get-tuple-element.203), channel_id=1, source_target_pairs={{0,24},{1,5},{2,26},{3,7},{4,28},{5,1},{6,30},{7,3},{8,16},{9,13},... | collective-permute-start | bytes 1769480 | tf_op jit(solution)/shard_map/ppermute | solution.py:458
  139.3 14.1 %collective-permute-start.31 = (f32[128,1024]{1,0:T(8,128)S(1)}, f32[128,1024]{1,0:T(8,128)S(1)}, u32[]{:S(2)}, u32[]{:S(2)}) collective-permute-start(f32[128,1024]{1,0:T(8,128)S(1)} %add_rows.21), channel_id=1, source_target_pairs={{0,24},{1,9},{2,26},{3,11},{4,28},{5,13},{6,30},{7,15},{8,16},{9,1... | collective-permute-start | bytes 1572872 | tf_op jit(solution)/shard_map/ppermute | solution.py:458
  150.6 12.8 %collective-permute-start.30 = (f32[128,1024]{1,0:T(8,128)S(1)}, f32[128,1024]{1,0:T(8,128)S(1)}, u32[]{:S(2)}, u32[]{:S(2)}) collective-permute-start(f32[128,1024]{1,0:T(8,128)S(1)} %add_rows.24), channel_id=1, source_target_pairs={{0,2},{1,9},{2,0},{3,11},{4,6},{5,13},{6,4},{7,15},{8,10},{9,1},{1... | collective-permute-start | bytes 1572872 | tf_op jit(solution)/shard_map/ppermute | solution.py:458
  150.7 17.2 %collective-permute-start.28 = (f32[80,1024]{1,0:T(8,128)S(1)}, f32[80,1024]{1,0:T(8,128)S(1)}, u32[]{:S(2)}, u32[]{:S(2)}) collective-permute-start(f32[80,1024]{1,0:T(8,128)S(1)} %get-tuple-element.211), channel_id=1, source_target_pairs={{0,4},{1,25},{2,6},{3,27},{4,0},{5,29},{6,2},{7,31},{8,12},{9,17},... | collective-permute-start | bytes 983048 | tf_op jit(solution)/shard_map/ppermute | solution.py:458
  167.9 3.5 %collective-permute-start.33 = (f32[16,1024]{1,0:T(8,128)S(1)}, f32[16,1024]{1,0:T(8,128)S(1)}, u32[]{:S(2)}, u32[]{:S(2)}) collective-permute-start(f32[16,1024]{1,0:T(8,128)S(1)} %get-tuple-element.222), channel_id=1, source_target_pairs={{0,2},{1,9},{2,0},{3,11},{4,6},{5,13},{6,4},{7,15},{8,10},{9,1},{1... | collective-permute-start | bytes 196616 | tf_op jit(solution)/shard_map/ppermute | solution.py:458
  168.0 16.4 %collective-permute-start.32 = (f32[64,1024]{1,0:T(8,128)S(1)}, f32[64,1024]{1,0:T(8,128)S(1)}, u32[]{:S(2)}, u32[]{:S(2)}) collective-permute-start(f32[64,1024]{1,0:T(8,128)S(1)} %add_rows.26), channel_id=1, source_target_pairs={{0,4},{1,25},{2,6},{3,27},{4,0},{5,29},{6,2},{7,31},{8,12},{9,17},... | collective-permute-start | bytes 786440 | tf_op jit(solution)/shard_map/ppermute | solution.py:458
  169.2 18.1 %collective-permute-start.34 = (f32[64,1024]{1,0:T(8,128)S(1)}, f32[64,1024]{1,0:T(8,128)S(1)}, u32[]{:S(2)}, u32[]{:S(2)}) collective-permute-start(f32[64,1024]{1,0:T(8,128)S(1)} %add_rows.28), channel_id=1, source_target_pairs={{0,24},{1,25},{2,26},{3,27},{4,28},{5,29},{6,30},{7,31},{8,16},{9,... | collective-permute-start | bytes 786440 | tf_op jit(solution)/shard_map/ppermute | solution.py:458
